TPU v7x, 32 devices: a whole 2x2x4 slice. The times are simulated.
32 devices in a mesh: ctx: 8 (over y, x, core), fsdp: 4 (over z).
Axes of the slice: x: 2, y: 2, z: 4, core: 2. Of those that a mesh axis runs over, the one named last changes fastest.
Arguments:
- inputs: bfloat16 [4, 512, 2048], P('fsdp', 'ctx'), may hold values from -6 to 6
- cotangent: bfloat16 [4, 512, 2048], P('fsdp', 'ctx'), may hold values from -6 to 6
- doc_lengths: int32 [4, 3], replicated, may hold values from 1 to 480, as said below
- att_routes: int32 [512, 4, 2], P('ctx'), may hold values from 0 to 7, all different within a row; in each aligned block of 256 rows (0 to 255, 256 to 511, ..., all dimensions but the last counted through in order) at most 80 rows name the same one
- ffn_routes: int32 [512, 4, 2], P('ctx'), may hold values from 0 to 7, all different within a row; in each aligned block of 256 rows (0 to 255, 256 to 511, ..., all dimensions but the last counted through in order) at most 80 rows name the same one
- kv_weight: float32 [2048, 2, 2048], P('ctx', None, 'fsdp'), may hold values from -0.125 to 0.125
- query_weight: float32 [2048, 8, 2048], P('ctx', None, 'fsdp'), may hold values from -0.125 to 0.125
- output_weight: float32 [2048, 8, 2048], P('ctx', None, 'fsdp'), may hold values from -0.75 to 0.75
- att_router: float32 [2048, 8], P('ctx'), may hold values from -0.09375 to 0.09375
- att_gain: float32 [2048], P('ctx'), may hold values from 0.5 to 1.5
- gate_up_weight: float32 [2048, 8, 2, 5632], P('ctx', None, None, 'fsdp'), may hold values from -0.125 to 0.125
- down_weight: float32 [2048, 8, 5632], P('ctx', None, 'fsdp'), may hold values from -0.078125 to 0.078125
- ffn_router: float32 [2048, 8], P('ctx'), may hold values from -0.09375 to 0.09375
- ffn_gain: float32 [2048], P('ctx'), may hold values from 0.5 to 1.5
Outputs:
- outputs: bfloat16 [4, 512, 2048], P('fsdp', 'ctx')
- input_grad: bfloat16 [4, 512, 2048], P('fsdp', 'ctx')
- kv_grad: float32 [2048, 2, 2048], P('ctx', None, 'fsdp')
- query_grad: float32 [2048, 8, 2048], P('ctx', None, 'fsdp')
- output_grad: float32 [2048, 8, 2048], P('ctx', None, 'fsdp')
- att_router_grad: float32 [2048, 8], P('ctx')
- att_gain_grad: float32 [2048], P('ctx')
- gate_up_grad: float32 [2048, 8, 2, 5632], P('ctx', None, None, 'fsdp')
- down_grad: float32 [2048, 8, 5632], P('ctx', None, 'fsdp')
- ffn_router_grad: float32 [2048, 8], P('ctx')
- ffn_gain_grad: float32 [2048], P('ctx')
Inputs may be any that keep to these rules, and one draw needn't show every extreme that they name: `doc_lengths`: each stream holds its 3 documents from position 0 on, in order, and the rest of its 512 positions is padding; every stream has at least one padding position; in every stream one document has exactly 480 positions. `att_routes`: the two experts of a position differ; within the rows of one device (aligned blocks of 256 rows, positions slowest) no expert is named by more than 80 rows. `ffn_routes`: the two experts of a position differ; within the rows of one device (aligned blocks of 256 rows, positions slowest) no expert is named by more than 80 rows.
All inputs are finite; a program needn't handle non-finite values.
Results may differ from a plain program's by a relative error of at most 0.025.
Values may be sent and summed in bfloat16 or wider, within the bound.
No kernel may reach another device: no remote copies, remote signals or barrier semaphores. Data moves between devices by JAX's collectives and lax.ppermute only.
A program may use at most 576 MiB of HBM per device.

v0:
```python
import jax
import jax.numpy as jnp
from jax import lax
from jax.sharding import PartitionSpec as P

D = 2048
HEADS = 16
HD = 128
E_A = 8
E_F = 8
FF = 5632
DOCS = 3


norm_eps = 1e-06
rope_base = 10000.0
masked_score = -1e30


def doc_layout(doc_lengths, seq_len):
    doc_ends = jnp.cumsum(doc_lengths, axis=1)
    starts = doc_ends - doc_lengths
    positions = jnp.arange(seq_len, dtype=jnp.int32)
    doc_index = jnp.sum(
        (positions[None, :, None] >= doc_ends[:, None, :]).astype(jnp.int32), axis=2
    )
    labels = jnp.arange(doc_lengths.shape[1], dtype=jnp.int32)
    doc_start = jnp.sum(
        jnp.where(doc_index[:, :, None] == labels[None, None, :], starts[:, None, :], 0), axis=2
    )
    return (doc_index, positions[None, :] - doc_start)


def rope_tables(doc_place, head_dim):
    halves = jnp.arange(head_dim // 2, dtype=jnp.float32)
    inverse_freq = rope_base ** (-2.0 * halves / head_dim)
    angles = doc_place.astype(jnp.float32)[..., None] * inverse_freq
    return (jnp.cos(angles), jnp.sin(angles))


def rotate(values, cos_part, sin_part):
    half_dim = values.shape[-1] // 2
    first_half = values[..., :half_dim]
    second_half = values[..., half_dim:]
    return jnp.concatenate(
        (
            first_half * cos_part - second_half * sin_part,
            second_half * cos_part + first_half * sin_part,
        ),
        axis=-1,
    )


def unrotate(values, cos_part, sin_part):
    half_dim = values.shape[-1] // 2
    first_half = values[..., :half_dim]
    second_half = values[..., half_dim:]
    return jnp.concatenate(
        (
            first_half * cos_part + second_half * sin_part,
            second_half * cos_part - first_half * sin_part,
        ),
        axis=-1,
    )


def expert_table(route_rows, experts, capacity):
    row_count = route_rows.shape[0]
    flat_routes = route_rows.reshape(-1)
    labels = jnp.arange(experts, dtype=jnp.int32)
    onehot = (flat_routes[:, None] == labels[None, :]).astype(jnp.int32)
    slot_of = jnp.sum((jnp.cumsum(onehot, axis=0) - 1) * onehot, axis=1)
    slot_table = jnp.full((experts, capacity), 2 * row_count, jnp.int32)
    return slot_table.at[flat_routes, slot_of].set(jnp.arange(2 * row_count, dtype=jnp.int32))


def pad_rows(values):
    return jnp.concatenate((values, jnp.zeros((1, values.shape[1]), values.dtype)), axis=0)


def put_slots(values, slot_table, slot_total):
    feature = values.shape[-1]
    holder = jnp.zeros((slot_total + 1, feature), values.dtype)
    return holder.at[slot_table.reshape(-1)].set(values.reshape(-1, feature))[:slot_total]


def add_tokens(values, slot_table, row_count):
    feature = values.shape[-1]
    holder = jnp.zeros((row_count + 1, feature), values.dtype)
    return holder.at[(slot_table // 2).reshape(-1)].add(values.reshape(-1, feature))[:row_count]


def rms_forward(values, gain_row):
    inv_rms = lax.rsqrt(jnp.mean(values * values, axis=-1, keepdims=True) + norm_eps)
    normal_part = values * inv_rms
    return (normal_part * gain_row, normal_part, inv_rms)


def rms_backward(grad_out, normal_part, inv_rms, gain_row):
    grad_normal = grad_out * gain_row
    grad_in = inv_rms * (
        grad_normal - normal_part * jnp.mean(grad_normal * normal_part, axis=-1, keepdims=True)
    )
    return (grad_in, jnp.sum(grad_out * normal_part, axis=0))


def router_back(grad_gates, gate_probs, route_hot):
    grad_chosen = gate_probs * (
        grad_gates - jnp.sum(gate_probs * grad_gates, axis=1, keepdims=True)
    )
    return jnp.sum(route_hot * grad_chosen[:, :, None], axis=1)


def round_trip(values):
    return lax.optimization_barrier(values.astype(jnp.bfloat16)).astype(jnp.float32)


def per_device(
    inputs,
    cotangent,
    doc_lengths,
    att_routes,
    ffn_routes,
    kv_weight,
    query_weight,
    output_weight,
    att_router,
    att_gain,
    gate_up_weight,
    down_weight,
    ffn_router,
    ffn_gain,
):
    n_ctx = lax.axis_size("ctx")
    n_fsdp = lax.axis_size("fsdp")
    stream_index = lax.axis_index("fsdp")
    block_index = lax.axis_index("ctx")
    tok_local = inputs.shape[1]
    seq_len = tok_local * n_ctx
    row_count = n_fsdp * tok_local
    heads_local = HEADS // n_fsdp
    local_features = heads_local * HD
    ffn_local = FF // n_fsdp
    att_capacity = tok_local * n_fsdp * 5 // (2 * E_A)
    ffn_capacity = tok_local * n_fsdp * 5 // (2 * E_F)
    score_scale = HD ** (-0.5)
    (
        kv_full,
        query_full,
        output_full,
        att_router_full,
        att_gain_full,
        gate_up_full,
        down_full,
        ffn_router_full,
        ffn_gain_full,
    ) = (
        lax.all_gather(kv_weight.astype(jnp.bfloat16), "ctx", axis=0, tiled=True),
        lax.all_gather(query_weight.astype(jnp.bfloat16), "ctx", axis=0, tiled=True),
        lax.all_gather(output_weight.astype(jnp.bfloat16), "ctx", axis=0, tiled=True),
        lax.all_gather(att_router.astype(jnp.bfloat16), "ctx", axis=0, tiled=True),
        lax.all_gather(att_gain.astype(jnp.bfloat16), "ctx", axis=0, tiled=True),
        lax.all_gather(gate_up_weight.astype(jnp.bfloat16), "ctx", axis=0, tiled=True),
        lax.all_gather(down_weight.astype(jnp.bfloat16), "ctx", axis=0, tiled=True),
        lax.all_gather(ffn_router.astype(jnp.bfloat16), "ctx", axis=0, tiled=True),
        lax.all_gather(ffn_gain.astype(jnp.bfloat16), "ctx", axis=0, tiled=True),
    )
    all_inputs, all_cot = (
        lax.all_gather(inputs, "fsdp", axis=0, tiled=True),
        lax.all_gather(cotangent, "fsdp", axis=0, tiled=True),
    )
    doc_index, doc_place = doc_layout(doc_lengths, seq_len)
    query_doc = lax.dynamic_slice_in_dim(doc_index, block_index * tok_local, tok_local, 1)
    query_place = lax.dynamic_slice_in_dim(doc_place, block_index * tok_local, tok_local, 1)
    query_keep = query_doc < DOCS
    query_pos = block_index * tok_local + jnp.arange(tok_local, dtype=jnp.int32)
    keep_rows = query_keep.reshape(row_count, 1).astype(jnp.float32)
    cos_part, sin_part = rope_tables(query_place.reshape(row_count), HD)
    att_route_rows = jnp.transpose(att_routes, (1, 0, 2)).reshape(row_count, 2)
    ffn_route_rows = jnp.transpose(ffn_routes, (1, 0, 2)).reshape(row_count, 2)
    att_hot = (
        att_route_rows[:, :, None] == jnp.arange(E_A, dtype=jnp.int32)[None, None, :]
    ).astype(jnp.float32)
    ffn_hot = (
        ffn_route_rows[:, :, None] == jnp.arange(E_F, dtype=jnp.int32)[None, None, :]
    ).astype(jnp.float32)
    att_table = expert_table(att_route_rows, E_A, att_capacity)
    ffn_table = expert_table(ffn_route_rows, E_F, ffn_capacity)
    x_rows = all_inputs.reshape(row_count, D).astype(jnp.float32)
    att_gain_row = att_gain_full.astype(jnp.float32)
    att_scaled, att_normal, att_inv = rms_forward(x_rows, att_gain_row)
    att_hidden = att_scaled.astype(jnp.bfloat16)
    att_logits = jnp.dot(att_hidden, att_router_full, preferred_element_type=jnp.float32)
    att_gates = jax.nn.softmax(jnp.sum(att_hot * att_logits[:, None, :], axis=2), axis=1)
    kv_proj = jnp.einsum("rd,dkf->rkf", att_hidden, kv_full, preferred_element_type=jnp.float32)
    key_rot = rotate(
        kv_proj[:, 0].reshape(row_count, heads_local, HD), cos_part[:, None], sin_part[:, None]
    )
    key_low = key_rot.reshape(n_fsdp, tok_local, local_features).astype(jnp.bfloat16)
    value_low = kv_proj[:, 1].reshape(n_fsdp, tok_local, local_features).astype(jnp.bfloat16)
    query_in = pad_rows(att_hidden)[att_table // 2]
    query_expert = jnp.einsum(
        "ecd,def->ecf", query_in, query_full, preferred_element_type=jnp.float32
    )
    query_pre = put_slots(query_expert, att_table, 2 * row_count).reshape(
        row_count, 2, heads_local, HD
    )
    query_rot = rotate(query_pre, cos_part[:, None, None], sin_part[:, None, None])
    query_low = query_rot.reshape(n_fsdp, tok_local, 2, heads_local, HD).astype(jnp.bfloat16)

    def piece_mask(piece_rows):
        key_pos = jnp.arange(piece_rows, dtype=jnp.int32)
        allowed = (
            (query_doc[:, :, None] == doc_index[:, None, :])
            & (key_pos[None, None, :] <= query_pos[None, :, None])
            & query_keep[:, :, None]
        )
        return allowed[:, None, :, None, :]

    start_max = jnp.full((n_fsdp, heads_local, tok_local, 2), masked_score, jnp.float32)
    run_max = start_max
    key_part = lax.all_gather(key_low, "ctx", axis=1, tiled=True)
    value_part = lax.all_gather(value_low, "ctx", axis=1, tiled=True)
    piece_rows = key_part.shape[1]
    key_heads = key_part.reshape(n_fsdp, piece_rows, heads_local, HD)
    value_heads = value_part.reshape(n_fsdp, piece_rows, heads_local, HD)
    scores = (
        jnp.einsum("btshd,buhd->bhtsu", query_low, key_heads, preferred_element_type=jnp.float32)
        * score_scale
    )
    allowed = piece_mask(piece_rows)
    new_max = jnp.maximum(run_max, jnp.max(jnp.where(allowed, scores, masked_score), axis=4))
    weights = jnp.where(allowed, jnp.exp(scores - new_max[..., None]), 0.0)
    run_sum = jnp.sum(weights, axis=4)
    run_acc = jnp.einsum(
        "bhtsu,buhd->bhtsd",
        weights.astype(jnp.bfloat16),
        value_heads,
        preferred_element_type=jnp.float32,
    )
    run_max, run_sum, run_acc = (new_max, run_sum, run_acc)
    final_sum = jnp.where(run_sum > 0, run_sum, 1.0)
    head_keep = query_keep.astype(jnp.float32)[:, None, :, None]
    att_heads = run_acc / final_sum[..., None] * head_keep[..., None]
    log_total = run_max + jnp.log(final_sum)
    att_slots = (
        jnp.transpose(att_heads, (0, 2, 3, 1, 4))
        .reshape(2 * row_count, local_features)
        .astype(jnp.bfloat16)
    )
    out_in = pad_rows(att_slots)[att_table]
    out_expert = jnp.einsum("ecf,def->ecd", out_in, output_full, preferred_element_type=jnp.float32)
    out_slots = put_slots(out_expert, att_table, 2 * row_count).reshape(row_count, 2, D)
    att_part = jnp.sum(att_gates[:, :, None] * out_slots, axis=1)
    att_total = lax.psum(att_part.astype(jnp.bfloat16), "fsdp").astype(jnp.float32)
    residual = x_rows + att_total
    ffn_gain_row = ffn_gain_full.astype(jnp.float32)
    ffn_scaled, ffn_normal, ffn_inv = rms_forward(residual, ffn_gain_row)
    ffn_hidden = ffn_scaled.astype(jnp.bfloat16)
    ffn_logits = jnp.dot(ffn_hidden, ffn_router_full, preferred_element_type=jnp.float32)
    ffn_gates = jax.nn.softmax(jnp.sum(ffn_hot * ffn_logits[:, None, :], axis=2), axis=1)
    ffn_in = pad_rows(ffn_hidden)[ffn_table // 2]
    gate_up = jnp.einsum("ecd,dejf->ecjf", ffn_in, gate_up_full, preferred_element_type=jnp.float32)
    gate_pre = gate_up[:, :, 0]
    up_pre = gate_up[:, :, 1]
    sigmoid_gate = jax.nn.sigmoid(gate_pre)
    silu_gate = jax.nn.silu(gate_pre)
    activated = (silu_gate * up_pre).astype(jnp.bfloat16)
    ffn_expert = jnp.einsum(
        "ecf,def->ecd", activated, down_full, preferred_element_type=jnp.float32
    )
    ffn_slots = put_slots(ffn_expert, ffn_table, 2 * row_count).reshape(row_count, 2, D)
    ffn_part = jnp.sum(ffn_gates[:, :, None] * ffn_slots, axis=1)
    ffn_total = lax.psum(ffn_part.astype(jnp.bfloat16), "fsdp").astype(jnp.float32)
    final_rows = residual + ffn_total
    outputs = lax.dynamic_slice_in_dim(
        final_rows.reshape(n_fsdp, tok_local, D), stream_index, 1, 0
    ).astype(jnp.bfloat16)
    grad_rows = all_cot.reshape(row_count, D).astype(jnp.float32) * keep_rows
    grad_ffn_gates = jnp.sum(grad_rows[:, None, :] * ffn_slots, axis=2)
    grad_ffn_slots = (
        (ffn_gates[:, :, None] * grad_rows[:, None, :])
        .astype(jnp.bfloat16)
        .reshape(2 * row_count, D)
    )
    grad_expert = pad_rows(grad_ffn_slots)[ffn_table]
    grad_act = jnp.einsum(
        "ecd,def->ecf", grad_expert, down_full, preferred_element_type=jnp.float32
    )
    grad_gate = grad_act * up_pre * sigmoid_gate * (1.0 + gate_pre * (1.0 - sigmoid_gate))
    grad_up = grad_act * silu_gate
    grad_gate_up = jnp.stack((grad_gate, grad_up), axis=2).astype(jnp.bfloat16)
    grad_ffn_in = jnp.einsum(
        "ecjf,dejf->ecd", grad_gate_up, gate_up_full, preferred_element_type=jnp.float32
    )
    grad_ffn_hidden = add_tokens(grad_ffn_in, ffn_table, row_count)
    ffn_sum_back, ffn_gate_back = (
        lax.psum(grad_ffn_hidden.astype(jnp.bfloat16), "fsdp").astype(jnp.float32),
        lax.psum(grad_ffn_gates.astype(jnp.bfloat16), "fsdp").astype(jnp.float32),
    )
    grad_ffn_logits = router_back(ffn_gate_back, ffn_gates, ffn_hot).astype(jnp.bfloat16)
    ffn_router_term = jnp.einsum(
        "rd,re->de", ffn_hidden, grad_ffn_logits, preferred_element_type=jnp.float32
    )
    grad_hidden_two = ffn_sum_back + jnp.einsum(
        "re,de->rd", grad_ffn_logits, ffn_router_full, preferred_element_type=jnp.float32
    )
    grad_resid_part, ffn_gain_term = rms_backward(
        grad_hidden_two, ffn_normal, ffn_inv, ffn_gain_row
    )
    grad_mid = grad_rows + grad_resid_part
    gate_up_piece = jnp.einsum(
        "ecd,ecjf->dejf", ffn_in, grad_gate_up, preferred_element_type=jnp.float32
    ).reshape(D // n_ctx * lax.axis_size("ctx"), E_F, 2 * ffn_local)
    down_piece = jnp.einsum(
        "ecd,ecf->def", grad_expert, activated, preferred_element_type=jnp.float32
    )
    joined = lax.psum_scatter(
        jnp.concatenate((gate_up_piece, down_piece), axis=2).astype(jnp.bfloat16),
        "ctx",
        scatter_dimension=0,
        tiled=True,
    ).astype(jnp.float32)
    gate_up_grad = joined[:, :, : 2 * ffn_local].reshape(joined.shape[0], E_F, 2, ffn_local)
    down_grad = joined[:, :, 2 * ffn_local :]
    grad_att_gates = jnp.sum(grad_mid[:, None, :] * out_slots, axis=2)
    grad_out_slots = (
        (att_gates[:, :, None] * grad_mid[:, None, :])
        .astype(jnp.bfloat16)
        .reshape(2 * row_count, D)
    )
    grad_out_expert = pad_rows(grad_out_slots)[att_table]
    grad_out_in = jnp.einsum(
        "ecd,def->ecf", grad_out_expert, output_full, preferred_element_type=jnp.float32
    )
    output_term = jnp.einsum(
        "ecf,ecd->def", out_in, grad_out_expert, preferred_element_type=jnp.float32
    )
    grad_att = put_slots(grad_out_in, att_table, 2 * row_count).astype(jnp.bfloat16)
    grad_heads = (
        jnp.transpose(grad_att.reshape(n_fsdp, tok_local, 2, heads_local, HD), (0, 3, 1, 2, 4))
        * query_keep.astype(jnp.bfloat16)[:, None, :, None, None]
    )
    delta = jnp.sum(grad_heads.astype(jnp.float32) * att_heads, axis=4)
    key_part = lax.all_gather(key_low, "ctx", axis=1, tiled=True)
    value_part = lax.all_gather(value_low, "ctx", axis=1, tiled=True)
    piece_rows = key_part.shape[1]
    key_heads = key_part.reshape(n_fsdp, piece_rows, heads_local, HD)
    value_heads = value_part.reshape(n_fsdp, piece_rows, heads_local, HD)
    scores = (
        jnp.einsum("btshd,buhd->bhtsu", query_low, key_heads, preferred_element_type=jnp.float32)
        * score_scale
    )
    allowed = piece_mask(piece_rows)
    probs = jnp.where(allowed, jnp.exp(scores - log_total[..., None]), 0.0)
    grad_probs = jnp.einsum(
        "bhtsd,buhd->bhtsu", grad_heads, value_heads, preferred_element_type=jnp.float32
    )
    grad_scores = (probs * (grad_probs - delta[..., None])).astype(jnp.bfloat16)
    grad_query = jnp.einsum(
        "bhtsu,buhd->btshd", grad_scores, key_heads, preferred_element_type=jnp.float32
    )
    key_piece = (
        jnp.einsum(
            "bhtsu,btshd->buhd", grad_scores, query_low, preferred_element_type=jnp.float32
        ).reshape(n_fsdp, piece_rows, local_features)
        * score_scale
    )
    value_piece = jnp.einsum(
        "bhtsu,bhtsd->buhd",
        probs.astype(jnp.bfloat16),
        grad_heads,
        preferred_element_type=jnp.float32,
    ).reshape(n_fsdp, piece_rows, local_features)
    grad_keys = key_piece
    grad_values = value_piece
    grad_query, grad_keys, grad_values = (grad_query, grad_keys, grad_values)
    key_grad_own, value_grad_own = (
        lax.psum_scatter(
            grad_keys.astype(jnp.bfloat16), "ctx", scatter_dimension=1, tiled=True
        ).astype(jnp.float32),
        lax.psum_scatter(
            grad_values.astype(jnp.bfloat16), "ctx", scatter_dimension=1, tiled=True
        ).astype(jnp.float32),
    )
    grad_key_pre = unrotate(
        round_trip(key_grad_own).reshape(row_count, heads_local, HD),
        cos_part[:, None],
        sin_part[:, None],
    ).reshape(row_count, local_features)
    grad_kv = jnp.stack(
        (grad_key_pre, value_grad_own.reshape(row_count, local_features)), axis=1
    ).astype(jnp.bfloat16)
    grad_query_pre = (
        unrotate(
            round_trip(grad_query * score_scale).reshape(row_count, 2, heads_local, HD),
            cos_part[:, None, None],
            sin_part[:, None, None],
        )
        .reshape(2 * row_count, local_features)
        .astype(jnp.bfloat16)
    )
    grad_query_expert = pad_rows(grad_query_pre)[att_table]
    grad_att_in = jnp.einsum(
        "ecf,def->ecd", grad_query_expert, query_full, preferred_element_type=jnp.float32
    )
    query_term = jnp.einsum(
        "ecd,ecf->def", query_in, grad_query_expert, preferred_element_type=jnp.float32
    )
    kv_term = jnp.einsum("rd,rkf->dkf", att_hidden, grad_kv, preferred_element_type=jnp.float32)
    grad_att_hidden = add_tokens(grad_att_in, att_table, row_count) + jnp.einsum(
        "rkf,dkf->rd", grad_kv, kv_full, preferred_element_type=jnp.float32
    )
    att_sum_back, att_gate_back = (
        lax.psum(grad_att_hidden.astype(jnp.bfloat16), "fsdp").astype(jnp.float32),
        lax.psum(grad_att_gates.astype(jnp.bfloat16), "fsdp").astype(jnp.float32),
    )
    grad_att_logits = router_back(att_gate_back, att_gates, att_hot).astype(jnp.bfloat16)
    att_router_term = jnp.einsum(
        "rd,re->de", att_hidden, grad_att_logits, preferred_element_type=jnp.float32
    )
    grad_hidden_one = att_sum_back + jnp.einsum(
        "re,de->rd", grad_att_logits, att_router_full, preferred_element_type=jnp.float32
    )
    grad_input_part, att_gain_term = rms_backward(
        grad_hidden_one, att_normal, att_inv, att_gain_row
    )
    grad_input = grad_mid + grad_input_part
    input_grad = lax.dynamic_slice_in_dim(
        grad_input.reshape(n_fsdp, tok_local, D), stream_index, 1, 0
    ).astype(jnp.bfloat16)
    (
        kv_grad,
        query_grad,
        output_grad,
        att_router_grad,
        att_gain_grad,
        ffn_router_grad,
        ffn_gain_grad,
    ) = (
        lax.psum_scatter(
            kv_term.astype(jnp.bfloat16), "ctx", scatter_dimension=0, tiled=True
        ).astype(jnp.float32),
        lax.psum_scatter(
            query_term.astype(jnp.bfloat16), "ctx", scatter_dimension=0, tiled=True
        ).astype(jnp.float32),
        lax.psum_scatter(
            output_term.astype(jnp.bfloat16), "ctx", scatter_dimension=0, tiled=True
        ).astype(jnp.float32),
        lax.psum_scatter(
            att_router_term.astype(jnp.bfloat16), "ctx", scatter_dimension=0, tiled=True
        ).astype(jnp.float32),
        lax.psum_scatter(
            att_gain_term.astype(jnp.bfloat16), "ctx", scatter_dimension=0, tiled=True
        ).astype(jnp.float32),
        lax.psum_scatter(
            ffn_router_term.astype(jnp.bfloat16), "ctx", scatter_dimension=0, tiled=True
        ).astype(jnp.float32),
        lax.psum_scatter(
            ffn_gain_term.astype(jnp.bfloat16), "ctx", scatter_dimension=0, tiled=True
        ).astype(jnp.float32),
    )
    return (
        outputs,
        input_grad,
        kv_grad,
        query_grad,
        output_grad,
        att_router_grad,
        att_gain_grad,
        gate_up_grad,
        down_grad,
        ffn_router_grad,
        ffn_gain_grad,
    )


def solution(mesh):
    in_specs = (
        P("fsdp", "ctx", None),
        P("fsdp", "ctx", None),
        P(),
        P("ctx", None, None),
        P("ctx", None, None),
        P("ctx", None, "fsdp"),
        P("ctx", None, "fsdp"),
        P("ctx", None, "fsdp"),
        P("ctx", None),
        P("ctx"),
        P("ctx", None, None, "fsdp"),
        P("ctx", None, "fsdp"),
        P("ctx", None),
        P("ctx"),
    )
    out_specs = (
        P("fsdp", "ctx", None),
        P("fsdp", "ctx", None),
        P("ctx", None, "fsdp"),
        P("ctx", None, "fsdp"),
        P("ctx", None, "fsdp"),
        P("ctx", None),
        P("ctx"),
        P("ctx", None, None, "fsdp"),
        P("ctx", None, "fsdp"),
        P("ctx", None),
        P("ctx"),
    )
    return jax.shard_map(
        per_device, mesh=mesh, in_specs=in_specs, out_specs=out_specs, check_vma=False
    )
```

profile of v0, /device:TPU:0, one launch (start us, length us, event | category | flops | bytes accessed | tf_op | source)
XLA Modules:
  0.0 2660.2 jit_solution(15851419901239234152)
XLA Ops:
  23.9 16.4 all-gather.12.cloned.1.call-done
  43.4 35.6 %all-gather.16.cloned.1.call-done = bf16[2048,2,512]{2,0,1:T(8,128)(2,1)} async-done(((bf16[256,2,512]{2,0,1:T(8,128)(2,1)}), bf16[2048,2,512]{2,0,1:T(8,128)(2,1)}) %all-gather.16.cloned.1.call-update) | async-done | bytes 4194320 | tf_op jit(solution)/shard_map/all_gather | solution.py:158
  102.6 22.1 scatter_fusion
  150.6 85.2 %all-gather.14.cloned.1.call-done = bf16[2048,8,512]{2,0,1:T(8,128)(2,1)} async-done(((bf16[256,8,512]{2,0,1:T(8,128)(2,1)}), bf16[2048,8,512]{2,0,1:T(8,128)(2,1)}) %all-gather.14.cloned.1.call-update) | async-done | bytes 16777232 | tf_op jit(solution)/shard_map/all_gather | solution.py:159
  267.5 60.5 %all-gather.22.cloned.1.call-done = bf16[2048,8,512]{2,0,1:T(8,128)(2,1)} async-done(((bf16[256,8,512]{2,0,1:T(8,128)(2,1)}), bf16[2048,8,512]{2,0,1:T(8,128)(2,1)}) %all-gather.22.cloned.1.call-update) | async-done | bytes 16777232 | tf_op jit(solution)/shard_map/all_gather | solution.py:160
  328.0 13.3 fusion.100
  341.3 11.4 scatter_custom_fusion.2
  373.4 16.4 copy.423
  410.4 22.1 scatter_fusion.1
  461.6 376.0 %all-gather.24.cloned.1.call-done = bf16[2048,8,2,1408]{3,0,2,1:T(8,128)(2,1)} async-done(((bf16[256,8,2,1408]{3,0,2,1:T(8,128)(2,1)}), bf16[2048,8,2,1408]{3,0,2,1:T(8,128)(2,1)}) %all-gather.24.cloned.1.call-update) | async-done | bytes 92274704 | tf_op jit(solution)/shard_map/all_gather | solution.py:163
  837.6 41.1 %fusion.102 = f32[8,80,2,1408]{3,1,2,0:T(8,128)} fusion(bf16[8,80,2048,1]{2,1,3,0:T(8,128)(2,1)} %bitcast.249, bf16[2048,8,2,1408]{3,0,2,1:T(8,128)(2,1)} %all-gather.24.cloned.1.call-done), kind=kOutput, calls=%fused_computation.260 | convolution fusion | flops 7381975040 | bytes 102105088 | tf_op jit(solution)/shard_map/ecd,dejf->ecjf/dot_general | solution.py:263
  882.8 171.6 %all-gather.26.cloned.1.call-done = bf16[2048,8,1408]{2,0,1:T(8,128)(2,1)} async-done(((bf16[256,8,1408]{2,0,1:T(8,128)(2,1)}), bf16[2048,8,1408]{2,0,1:T(8,128)(2,1)}) %all-gather.26.cloned.1.call-update) | async-done | bytes 46137360 | tf_op jit(solution)/shard_map/all_gather | solution.py:164
  1054.4 23.8 fusion.103
  1078.2 11.8 scatter_custom_fusion.4
  1096.1 11.7 psum.45
  1114.9 21.6 fusion.40
  1136.4 38.4 %fusion = f32[8,80,2048,1]{2,1,0,3:T(8,128)} fusion(bf16[2048,8,2,1408]{3,0,2,1:T(8,128)(2,1)} %all-gather.24.cloned.1.call-done, bf16[8,80,1,1408]{3,1,0,2:T(8,128)(2,1)} %get-tuple-element.115, bf16[8,80,1,1408]{3,1,0,2:T(8,128)(2,1)S(1)} %get-tuple-element.114), kind=kOutput, calls=%fused_computation.15 | convolution fusion | flops 7383777280 | bytes 101122048 | tf_op jit(solution)/shard_map/ecjf,dejf->ecd/dot_general | solution.py:293
  1174.9 16.4 scatter_custom_fusion.5
  1194.3 48.9 %all-reduce.20.cloned.1.call-done = bf16[256,2048]{1,0:T(8,128)(2,1)} async-done(((bf16[256,2048]{1,0:T(8,128)(2,1)}), bf16[256,2048]{1,0:T(8,128)(2,1)}) %all-reduce.20.cloned.1.call-update) | async-done | bytes 1048592 | tf_op jit(solution)/shard_map/psum | solution.py:298
  1343.2 13.3 fusion.105
  1356.6 16.1 scatter_custom_fusion.7
  1372.7 11.6 all-reduce.22.cloned.1.call-done
  1417.1 19.6 convert_bitcast_fusion
  1436.8 63.9 %copy.364 = bf16[2048,8,1408]{2,1,0:T(8,128)(2,1)} copy(bf16[2048,8,1408]{0,2,1:T(8,128)(2,1)} %convert_bitcast_fusion) | data formatting | bytes 92274688 | tf_op jit(solution)/shard_map/ecd,ecf->def/transpose | solution.py:315
  1500.7 36.0 %convolution_convert_fusion = bf16[8,2,1408,2048]{3,2,1,0:T(8,128)(2,1)} fusion(bf16[8,80,2048,1]{2,1,3,0:T(8,128)(2,1)S(1)} %bitcast.250, bf16[8,80,1,1408]{3,1,0,2:T(8,128)(2,1)} %get-tuple-element.115, bf16[8,80,1,1408]{3,1,0,2:T(8,128)(2,1)} %copy-done.30), kind=kOutput, calls=%fused_computation.17 | convolution fusion | flops 7429914624 | bytes 98500608 | tf_op jit(solution)/shard_map/ecd,ecjf->dejf/dot_general | solution.py:312
  1536.7 130.8 %copy.363 = bf16[2048,8,2816]{2,1,0:T(8,128)(2,1)} copy(bf16[2048,8,2816]{0,2,1:T(8,128)(2,1)} %bitcast.66) | data formatting | bytes 184549376 | tf_op jit(solution)/shard_map/reshape | solution.py:314
  1667.5 97.4 %pad_maximum_fusion = bf16[2048,8,4224]{2,1,0:T(8,128)(2,1)} fusion(bf16[2048,8,1408]{2,1,0:T(8,128)(2,1)} %copy.364, bf16[2048,8,2816]{2,1,0:T(8,128)(2,1)} %copy.363), kind=kLoop, calls=%fused_computation.14 | loop fusion | flops 276824064 | bytes 276824064 | tf_op jit(solution)/shard_map/concatenate | solution.py:319
  1772.0 13.4 all-reduce.10
  1799.3 39.9 %reduce-scatter.11.cloned.1.call-done = bf16[256,8,512]{2,0,1:T(8,128)(2,1)} async-done(((bf16[2048,8,512]{2,0,1:T(8,128)(2,1)}), bf16[256,8,512]{2,0,1:T(8,128)(2,1)}) %reduce-scatter.11.cloned.1.call-update) | async-done | bytes 2097168 | tf_op jit(solution)/shard_map/reduce_scatter | solution.py:447
  1844.0 761.3 %reduce-scatter.15.cloned.1.call-done = bf16[256,8,4224]{2,1,0:T(8,128)(2,1)} async-done(((bf16[2048,8,4224]{2,1,0:T(8,128)(2,1)}), bf16[256,8,4224]{2,1,0:T(8,128)(2,1)}) %reduce-scatter.15.cloned.1.call-update) | async-done | bytes 17301520 | tf_op jit(solution)/shard_map/reduce_scatter | solution.py:318
  2605.4 13.0 slice.135
  2618.4 27.0 %reshape.702 = f32[256,8,2,1408]{3,2,1,0:T(2,128)} reshape(f32[256,8,2816]{2,1,0:T(8,128)} %slice.135) | data formatting | bytes 46137344 | tf_op jit(solution)/shard_map/reshape | solution.py:324
  (399 shorter events, 355.4 us)
Async XLA Ops:
  7.2 33.1 %all-gather.12.cloned.1.call-start = ((), (), s32[]{:S(2)}) async-start(), calls=%async_computation.6 | async-start | bytes 1310720 | tf_op jit(solution)/shard_map/all_gather | solution.py:169
  7.9 71.1 %all-gather.16.cloned.1.call-start = ((), (), s32[]{:S(2)}) async-start(), calls=%async_computation.8 | async-start | bytes 4718592 | tf_op jit(solution)/shard_map/all_gather | solution.py:158
  10.2 132.9 %all-gather.18.cloned.1.call-start = ((), (), s32[]{:S(2)}) async-start(), calls=%async_computation.9 | async-start | bytes 2359296 | tf_op jit(solution)/shard_map/all_gather | solution.py:222
  23.3 59.1 %copy-start.45 = (f32[8,1,256]{2,1,0:T(1,128)}, f32[8,1,256]{2,1,0:T(1,128)S(1)}, u32[]{:S(2)}) copy-start(f32[8,1,256]{2,1,0:T(1,128)S(1)} %convert_element_type.366) | copy-start | bytes 24580
  23.9 231.8 %copy-start.24 = (f32[256,64]{1,0:T(8,128)}, f32[256,64]{1,0:T(8,128)S(1)}, u32[]{:S(2)}) copy-start(f32[256,64]{1,0:T(8,128)S(1)} %get-tuple-element.140) | copy-start | bytes 196612
  23.9 231.8 %copy-start.26 = (f32[256,64]{1,0:T(8,128)}, f32[256,64]{1,0:T(8,128)S(1)}, u32[]{:S(2)}) copy-start(f32[256,64]{1,0:T(8,128)S(1)} %get-tuple-element.141) | copy-start | bytes 196612
  41.9 40.6 %copy-start.62 = (f32[256]{0:T(256)}, f32[256]{0:T(256)S(1)}, u32[]{:S(2)}) copy-start(f32[256]{0:T(256)S(1)} %rsqrt.20) | copy-start | bytes 3076
  43.4 95.4 %copy-start.4 = (bf16[256,2048]{1,0:T(8,128)(2,1)}, bf16[256,2048]{1,0:T(8,128)(2,1)S(1)}, u32[]{:S(2)}) copy-start(bf16[256,2048]{1,0:T(8,128)(2,1)S(1)} %fusion.23) | copy-start | bytes 3145732
  85.3 60.6 %all-gather.20.cloned.1.call-start = ((), (), s32[]{:S(2)}) async-start(), calls=%async_computation.10 | async-start | bytes 2359296 | tf_op jit(solution)/shard_map/all_gather | solution.py:223
  87.4 148.5 %all-gather.14.cloned.1.call-start = ((), (), s32[]{:S(2)}) async-start(), calls=%async_computation.7 | async-start | bytes 18874368 | tf_op jit(solution)/shard_map/all_gather | solution.py:159
  93.2 234.9 %all-gather.22.cloned.1.call-start = ((), (), s32[]{:S(2)}) async-start(), calls=%async_computation.11 | async-start | bytes 18874368 | tf_op jit(solution)/shard_map/all_gather | solution.py:160
  99.0 342.1 %all-gather.28.cloned.1.call-start = ((), (), s32[]{:S(2)}) async-start(), calls=%async_computation.15 | async-start | bytes 1310720 | tf_op jit(solution)/shard_map/all_gather | solution.py:170
  99.8 354.5 %all-reduce.18.cloned.1.call-start = ((), (), s32[]{:S(2)}) async-start(), calls=%async_computation.12 | async-start | bytes 2097152 | tf_op jit(solution)/shard_map/psum | solution.py:255
  137.0 122.6 %copy-start.31 = (pred[4,64,512]{2,1,0:T(8,128)(4,1)}, pred[4,64,512]{2,1,0:T(8,128)(4,1)S(1)}, u32[]{:S(2)}) copy-start(pred[4,64,512]{2,1,0:T(8,128)(4,1)S(1)} %and_and_fusion) | copy-start | bytes 393220
  145.9 111.4 %copy-start.6 = (bf16[4,512,512]{1,2,0:T(8,128)(2,1)}, bf16[4,512,512]{1,2,0:T(8,128)(2,1)S(1)}, u32[]{:S(2)}) copy-start(bf16[4,512,512]{1,2,0:T(8,128)(2,1)S(1)} %copy.327) | copy-start | bytes 6291460
  267.5 73.8 %copy-start.21 = (bf16[640,512]{1,0:T(8,128)(2,1)}, bf16[640,512]{1,0:T(8,128)(2,1)S(1)}, u32[]{:S(2)}) copy-start(bf16[640,512]{1,0:T(8,128)(2,1)S(1)} %gather_fusion.1) | copy-start | bytes 1966084
  373.3 464.2 %all-gather.24.cloned.1.call-start = ((), (), s32[]{:S(2)}) async-start(), calls=%async_computation.13 | async-start | bytes 103809024 | tf_op jit(solution)/shard_map/all_gather | solution.py:163
  389.8 664.5 %all-gather.26.cloned.1.call-start = ((), (), s32[]{:S(2)}) async-start(), calls=%async_computation.14 | async-start | bytes 51904512 | tf_op jit(solution)/shard_map/all_gather | solution.py:164
  398.5 844.7 %all-reduce.20.cloned.1.call-start = ((), (), s32[]{:S(2)}) async-start(), calls=%async_computation.16 | async-start | bytes 2097152 | tf_op jit(solution)/shard_map/psum | solution.py:298
  882.8 195.4 %copy-start.16 = (bf16[8,80,1408]{2,1,0:T(8,128)(2,1)}, bf16[8,80,1408]{2,1,0:T(8,128)(2,1)S(1)}, u32[]{:S(2)}) copy-start(bf16[8,80,1408]{2,1,0:T(8,128)(2,1)S(1)} %multiply_convert_fusion.5) | copy-start | bytes 5406724
  1136.4 38.4 %copy-start.30 = (bf16[8,80,1,1408]{3,1,0,2:T(8,128)(2,1)}, bf16[8,80,1,1408]{3,1,0,2:T(8,128)(2,1)S(1)}, u32[]{:S(2)}) copy-start(bf16[8,80,1,1408]{3,1,0,2:T(8,128)(2,1)S(1)} %get-tuple-element.114) | copy-start | bytes 5406724
  1174.9 68.3 %copy-start.13 = (bf16[256,2048]{1,0:T(8,128)(2,1)S(1)}, bf16[256,2048]{1,0:T(8,128)(2,1)}, u32[]{:S(2)}) copy-start(bf16[256,2048]{1,0:T(8,128)(2,1)} %all-reduce.18.cloned.1.call-done) | copy-start | bytes 3145732
  1194.0 190.3 %all-reduce.22.cloned.1.call-start = ((), (), s32[]{:S(2)}) async-start(), calls=%async_computation.23 | async-start | bytes 8388608
  1194.3 51.8 %copy-start.23 = (bf16[4,64,2048]{2,1,0:T(8,128)(2,1)S(1)}, bf16[4,64,2048]{2,1,0:T(8,128)(2,1)}, u32[]{:S(2)}) copy-start(bf16[4,64,2048]{2,1,0:T(8,128)(2,1)} %all-gather.28.cloned.1.call-done) | copy-start | bytes 3145732
  1303.6 462.2 %reduce-scatter.17.cloned.1.call-start = ((), (), s32[]{:S(2)}) async-start(), calls=%async_computation.22 | async-start | bytes 36864 | tf_op jit(solution)/shard_map/reduce_scatter | solution.py:456
  1322.7 444.6 %reduce-scatter.13.cloned.1.call-start = ((), (), s32[]{:S(2)}) async-start(), calls=%async_computation.20 | async-start | bytes 36864 | tf_op jit(solution)/shard_map/reduce_scatter | solution.py:450
  1343.2 425.4 %all-reduce.24.cloned.1.call-start = ((), (), s32[]{:S(2)}) async-start(), calls=%async_computation.24 | async-start | bytes 4194304 | tf_op jit(solution)/shard_map/psum | solution.py:274
  1392.0 399.7 %reduce-scatter.7.cloned.1.call-start = ((), (), s32[]{:S(2)}) async-start(), calls=%async_computation.17 | async-start | bytes 4718592 | tf_op jit(solution)/shard_map/reduce_scatter | solution.py:441
  1395.4 398.8 %reduce-scatter.9.cloned.1.call-start = ((), (), s32[]{:S(2)}) async-start(), calls=%async_computation.18 | async-start | bytes 18874368 | tf_op jit(solution)/shard_map/reduce_scatter | solution.py:444
  1405.7 433.5 %reduce-scatter.11.cloned.1.call-start = ((), (), s32[]{:S(2)}) async-start(), calls=%async_computation.19 | async-start | bytes 18874368 | tf_op jit(solution)/shard_map/reduce_scatter | solution.py:447
  1415.7 1189.7 %reduce-scatter.15.cloned.1.call-start = ((), (), s32[]{:S(2)}) async-start(), calls=%async_computation.21 | async-start | bytes 155713536 | tf_op jit(solution)/shard_map/reduce_scatter | solution.py:318
  1436.8 63.9 %copy-start.9 = (bf16[640,2048]{1,0:T(8,128)(2,1)S(1)}, bf16[640,2048]{1,0:T(8,128)(2,1)}, u32[]{:S(2)}) copy-start(bf16[640,2048]{1,0:T(8,128)(2,1)} %gather_fusion.2) | copy-start | bytes 7864324
  (57 other events, 348.5 us)
Sparse Core Ops, SparseCore 0:
  9.6 30.6 all-gather.11
  42.7 36.1 all-gather.15
  85.4 27.8 all-gather.17
  115.7 27.8 all-gather.19
  145.9 89.8 all-gather.13
  238.1 89.8 all-gather.21
  329.6 27.9 all-gather.27
  373.4 51.8 all-reduce.17
  428.0 409.5 all-gather.23
  840.1 214.2 all-gather.25
  1194.1 49.0 all-reduce.19
  1303.7 80.6 all-reduce.21
  1388.2 31.3 reduce-scatter.16
  1423.0 31.2 reduce-scatter.12
  1457.3 87.0 all-reduce.23
  1548.1 50.2 reduce-scatter.6
  1602.9 115.9 reduce-scatter.8
  1722.7 116.4 reduce-scatter.10
  1843.3 762.0 reduce-scatter.14
where the time goes:
time: 2680 us; the launch traced here: 2660 us
  waiting for transfers between devices  1610 us (60%)
  local copies, waits for them, and re-layouts  482 us (18%)
  matrix products  279 us (10%)
  other arithmetic  201 us (8%)
  blocking collectives  71.9 us (3%)
    reduce_scatter x1, waiting for transfers between devices, per_device(): lax.psum_scatter(jnp.concatenate((gate_up_piece, down_piece), axis=2).ast...  761 us
    all_gather x1, waiting for transfers between devices, per_device(): lax.all_gather(gate_up_weight.astype(jnp.bfloat16), 'ctx', axis=0, tiled=...  376 us
    all_gather x1, waiting for transfers between devices, per_device(): lax.all_gather(down_weight.astype(jnp.bfloat16), 'ctx', axis=0, tiled=True)  172 us
    reshape x1, local copies, waits for them, and re-layouts, per_device(): gate_up_piece = jnp.einsum('ecd,ecjf->dejf', ffn_in, grad_gate_up, prefer...  131 us
    concatenate x1, other arithmetic, per_device(): jnp.concatenate((gate_up_piece, down_piece), axis=2).astype(jnp.bfloat16)  97.4 us
    all_gather x1, waiting for transfers between devices, per_device(): lax.all_gather(query_weight.astype(jnp.bfloat16), 'ctx', axis=0, tiled=True)  85.2 us
    unnamed x154, local copies, waits for them, and re-layouts  65.2 us
    transpose x1, local copies, waits for them, and re-layouts, per_device(): jnp.einsum('ecd,ecf->def', grad_expert, activated, preferred_element_type...  63.9 us
  transfers between devices with their start and end apart: 19, of which 10 were waited for; matrix products, arithmetic and copies ran while one was open for 27% of the time, Pallas kernels for 0%

commit v1 on v0

v1 whole, which is shorter than its diff:
```python
import functools

import jax
import jax.numpy as jnp
from jax import lax
from jax.experimental import pallas as pl
from jax.experimental.pallas import tpu as pltpu
from jax.sharding import PartitionSpec as P

D = 2048
HEADS = 16
HD = 128
E_A = 8
E_F = 8
FF = 5632
DOCS = 3

norm_eps = 1e-06
rope_base = 10000.0
masked_score = -1e30

BF = jnp.bfloat16
F32 = jnp.float32
VMEM_CAP = 60 * 1024 * 1024


def dot(a, b):
    return lax.dot_general(a, b, (((1,), (0,)), ((), ())), preferred_element_type=F32)


def dot_nt(a, b):
    return lax.dot_general(a, b, (((1,), (1,)), ((), ())), preferred_element_type=F32)


def dot_tn(a, b):
    return lax.dot_general(a, b, (((0,), (0,)), ((), ())), preferred_element_type=F32)


def spec(shape, index=None):
    if index is not None:
        return pl.BlockSpec(shape, index)
    zeros = (0,) * len(shape)
    return pl.BlockSpec(shape, lambda *_: zeros, pipeline_mode=pl.Buffered(1))


def call(body, sc, grid, in_specs, out_specs, out_shape, scratch=(), aliases=None, flops=0, size=0):
    return functools.partial(
        pl.pallas_call(
            body,
            out_shape=out_shape,
            grid_spec=pltpu.PrefetchScalarGridSpec(
                num_scalar_prefetch=1,
                grid=grid,
                in_specs=in_specs,
                out_specs=jax.tree.map(
                    lambda s: pl.BlockSpec(s.block_shape, s.index_map), out_specs
                ),
                scratch_shapes=list(scratch),
            ),
            input_output_aliases=aliases or {},
            compiler_params=pltpu.CompilerParams(
                dimension_semantics=("arbitrary",) * len(grid), vmem_limit_bytes=VMEM_CAP
            ),
            cost_estimate=pl.CostEstimate(flops=flops, bytes_accessed=size, transcendentals=0),
        ),
        sc,
    )


def proj_body(n_extra, width, sc, route, xo, xt, *refs):
    wm, wt = refs[0], refs[1]
    out = refs[-1]
    a, b = xo[...], xt[...]
    r0, r1 = route[:, 0:1], route[:, 1:2]
    acc0 = jnp.zeros((a.shape[0], width), F32)
    acc1 = acc0
    for e in range(E_A):
        r = dot(a, wm[e]) + dot(b, wt[e])
        acc0 = jnp.where(r0 == e, r, acc0)
        acc1 = jnp.where(r1 == e, r, acc1)
    out[:, 0:width] = acc0.astype(BF)
    out[:, width : 2 * width] = acc1.astype(BF)
    if n_extra:
        km, kt = refs[2], refs[3]
        for i in range(n_extra):
            out[:, (2 + i) * width : (3 + i) * width] = (dot(a, km[i]) + dot(b, kt[i])).astype(BF)


def rotate(u, cosf, sinf):
    return u * cosf + pltpu.roll(u, HD // 2, 1) * sinf


def unrotate(u, cosf, sinf):
    return u * cosf - pltpu.roll(u, HD // 2, 1) * sinf


def add_halves(refs):
    a0, a1, b0, b1 = refs
    top = a0[...].astype(F32) + a1[...].astype(F32)
    low = b0[...].astype(F32) + b1[...].astype(F32)
    return jnp.concatenate((top, low), axis=0)


def allowed_pairs(doc_col, doc_row):
    n = doc_col.shape[0]
    t = lax.broadcasted_iota(jnp.int32, (n, n), 0)
    u = lax.broadcasted_iota(jnp.int32, (n, n), 1)
    return (doc_col[...] == doc_row[...]) & (u <= t) & (doc_col[...] < DOCS)


def attend_body(hc, sc, a0, a1, b0, b1, doc_col, doc_row, cosr, sinr, qkv, out, lse):
    width = hc * HD
    u = add_halves((a0, a1, b0, b1))
    cosf, sinf = cosr[...], sinr[...]
    ok = allowed_pairs(doc_col, doc_row)
    for h in range(hc):
        at = 2 * width + h * HD
        k = rotate(u[:, at : at + HD], cosf, sinf).astype(BF)
        v = u[:, at + width : at + width + HD].astype(BF)
        qkv[:, at : at + HD] = k
        qkv[:, at + width : at + width + HD] = v
        for j in range(2):
            lo = j * width + h * HD
            q = rotate(u[:, lo : lo + HD], cosf, sinf).astype(BF)
            qkv[:, lo : lo + HD] = q
            s = jnp.where(ok, dot_nt(q, k) * (HD**-0.5), masked_score)
            m = jnp.max(s, axis=1, keepdims=True)
            p = jnp.where(ok, jnp.exp(s - m), 0.0)
            total = jnp.sum(p, axis=1, keepdims=True)
            total = jnp.where(total > 0, total, 1.0)
            out[:, lo : lo + HD] = (dot(p.astype(BF), v) / total).astype(BF)
            lse[:, 2 * h + j : 2 * h + j + 1] = m + jnp.log(total)


def attend_back_body(hc, sc, a0, a1, b0, b1, qkv, att, lse, gates, doc_col, doc_row, cosr, sinr, grads, dgate):
    width = hc * HD
    u = add_halves((a0, a1, b0, b1))
    cosf, sinf = cosr[...], sinr[...]
    ok = allowed_pairs(doc_col, doc_row)
    keep = (doc_col[...] < DOCS).astype(F32)
    dg = [jnp.zeros((u.shape[0], 1), F32) for _ in range(2)]
    for h in range(hc):
        at = 2 * width + h * HD
        k = qkv[:, at : at + HD]
        v = qkv[:, at + width : at + width + HD]
        dk = jnp.zeros((u.shape[0], HD), F32)
        dv = dk
        for j in range(2):
            lo = j * width + h * HD
            q = qkv[:, lo : lo + HD]
            o = att[:, lo : lo + HD].astype(F32)
            raw = u[:, lo : lo + HD]
            dg[j] = dg[j] + jnp.sum(raw * o, axis=1, keepdims=True)
            do = (raw * (gates[:, j : j + 1] * keep)).astype(BF)
            delta = jnp.sum(do.astype(F32) * o, axis=1, keepdims=True)
            s = dot_nt(q, k) * (HD**-0.5)
            p = jnp.where(ok, jnp.exp(s - lse[:, 2 * h + j : 2 * h + j + 1]), 0.0)
            ds = (p * (dot_nt(do, v) - delta)).astype(BF)
            dq = dot(ds, k) * (HD**-0.5)
            grads[:, lo : lo + HD] = unrotate(dq, cosf, sinf).astype(BF)
            dk = dk + dot_tn(ds, q)
            dv = dv + dot_tn(p.astype(BF), do)
        grads[:, at : at + HD] = unrotate(dk * (HD**-0.5), cosf, sinf).astype(BF)
        grads[:, at + width : at + width + HD] = dv.astype(BF)
    dgate[...] = jnp.zeros_like(dgate)
    dgate[:, 0:1] = dg[0]
    dgate[:, 1:2] = dg[1]


def chosen(route, vals, lo, width, e, scale=None):
    a = vals[:, lo : lo + width].astype(F32)
    b = vals[:, lo + width : lo + 2 * width].astype(F32)
    s0 = scale[:, 0:1] if scale is not None else 1.0
    s1 = scale[:, 1:2] if scale is not None else 1.0
    w0 = jnp.where(route[:, 0:1] == e, s0, 0.0)
    w1 = jnp.where(route[:, 1:2] == e, s1, 0.0)
    return (a * w0 + b * w1).astype(BF)


def att_out_body(width, sc, route, gates, om, ot, wm, wt, prev, out):
    acc = jnp.zeros(out.shape[1:], F32)
    for e in range(E_A):
        acc += dot_nt(chosen(route, om, 0, width, e, gates), wm[e])
        acc += dot_nt(chosen(route, ot, 0, width, e, gates), wt[e])
    out[0] = acc.astype(BF)


def att_in_back_body(width, sc, route, gm, gt, wm, wt, km, kt, prev, out):
    acc = jnp.zeros(out.shape[1:], F32)
    for e in range(E_A):
        acc += dot_nt(chosen(route, gm, 0, width, e), wm[e])
        acc += dot_nt(chosen(route, gt, 0, width, e), wt[e])
    for i in range(2):
        lo = (2 + i) * width
        acc += dot_nt(gm[:, lo : lo + width], km[i]) + dot_nt(gt[:, lo : lo + width], kt[i])
    out[0] = acc.astype(BF)


def att_weight_body(width, n, gated, extra, sc, *refs):
    xt, route, gates = refs[0], refs[1], refs[2]
    pieces = refs[3 : 3 + 2 * n]
    out = refs[3 + 2 * n]
    out2 = refs[4 + 2 * n] if extra else None
    half = pl.program_id(0)
    e = pl.program_id(1)
    for side in range(2):

        @pl.when(half == side)
        def _():
            acc = jnp.zeros((xt.shape[1], width), F32)
            for k in range(n):
                s = sc[k]
                sel = chosen(route[s], pieces[2 * k + side], 0, width, e, gates[s] if gated else None)
                acc += dot(xt[s], sel)
            out[0] = acc
            if extra:

                @pl.when(e < 2)
                def _():
                    acc = jnp.zeros((xt.shape[1], width), F32)
                    for k in range(n):
                        vals = pieces[2 * k + side]
                        both = [vals[:, (2 + i) * width : (3 + i) * width] for i in range(2)]
                        acc += dot(xt[sc[k]], jnp.where(e == 0, both[0].astype(F32), both[1].astype(F32)).astype(BF))
                    out2[0] = acc


def row_chunks(rows):
    step = min(rows, 1024)
    return [(i, step) for i in range(0, rows, step)]


def group_proj_body(sc, pos, xo, xt, wm, wt, out, xs):
    i = pl.program_id(0)
    ts = out.shape[0]
    dc = xo.shape[1]
    p0, first, last = sc[0], sc[1], sc[2]

    @pl.when(i == 0)
    def _():
        a = jnp.zeros((ts, dc), F32)
        b = a
        for lo, n in row_chunks(xo.shape[0]):
            ids = p0 + lax.broadcasted_iota(jnp.int32, (ts, n), 0)
            hot = (pos[0:1, lo : lo + n] == ids) | (pos[1:2, lo : lo + n] == ids)
            hot = jnp.where(hot, 1.0, 0.0).astype(BF)
            a = a + dot(hot, xo[lo : lo + n, :])
            b = b + dot(hot, xt[lo : lo + n, :])
        xs[:, 0:dc] = a.astype(BF)
        xs[:, dc : 2 * dc] = b.astype(BF)
        out[...] = (dot(xs[:, 0:dc], wm[0]) + dot(xs[:, dc : 2 * dc], wt[0])).astype(BF)

    e = jnp.minimum(first + i, last)

    @pl.when((i > 0) & (first + i <= last))
    def _():
        rows = p0 + lax.broadcasted_iota(jnp.int32, (ts, 1), 0)
        r = dot(xs[:, 0:dc], wm[0]) + dot(xs[:, dc : 2 * dc], wt[0])
        out[...] = jnp.where(rows >= sc[3 + e], r, out[...].astype(F32)).astype(BF)


def middle_body(fl, sc, pos, rowv, g0, g1, d0, d1, dgu, act, tok):
    ts = g0.shape[0]
    rows = pos.shape[1]
    p0 = sc[0]
    inv = jnp.zeros((ts, 1), F32)
    gate = inv
    for lo, n in row_chunks(rows):
        ids = p0 + lax.broadcasted_iota(jnp.int32, (ts, n), 0)
        is0 = jnp.where(pos[0:1, lo : lo + n] == ids, 1.0, 0.0)
        is1 = jnp.where(pos[1:2, lo : lo + n] == ids, 1.0, 0.0)
        inv += jnp.sum((is0 + is1) * rowv[0:1, lo : lo + n], axis=1, keepdims=True)
        gate += jnp.sum(is0 * rowv[1:2, lo : lo + n] + is1 * rowv[2:3, lo : lo + n], axis=1, keepdims=True)
    dpf = jnp.zeros((ts, 1), F32)
    dn = dpf
    step = 128
    for lo in range(0, fl, step):
        gt = (g0[:, lo : lo + step].astype(F32) + g1[:, lo : lo + step].astype(F32)) * inv
        up = (g0[:, fl + lo : fl + lo + step].astype(F32) + g1[:, fl + lo : fl + lo + step].astype(F32)) * inv
        raw = d0[:, lo : lo + step].astype(F32) + d1[:, lo : lo + step].astype(F32)
        sg = 1.0 / (1.0 + jnp.exp(-gt))
        silu = gt * sg
        a = (silu * up).astype(BF)
        act[:, lo : lo + step] = a
        da = raw * gate
        dgt = da * up * (sg * (1.0 + gt * (1.0 - sg)))
        dup = da * silu
        dgu[:, lo : lo + step] = dgt.astype(BF)
        dgu[:, fl + lo : fl + lo + step] = dup.astype(BF)
        dpf += jnp.sum(raw * a.astype(F32), axis=1, keepdims=True)
        dn += jnp.sum(dgt * gt + dup * up, axis=1, keepdims=True)
    for lo, n in row_chunks(rows):
        ids = p0 + lax.broadcasted_iota(jnp.int32, (ts, n), 0)
        is0 = jnp.where(pos[0:1, lo : lo + n] == ids, 1.0, 0.0)
        is1 = jnp.where(pos[1:2, lo : lo + n] == ids, 1.0, 0.0)
        t0 = jnp.sum(is0 * dpf, axis=0, keepdims=True)
        t1 = jnp.sum(is1 * dpf, axis=0, keepdims=True)
        t2 = jnp.sum((is0 + is1) * dn, axis=0, keepdims=True)
        tok[:, lo : lo + n] = jnp.concatenate((t0, t1, t2, jnp.zeros((5, n), F32)), axis=0)


def group_back_body(sc, posc, wcol, d, w, prev, out, dh):
    i = pl.program_id(0)
    ts = d.shape[0]
    p0, first, last = sc[0], sc[1], sc[2]
    e = jnp.minimum(first + i, last)

    @pl.when(i == 0)
    def _():
        dh[...] = dot_nt(d[...], w[0])

    @pl.when((i > 0) & (first + i <= last))
    def _():
        rows = p0 + lax.broadcasted_iota(jnp.int32, (ts, 1), 0)
        dh[...] = jnp.where(rows >= sc[3 + e], dot_nt(d[...], w[0]), dh[...])

    @pl.when(i == pl.num_programs(0) - 1)
    def _():
        vals = dh[...].astype(BF)
        for lo, n in row_chunks(out.shape[0]):
            ids = p0 + lax.broadcasted_iota(jnp.int32, (n, ts), 1)
            hot = jnp.where(posc[lo : lo + n, 0:1] == ids, wcol[lo : lo + n, 0:1], 0.0)
            hot = hot + jnp.where(posc[lo : lo + n, 1:2] == ids, wcol[lo : lo + n, 1:2], 0.0)
            out[lo : lo + n, :] = prev[lo : lo + n, :] + dot(hot.astype(BF), vals)


def sort_t_body(sc, posc, wcol, xt, out):
    p0 = sc[pl.program_id(0)]
    ts = out.shape[1]
    acc = jnp.zeros(out.shape, F32)
    for lo, n in row_chunks(xt.shape[1]):
        ids = p0 + lax.broadcasted_iota(jnp.int32, (n, ts), 1)
        hot = jnp.where(posc[lo : lo + n, 0:1] == ids, wcol[lo : lo + n, 0:1], 0.0)
        hot = hot + jnp.where(posc[lo : lo + n, 1:2] == ids, wcol[lo : lo + n, 1:2], 0.0)
        acc += dot(xt[:, lo : lo + n], hot.astype(BF))
    out[...] = acc.astype(BF)


def group_weight_body(n, sc, xs, *refs):
    pieces, out = refs[:n], refs[n]
    ts = pieces[0].shape[0]
    e = pl.program_id(1)
    lo, hi = sc[n + e], sc[n + e + 1]
    out[...] = jnp.zeros_like(out)
    for i in range(n):
        p0 = sc[i]

        @pl.when((p0 < hi) & (p0 + ts > lo))
        def _():
            ids = p0 + lax.broadcasted_iota(jnp.int32, (1, ts), 1)
            ok = jnp.where((ids >= lo) & (ids < hi), 1.0, 0.0).astype(BF)
            out[0] += dot(xs[:, i * ts : (i + 1) * ts] * ok, pieces[i][...])


def per_device(
    inputs,
    cotangent,
    doc_lengths,
    att_routes,
    ffn_routes,
    kv_weight,
    query_weight,
    output_weight,
    att_router,
    att_gain,
    gate_up_weight,
    down_weight,
    ffn_router,
    ffn_gain,
):
    n_ctx = lax.axis_size("ctx")
    n_z = lax.axis_size("fsdp")
    c = lax.axis_index("ctx")
    f = lax.axis_index("fsdp")
    n_chip = n_ctx // 2
    chip, core = c // 2, c % 2
    tok = inputs.shape[1]
    seq = tok * n_ctx
    dc = D // n_ctx
    rows = n_z * seq
    hc = HEADS // n_z // 2
    width = hc * HD
    half = seq // 2
    fl_real = FF // n_z
    fl = -(-fl_real // 128) * 128
    ts = 2 * rows // n_ctx // 2
    assert n_chip == n_z

    def swap(x, axis, k, n):
        return lax.ppermute(x, axis, [(i, i ^ k) for i in range(n)])

    def core_swap(x):
        return swap(x, "ctx", 1, n_ctx)

    def chip_swap(x, k):
        return swap(x, "ctx", 2 * k, n_ctx)

    def z_swap(x, k):
        return swap(x, "fsdp", k, n_z)

    chip_bits = [1 << i for i in range(n_chip.bit_length() - 1)]
    z_bits = [1 << i for i in range(n_z.bit_length() - 1)]

    def z_gather(x):
        return [x] + [z_swap(x, k) for k in range(1, n_z)]

    def z_reduce(pieces):
        total = pieces[0].astype(F32)
        for k in range(1, n_z):
            total = total + z_swap(pieces[k], k).astype(F32)
        return total

    def small_sum(x, over_ctx, over_z):
        if over_ctx:
            for k in [1] + [2 * b for b in chip_bits]:
                x = x + swap(x, "ctx", k, n_ctx)
        if over_z:
            for k in z_bits:
                x = x + z_swap(x, k)
        return x

    def chip_reduce(pieces):
        result = []
        for h, order in ((0, chip_bits), (1, chip_bits[::-1])):
            cur = dict(pieces[h])
            for step, b in enumerate(order):
                keep = {k: v for k, v in cur.items() if not k & b}
                for k, v in cur.items():
                    if k & b:
                        got = chip_swap(v, b)
                        if step == len(order) - 1:
                            return_pair = (keep[k ^ b], got)
                        else:
                            keep[k ^ b] = (keep[k ^ b].astype(F32) + got.astype(F32)).astype(BF)
                cur = keep
            result.extend(return_pair)
        return result

    def chip_gather(halves):
        result = {k: [None, None] for k in range(n_chip)}
        for h, order in ((0, chip_bits), (1, chip_bits[::-1])):
            cur = {0: halves[h]}
            for b in order:
                for k, v in list(cur.items()):
                    cur[k ^ b] = chip_swap(v, b)
            for k, v in cur.items():
                result[k][h] = v
        return result

    def rel(x):
        return jnp.take(x, f ^ jnp.arange(n_z, dtype=jnp.int32), axis=0)

    x_loc = inputs[0].astype(F32)
    ends = jnp.cumsum(doc_lengths, axis=1)
    starts = ends - doc_lengths
    positions = jnp.arange(seq, dtype=jnp.int32)
    doc_abs = jnp.sum((positions[None, :, None] >= ends[:, None, :]).astype(jnp.int32), axis=2)
    labels = jnp.arange(DOCS, dtype=jnp.int32)
    begin = jnp.sum(jnp.where(doc_abs[:, :, None] == labels, starts[:, None, :], 0), axis=2)
    place_abs = positions[None, :] - begin
    my_pos = c * tok + jnp.arange(tok, dtype=jnp.int32)
    my_ends = lax.dynamic_slice_in_dim(ends, f, 1, 0)
    my_keep = (my_pos < my_ends[0, DOCS - 1]).astype(F32)[:, None]
    inv1_loc = lax.rsqrt(jnp.mean(x_loc * x_loc, axis=1, keepdims=True) + norm_eps)
    n1_loc = x_loc * inv1_loc
    dy_loc = cotangent[0].astype(F32) * my_keep
    payload = jnp.stack((n1_loc.astype(BF), dy_loc.astype(BF), inputs[0]), axis=1)
    payload = payload.reshape(tok, 3, n_ctx, dc).transpose(2, 0, 1, 3).reshape(n_ctx, tok, 3 * dc)
    payload = lax.all_to_all(payload, "ctx", 0, 0, tiled=True).reshape(seq, 3 * dc)
    x_col = payload[:, 2 * dc :].astype(F32)
    nd = z_gather(payload[:, : 2 * dc])
    nd_t = [core_swap(v) for v in nd]
    nd_o = jnp.concatenate(nd, axis=0)
    nd_t = jnp.concatenate(nd_t, axis=0)

    small = jnp.concatenate((att_gain[None], ffn_gain[None]), axis=0).astype(BF)
    small_t = core_swap(small)
    ga, gf = small[0:1].astype(F32), small[1:2].astype(F32)
    ga_t, gf_t = small_t[0:1].astype(F32), small_t[1:2].astype(F32)
    ra, rf = att_router.astype(BF), ffn_router.astype(BF)

    routes = jnp.concatenate((att_routes, ffn_routes), axis=2)
    routes = lax.all_gather(routes, "ctx", axis=0, tiled=True)
    routes = rel(jnp.transpose(routes, (1, 0, 2))).reshape(rows, 4)
    route_row = jnp.transpose(routes)
    att_route3 = routes[:, :2].reshape(n_z, seq, 2)
    experts = jnp.arange(E_F, dtype=jnp.int32)
    hot = (route_row[2:4, None, :] == experts[None, :, None]).astype(F32)
    blocks = rows // 128
    hot_b = hot.reshape(2 * E_F, blocks, 128)
    lane = jnp.arange(128)
    tri = (lane[:, None] < lane[None, :]).astype(BF)
    before = jnp.einsum("anl,lm->anm", hot_b.astype(BF), tri, preferred_element_type=F32)
    totals = jnp.sum(hot_b, axis=2)
    lane_b = jnp.arange(blocks)
    tri_b = (lane_b[:, None] < lane_b[None, :]).astype(BF)
    before_b = jnp.dot(totals.astype(BF), tri_b, preferred_element_type=F32)
    rank = (before + before_b[:, :, None]).reshape(2, E_F, rows)
    counts = jnp.sum(totals, axis=1).reshape(2, E_F)
    per_expert = counts[0] + counts[1]
    off = jnp.sum(jnp.where(experts[:, None] > experts[None, :], per_expert[None, :], 0.0), axis=1)
    base = jnp.stack((off, off + counts[0]))
    pos_row = jnp.sum(hot * (base[:, :, None] + rank), axis=1).astype(jnp.int32)
    pos_col = jnp.transpose(pos_row)
    offsets = jnp.concatenate((off, jnp.sum(per_expert)[None])).astype(jnp.int32)

    def tile_scalars(p0):
        first = jnp.sum((offsets[1:] <= p0).astype(jnp.int32))
        last = jnp.sum((offsets[1:] <= p0 + ts - 1).astype(jnp.int32))
        return jnp.concatenate((jnp.stack((p0, first, last)), offsets))

    def start_of(k, other, h):
        return 2 * ts * (2 * (chip ^ k) + (core ^ other)) + h * ts

    def split_halves(w):
        mine = lax.dynamic_slice_in_dim(w, core * width, width, 2)
        theirs = lax.dynamic_slice_in_dim(w, (1 - core) * width, width, 2)
        return mine, theirs, core_swap(theirs)

    def e_major(w):
        return jnp.transpose(w.astype(BF), (1, 0, 2))

    wq_m, wq_t, wq_x = split_halves(e_major(query_weight))
    wk_m, wk_t, wk_x = split_halves(e_major(kv_weight))
    wo_m, wo_t, wo_x = split_halves(e_major(output_weight))

    def pad_lanes(w):
        return w if fl == fl_real else jnp.pad(w, [(0, 0)] * (w.ndim - 1) + [(0, fl - fl_real)])

    wd = pad_lanes(e_major(down_weight))
    wd_x = core_swap(wd)
    wg = pad_lanes(jnp.transpose(gate_up_weight.astype(BF), (1, 0, 2, 3))).reshape(E_F, dc, 2 * fl)
    wg_x = core_swap(wg)

    h1 = (nd_o[:, :dc].astype(F32) * ga).astype(BF)
    h1_x = (nd_t[:, :dc].astype(F32) * ga_t).astype(BF)
    dy = nd_o[:, dc:]
    dy_x = nd_t[:, dc:]

    la = lax.dot_general(ra, h1, (((0,), (1,)), ((), ())), preferred_element_type=F32)
    la = small_sum(la, True, False)

    def gates_of(logits, route2):
        picked = jnp.sum(jnp.where(route2[:, None, :] == experts[None, :, None], logits[None], 0.0), axis=1)
        return jax.nn.softmax(picked, axis=0)

    pa = gates_of(la, route_row[0:2])
    pa3 = jnp.transpose(pa).reshape(n_z, seq, 2)

    def project(xo, xt, weights, k, h):
        n_extra = 2 if len(weights) == 4 else 0
        cols = (2 + n_extra) * width
        at = lambda i, sc: (sc[0], 0)
        return call(
            functools.partial(proj_body, n_extra, width),
            jnp.reshape(2 * (chip ^ k) + h, (1,)),
            (1,),
            [spec((half, 4), at), spec((half, dc), at), spec((half, dc), at)] + [spec(w.shape) for w in weights],
            spec((half, cols)),
            jax.ShapeDtypeStruct((half, cols), BF),
            flops=2 * half * 2 * dc * (E_A + n_extra) * width,
            size=2 * (half * cols + 2 * half * dc + 2 * dc * (E_A + n_extra) * width),
        )(routes, xo, xt, *weights)

    def project_all(xo, xt, weights):
        return [{k: project(xo, xt, weights, k, h) for k in range(n_chip)[::-1]} for h in range(2)]

    qkv_parts = chip_reduce(project_all(h1, h1_x, (wq_m, wq_x, wk_m, wk_x)))

    s_abs = f ^ chip
    doc_one = lax.dynamic_index_in_dim(doc_abs, s_abs, 0, keepdims=False)
    place_one = lax.dynamic_index_in_dim(place_abs, s_abs, 0, keepdims=False)
    doc_col, doc_row = doc_one[:, None], doc_one[None, :]
    halves = jnp.arange(HD // 2, dtype=F32)
    angles = place_one.astype(F32)[:, None] * (rope_base ** (-2.0 * halves / HD))[None, :]
    cos, sin = jnp.cos(angles), jnp.sin(angles)
    cosf = jnp.concatenate((cos, cos), axis=1)
    sinf = jnp.concatenate((-sin, sin), axis=1)

    one = jnp.zeros((1,), jnp.int32)
    att_flops = 2 * hc * 2 * 2 * seq * seq * HD
    qkv, ao, lse = call(
        functools.partial(attend_body, hc),
        one,
        (1,),
        [spec((half, 4 * width))] * 4 + [spec((seq, 1)), spec((1, seq)), spec((seq, HD)), spec((seq, HD))],
        [spec((seq, 4 * width)), spec((seq, 2 * width)), spec((seq, 128))],
        [
            jax.ShapeDtypeStruct((seq, 4 * width), BF),
            jax.ShapeDtypeStruct((seq, 2 * width), BF),
            jax.ShapeDtypeStruct((seq, 128), F32),
        ],
        flops=att_flops,
        size=seq * width * 20,
    )(*qkv_parts, doc_col, doc_row, cosf, sinf)

    ao_m = [ao] + [chip_swap(ao, k) for k in range(1, n_chip)]
    ao_t = [core_swap(v) for v in ao_m]

    def into_stream(body, k, streams, vals, weights, buf, flops, cols):
        sc = jnp.reshape(chip ^ k, (1,))
        by_stream = [spec((pl.squeezed, seq, 2), lambda i, sc: (sc[0], 0, 0))] * len(streams)
        n_in = len(streams) + 2 + len(weights)
        return call(
            body,
            sc,
            (1,),
            by_stream
            + [spec((seq, cols))] * 2
            + [spec(w.shape) for w in weights]
            + [pl.BlockSpec(memory_space=pl.ANY)],
            spec((1, seq, dc), lambda i, sc: (sc[0], 0, 0)),
            jax.ShapeDtypeStruct((n_z, seq, dc), BF),
            aliases={n_in + 1: 0},
            flops=flops,
            size=2 * (2 * seq * cols + 2 * E_A * dc * width + seq * dc),
        )(*streams, *vals, *weights, buf)

    buf = jnp.zeros((n_z, seq, dc), BF)
    for k in range(n_chip):
        buf = into_stream(
            functools.partial(att_out_body, width),
            k,
            (att_route3, pa3),
            (ao_m[k], ao_t[k]),
            (wo_m, wo_t),
            buf,
            4 * seq * E_A * width * dc,
            2 * width,
        )
    y1 = x_col + z_reduce([buf[k] for k in range(n_z)])

    y1_low = jnp.concatenate(z_gather(y1.astype(BF)), axis=0)
    y1_all = y1_low.astype(F32)
    yg = (y1_all * gf).astype(BF)
    yg_x = (core_swap(y1_low).astype(F32) * gf_t).astype(BF)
    stat = jnp.concatenate(
        (
            lax.dot_general(rf, yg, (((0,), (1,)), ((), ())), preferred_element_type=F32),
            jnp.sum(y1_all * y1_all, axis=1)[None],
            jnp.zeros((7, rows), F32),
        ),
        axis=0,
    )
    stat = small_sum(stat, True, False)
    inv2 = lax.rsqrt(stat[8:9] / D + norm_eps)
    lf = stat[0:E_F] * inv2
    pf = gates_of(lf, route_row[2:4])
    rowv = jnp.concatenate((inv2, pf, jnp.zeros((5, rows), F32)), axis=0)
    pf_col = jnp.transpose(pf)
    ones_col = jnp.ones((rows, 2), F32)
    inv2_col = jnp.transpose(inv2)

    def group_proj(xo, xt, wm, wx, k, h):
        n = wm.shape[2]
        by_expert = spec((1, dc, n), lambda i, sc: (jnp.minimum(sc[1] + i, sc[2]), 0, 0))
        return call(
            group_proj_body,
            tile_scalars(start_of(k, 0, h)),
            (E_F,),
            [spec((2, rows)), spec((rows, dc)), spec((rows, dc)), by_expert, by_expert],
            spec((ts, n)),
            jax.ShapeDtypeStruct((ts, n), BF),
            [pltpu.VMEM((ts, 2 * dc), BF)],
            flops=2 * ts * 2 * dc * (rows + 2 * n),
            size=2 * (2 * rows * dc + 4 * dc * n + ts * n),
        )(pos_row, xo, xt, wm, wx)

    def group_all(xo, xt, wm, wx):
        return [{k: group_proj(xo, xt, wm, wx, k, h) for k in range(n_chip)[::-1]} for h in range(2)]

    da_parts = chip_reduce(group_all(dy, dy_x, wd, wd_x))
    gu_parts = chip_reduce(group_all(yg, yg_x, wg, wg_x))

    dgu_own, act_own, tok_sum = [], [], 0.0
    for h in range(2):
        a, b, t = call(
            functools.partial(middle_body, fl),
            tile_scalars(start_of(0, 0, h)),
            (1,),
            [spec((2, rows)), spec((8, rows))] + [spec((ts, 2 * fl))] * 2 + [spec((ts, fl))] * 2,
            [spec((ts, 2 * fl)), spec((ts, fl)), spec((8, rows))],
            [
                jax.ShapeDtypeStruct((ts, 2 * fl), BF),
                jax.ShapeDtypeStruct((ts, fl), BF),
                jax.ShapeDtypeStruct((8, rows), F32),
            ],
            flops=ts * fl * 30,
            size=ts * fl * 18,
        )(pos_row, rowv, gu_parts[2 * h], gu_parts[2 * h + 1], da_parts[2 * h], da_parts[2 * h + 1])
        dgu_own.append(a)
        act_own.append(b)
        tok_sum = tok_sum + t

    tok_sum = rel(tok_sum.reshape(8, n_z, seq).transpose(1, 0, 2))
    tok_sum = rel(small_sum(tok_sum, True, True)).transpose(1, 0, 2).reshape(8, rows)

    def router_back(dgate, gates, route2):
        dlog = gates * (dgate - jnp.sum(gates * dgate, axis=0, keepdims=True))
        return jnp.sum(jnp.where(route2[:, None, :] == experts[None, :, None], dlog[:, None, :], 0.0), axis=0)

    dlf = router_back(tok_sum[0:2], pf, route_row[2:4])
    m2 = (tok_sum[2:3] + jnp.sum(dlf * lf, axis=0, keepdims=True)) / D
    dlf_low = dlf.astype(BF)

    def gather_pieces(own):
        got = chip_gather(own)
        out = []
        for k in range(n_chip):
            for h in range(2):
                out.append((k, 0, h, got[k][h]))
        for k in range(n_chip):
            for h in range(2):
                out.append((k, 1, h, core_swap(got[k][h])))
        return out

    dgu_pieces = gather_pieces(dgu_own)
    act_pieces = gather_pieces(act_own)

    def group_back(piece, wcol, w, prev):
        k, other, h, vals = piece
        n = w.shape[2]
        return call(
            group_back_body,
            tile_scalars(start_of(k, other, h)),
            (E_F,),
            [
                spec((rows, 2)),
                spec((rows, 2)),
                spec((ts, n)),
                spec((1, dc, n), lambda i, sc: (jnp.minimum(sc[1] + i, sc[2]), 0, 0)),
                spec((rows, dc)),
            ],
            spec((rows, dc)),
            jax.ShapeDtypeStruct((rows, dc), F32),
            [pltpu.VMEM((ts, dc), F32)],
            aliases={5: 0},
            flops=2 * ts * dc * (rows + 2 * n),
            size=2 * (ts * n + 2 * dc * n) + 8 * rows * dc,
        )(pos_col, wcol, vals, w, prev)

    dh2 = jnp.zeros((rows, dc), F32)
    for piece in dgu_pieces:
        dh2 = group_back(piece, ones_col, wg, dh2)
    dh2_own = z_reduce([dh2[k * seq : (k + 1) * seq].astype(BF) for k in range(n_z)])
    dh2_all = jnp.concatenate(z_gather(dh2_own.astype(BF)), axis=0).astype(F32)
    dh2_all = dh2_all + lax.dot_general(dlf_low, rf, (((0,), (1,)), ((), ())), preferred_element_type=F32)
    n2 = y1_all * inv2_col
    dy1 = dy.astype(F32) + inv2_col * (dh2_all * gf - n2 * jnp.transpose(m2))
    dy1_low = dy1.astype(BF)
    dy1_x = core_swap(dy1_low)

    dao_parts = chip_reduce(project_all(dy1_low, dy1_x, (wo_m, wo_x)))
    pa_one = lax.dynamic_index_in_dim(pa3, chip, 0, keepdims=False)
    grads, dgate = call(
        functools.partial(attend_back_body, hc),
        one,
        (1,),
        [spec((half, 2 * width))] * 4
        + [spec((seq, 4 * width)), spec((seq, 2 * width)), spec((seq, 128)), spec((seq, 2))]
        + [spec((seq, 1)), spec((1, seq)), spec((seq, HD)), spec((seq, HD))],
        [spec((seq, 4 * width)), spec((seq, 128))],
        [jax.ShapeDtypeStruct((seq, 4 * width), BF), jax.ShapeDtypeStruct((seq, 128), F32)],
        flops=att_flops * 5 // 2,
        size=seq * width * 30,
    )(*dao_parts, qkv, ao, lse, pa_one, doc_col, doc_row, cosf, sinf)
    g_m = [grads] + [chip_swap(grads, k) for k in range(1, n_chip)]
    g_t = [core_swap(v) for v in g_m]

    dpa = jnp.zeros((n_z, 8, seq), F32)
    dpa = lax.dynamic_update_slice(dpa, jnp.transpose(dgate[:, :8])[None], (s_abs, 0, 0))
    dpa = small_sum(dpa, True, True)
    dpa = lax.dynamic_index_in_dim(dpa, f, 0, keepdims=False)[0:2]

    buf = jnp.zeros((n_z, seq, dc), BF)
    for k in range(n_chip):
        buf = into_stream(
            functools.partial(att_in_back_body, width),
            k,
            (att_route3,),
            (g_m[k], g_t[k]),
            (wq_m, wq_t, wk_m, wk_t),
            buf,
            4 * seq * (E_A + 2) * width * dc,
            4 * width,
        )
    dh1 = z_reduce([buf[k] for k in range(n_z)])
    dla = router_back(dpa, pa[:, :seq], route_row[0:2, :seq]).astype(BF)
    dh1 = dh1 + lax.dot_general(dla, ra, (((0,), (1,)), ((), ())), preferred_element_type=F32)
    back = jnp.concatenate(((dh1 * ga).astype(BF), dy1_low[:seq]), axis=1)

    def to_rows(v):
        n = v.shape[1] // dc
        v = lax.all_to_all(v.reshape(n_ctx, tok, n * dc), "ctx", 0, 0, tiled=True)
        v = v.reshape(n_ctx, tok, n, dc).transpose(2, 1, 0, 3)
        return v.reshape(n, tok, D)

    back = to_rows(back).astype(F32)
    input_grad = back[1] + inv1_loc * (back[0] - n1_loc * jnp.mean(back[0] * n1_loc, axis=1, keepdims=True))
    input_grad = input_grad.astype(BF)[None]

    ffn = jnp.zeros((rows, dc), F32)
    for piece in act_pieces:
        ffn = group_back(piece, pf_col, wd, ffn)
    ffn = z_reduce([ffn[k * seq : (k + 1) * seq].astype(BF) for k in range(n_z)])
    outputs = to_rows((y1 + ffn).astype(BF))

    n_pieces = len(dgu_pieces)
    starts_all = jnp.stack([start_of(k, other, h) for k, other, h, _ in dgu_pieces])

    def sort_t(xt, wcol):
        return call(
            sort_t_body,
            starts_all,
            (n_pieces,),
            [spec((rows, 2)), spec((rows, 2)), spec((dc, rows))],
            spec((dc, ts), lambda i, sc: (0, i)),
            jax.ShapeDtypeStruct((dc, 2 * rows), BF),
            flops=4 * dc * rows * rows,
            size=6 * dc * rows,
        )(pos_col, wcol, xt)

    def group_weight(xs, pieces):
        n = pieces[0][3].shape[1]
        return call(
            functools.partial(group_weight_body, n_pieces),
            jnp.concatenate((starts_all, offsets)),
            (n // fl, E_F),
            [spec((dc, 2 * rows))] + [spec((ts, fl), lambda j, e, sc: (0, j))] * n_pieces,
            spec((1, dc, fl), lambda j, e, sc: (e, 0, j)),
            jax.ShapeDtypeStruct((E_F, dc, n), F32),
            flops=8 * dc * rows * n,
            size=4 * E_F * dc * n + 4 * rows * n,
        )(xs, *[p[3] for p in pieces])

    h2 = (n2 * gf).astype(BF)
    h2_s = sort_t(jnp.transpose(h2), ones_col)
    dfe_s = sort_t(jnp.transpose(dy), pf_col)
    gate_up_grad = group_weight(h2_s, dgu_pieces).reshape(E_F, dc, 2, fl)[..., :fl_real]
    gate_up_grad = jnp.transpose(gate_up_grad, (1, 0, 2, 3))
    down_grad = jnp.transpose(group_weight(dfe_s, act_pieces)[..., :fl_real], (1, 0, 2))

    def att_weight(xt, gated, extra, mine, theirs, cols):
        pieces = [v for pair in zip(mine, theirs) for v in pair]
        sc = jnp.concatenate((chip ^ jnp.arange(n_chip, dtype=jnp.int32), core[None]))
        outs = [(E_A, lambda i, e, sc: (e, 0, sc[n_chip] ^ i))]
        if extra:
            outs.append((2, lambda i, e, sc: (jnp.minimum(e, 1), 0, sc[n_chip] ^ i)))
        return call(
            functools.partial(att_weight_body, width, n_chip, gated, extra),
            sc,
            (2, E_A),
            [spec(xt.shape), spec((n_z, seq, 2)), spec((n_z, seq, 2))] + [spec((seq, cols))] * len(pieces),
            [spec((1, dc, width), at) for _, at in outs],
            [jax.ShapeDtypeStruct((n, dc, 2 * width), F32) for n, _ in outs],
            flops=4 * rows * dc * (E_A + 2) * width,
            size=8 * E_A * dc * width + 4 * rows * cols,
        )(xt, att_route3, pa3, *pieces)

    def stream_t(v):
        return jnp.transpose(v.reshape(n_z, seq, dc), (0, 2, 1))

    (output_grad,) = att_weight(stream_t(dy1_low), True, False, ao_m, ao_t, 2 * width)
    query_grad, kv_grad = att_weight(stream_t(h1), False, True, g_m, g_t, 4 * width)
    output_grad = jnp.transpose(output_grad, (1, 0, 2))
    query_grad = jnp.transpose(query_grad, (1, 0, 2))
    kv_grad = jnp.transpose(kv_grad, (1, 0, 2))

    own = slice(0, seq)
    tail = jnp.concatenate(
        (
            jnp.dot(dla, h1[own], preferred_element_type=F32),
            jnp.dot(dlf_low[:, own], h2[own], preferred_element_type=F32),
            jnp.sum(dh1 * nd_o[own, :dc].astype(F32), axis=0, keepdims=True),
            jnp.sum(dh2_all[own] * n2[own], axis=0, keepdims=True),
            jnp.zeros((6, dc), F32),
        ),
        axis=0,
    )
    tail = small_sum(tail, False, True)
    att_router_grad = jnp.transpose(tail[0:E_A])
    ffn_router_grad = jnp.transpose(tail[E_A : E_A + E_F])
    att_gain_grad = tail[E_A + E_F]
    ffn_gain_grad = tail[E_A + E_F + 1]

    return (
        outputs,
        input_grad,
        kv_grad,
        query_grad,
        output_grad,
        att_router_grad,
        att_gain_grad,
        gate_up_grad,
        down_grad,
        ffn_router_grad,
        ffn_gain_grad,
    )


def solution(mesh):
    in_specs = (
        P("fsdp", "ctx", None),
        P("fsdp", "ctx", None),
        P(),
        P("ctx", None, None),
        P("ctx", None, None),
        P("ctx", None, "fsdp"),
        P("ctx", None, "fsdp"),
        P("ctx", None, "fsdp"),
        P("ctx", None),
        P("ctx"),
        P("ctx", None, None, "fsdp"),
        P("ctx", None, "fsdp"),
        P("ctx", None),
        P("ctx"),
    )
    out_specs = (
        P("fsdp", "ctx", None),
        P("fsdp", "ctx", None),
        P("ctx", None, "fsdp"),
        P("ctx", None, "fsdp"),
        P("ctx", None, "fsdp"),
        P("ctx", None),
        P("ctx"),
        P("ctx", None, None, "fsdp"),
        P("ctx", None, "fsdp"),
        P("ctx", None),
        P("ctx"),
    )
    return jax.shard_map(
        per_device, mesh=mesh, in_specs=in_specs, out_specs=out_specs, check_vma=False
    )
```

time: 2680 us -> 1360 us (0.51)
  waiting for transfers between devices: 1610 us -> 253 us
  Pallas kernels: 0 us -> 600 us
  matrix products: 279 us -> 9.61 us
  local copies, waits for them, and re-layouts: 482 us -> 232 us
  starting transfers between devices: 0.78 us -> 121 us
  other arithmetic: 201 us -> 105 us
  blocking collectives: 71.9 us -> 13 us
    reduce_scatter x6 -> x0, waiting for transfers between devices: 801 us -> none  [the longest x1 761 us: per_device(): lax.psum_scatter(jnp.concatenate((gate_up_piece, down_piece), axis=2).ast...]
    all_gather x9 -> x0, waiting for transfers between devices: 745 us -> none  [the longest x1 376 us: per_device(): lax.all_gather(gate_up_weight.astype(jnp.bfloat16), 'ctx', axis=0, tiled=...]
    pallas_call x0 -> x82, Pallas kernels: none -> 600 us  [the longest x32 235 us: group_back(): call(group_back_body, tile_scalars(start_of(k, other, h)), (E_F,), [spec(...]
    dot_general x27 -> x8, matrix products: 279 us -> 9.61 us  [the longest x1 5.07 us: per_device(): lax.dot_general(dlf_low, rf, (((0,), (1,)), ((), ())), preferred_element_...]
    ppermute x0 -> x117, waiting for transfers between devices: none -> 253 us  [swap(): return lax.ppermute(x, axis, [(i, i ^ k) for i in range(n)])]
    ppermute x0 -> x117, starting transfers between devices: none -> 108 us  [swap(): return lax.ppermute(x, axis, [(i, i ^ k) for i in range(n)])]
    reshape x12 -> x9, local copies, waits for them, and re-layouts: 172 us -> 86.2 us  [the longest x2 43.6 us: per_device(): group_weight(h2_s, dgu_pieces).reshape(E_F, dc, 2, fl)[..., :fl_real]]
    scatter x6 -> x0, local copies, waits for them, and re-layouts: 79.8 us -> none  [the longest x2 44.2 us: expert_table(): slot_table.at[flat_routes, slot_of]]
  transfers between devices with their start and end apart: 19 -> 120, of which waited for: 10 -> 30; matrix products, arithmetic and copies ran while one was open for 27% -> 24% of each run, Pallas kernels for 0% -> 44%
where the time goes in v1:
time: 1360 us; the launch traced here: 1340 us
  Pallas kernels  600 us (44%)
  waiting for transfers between devices  253 us (19%)
  local copies, waits for them, and re-layouts  232 us (17%)
  starting transfers between devices  121 us (9%)
  other arithmetic  105 us (8%)
    ppermute x117, waiting for transfers between devices, swap(): return lax.ppermute(x, axis, [(i, i ^ k) for i in range(n)])  253 us
    pallas_call x32, Pallas kernels, group_back(): call(group_back_body, tile_scalars(start_of(k, other, h)), (E_F,), [spec(...  235 us
    ppermute x117, starting transfers between devices, swap(): return lax.ppermute(x, axis, [(i, i ^ k) for i in range(n)])  108 us
    pallas_call x16, Pallas kernels, group_proj(): call(group_proj_body, tile_scalars(start_of(k, 0, h)), (E_F,), [spec((2,...  99.3 us
    unnamed x225, local copies, waits for them, and re-layouts  72.8 us
    pallas_call x16, Pallas kernels, project(): call(functools.partial(proj_body, n_extra, width), jnp.reshape(2 * (chip...  53.7 us
    pallas_call x2, Pallas kernels, sort_t(): call(sort_t_body, starts_all, (n_pieces,), [spec((rows, 2)), spec((rows,...  51.9 us
    pallas_call x2, Pallas kernels, group_weight(): call(functools.partial(group_weight_body, n_pieces), jnp.concatenate((sta...  49.9 us
  transfers between devices with their start and end apart: 120, of which 30 were waited for; matrix products, arithmetic and copies ran while one was open for 24% of the time, Pallas kernels for 44%

profile of v1, /device:TPU:0, one launch (start us, length us, event | category | flops | bytes accessed | tf_op | source)
XLA Modules:
  0.0 1337.2 jit_solution(4557802815899492313)
XLA Ops:
  24.1 13.0 all_gather.3
  49.6 12.9 convert_bitcast_fusion
  83.8 25.2 %reshape.431 = bf16[8,256,2816]{2,0,1:T(8,128)(2,1)} reshape(bf16[8,256,2,1408]{3,2,0,1:T(2,128)(2,1)} %convert_bitcast_fusion) | data formatting | bytes 23068672 | tf_op jit(solution)/shard_map/reshape | solution.py:532
  109.0 11.3 copy.1110.wm.w
  120.3 8.5 copy.1147
  183.3 8.9 collective-permute-done.16
  193.2 9.1 collective-permute-done.15.a1
  222.0 14.7 %collective-permute-done.4 = f32[8,2048]{1,0:T(8,128)S(1)} collective-permute-done((f32[8,2048]{1,0:T(8,128)S(1)}, f32[8,2048]{1,0:T(8,128)S(1)}, u32[]{:S(2)}, u32[]{:S(2)}) %collective-permute-start.4) | collective-permute-done | bytes 65568 | tf_op jit(solution)/shard_map/ppermute | solution.py:390
  277.1 15.0 %collective-permute-done.27 = bf16[512,256]{0,1:T(8,128)(2,1)S(1)} collective-permute-done((bf16[512,256]{0,1:T(8,128)(2,1)}, bf16[512,256]{0,1:T(8,128)(2,1)S(1)}, u32[]{:S(2)}, u32[]{:S(2)}) %collective-permute-start.27) | collective-permute-done | bytes 262176 | tf_op jit(solution)/shard_map/ppermute | solution.py:390
  303.5 12.6 collective-permute-done.30
  490.6 17.4 %collective-permute-done.47 = bf16[256,2816]{1,0:T(8,128)(2,1)S(1)} collective-permute-done((bf16[256,2816]{1,0:T(8,128)(2,1)}, bf16[256,2816]{1,0:T(8,128)(2,1)S(1)}, u32[]{:S(2)}, u32[]{:S(2)}) %collective-permute-start.47) | collective-permute-done | bytes 1441824 | tf_op jit(solution)/shard_map/ppermute | solution.py:390
  509.5 21.6 %collective-permute-done.39.g1 = bf16[256,2816]{1,0:T(8,128)(2,1)} collective-permute-done((bf16[256,2816]{1,0:T(8,128)(2,1)S(1)}, bf16[256,2816]{1,0:T(8,128)(2,1)}, u32[]{:S(2)}, u32[]{:S(2)}) %collective-permute-start.39) | collective-permute-done | bytes 1441824 | tf_op jit(solution)/shard_map/ppermute | solution.py:390
  550.9 8.1 collective-permute-done.88
  590.6 9.6 collective-permute-done.45.d.refs_7_
  606.3 52.2 %collective-permute-done.54.d.refs_6_ = bf16[256,1408]{1,0:T(8,128)(2,1)} collective-permute-done((bf16[256,1408]{1,0:T(8,128)(2,1)}, bf16[256,1408]{1,0:T(8,128)(2,1)}, u32[]{:S(2)}, u32[]{:S(2)}) %collective-permute-start.54) | collective-permute-done | bytes 720928 | tf_op jit(solution)/shard_map/ppermute | solution.py:390
  690.9 8.0 shard_map.269.prev
  772.6 8.1 shard_map.270.prev
  780.7 7.9 shard_map.271.prev
  788.6 7.9 shard_map.272.prev
  851.2 8.3 shard_map.280.prev
  867.5 7.9 shard_map.282.prev
  947.5 16.2 %collective-permute-done.85 = bf16[512,256]{0,1:T(8,128)(2,1)} collective-permute-done((bf16[512,256]{0,1:T(8,128)(2,1)S(1)}, bf16[512,256]{0,1:T(8,128)(2,1)}, u32[]{:S(2)}, u32[]{:S(2)}) %collective-permute-start.85) | collective-permute-done | bytes 262176 | tf_op jit(solution)/shard_map/ppermute | solution.py:390
  968.7 25.9 %shard_map.301.xs = bf16[256,4096]{1,0:T(8,128)(2,1)} custom-call(s32[16]{0:T(128)} %stack.155.sc, s32[2048,2]{1,0:T(8,128)} %bitcast.302, f32[2048,2]{1,0:T(8,128)} %fusion.105.wcol, bf16[256,2048]{1,0:T(8,128)(2,1)} %get-tuple-element.170.xt), custom_call_target="tpu_custom_call" | custom-call | flops 4294967296 | bytes 3145728 | tf_op jit(solution)/shard_map/pallas_call | solution.py:812
  1000.8 17.3 %shard_map.302 = f32[8,256,1408]{2,1,0:T(8,128)} custom-call(s32[25]{0:T(128)} %concatenate.163.sc, bf16[256,4096]{1,0:T(8,128)(2,1)} %shard_map.301.xs, bf16[256,1408]{1,0:T(8,128)(2,1)} %get-tuple-element.27.d.refs_0_, bf16[256,1408]{1,0:T(8,128)(2,1)} %get-tuple-element.26.d.refs_1_, bf16[256,1408]{1,0:T(8,128)(2,1)} %collective-permute-done.53.d.refs_2_, ...), custom_call_target="tpu_custom_call" | custom-call | flops 5905580032 | bytes 23068672 | tf_op jit(solution)/shard_map/pallas_call | solution.py:825
  1018.2 15.4 %copy.1107 = f32[256,8,1408]{2,1,0:T(8,128)} copy(f32[256,8,1408]{2,0,1:T(8,128)} %bitcast.316) | data formatting | bytes 23068672
  1088.1 26.0 %shard_map.299.xs = bf16[256,4096]{1,0:T(8,128)(2,1)} custom-call(s32[16]{0:T(128)} %stack.155.sc, s32[2048,2]{1,0:T(8,128)} %bitcast.303, f32[2048,2]{1,0:T(8,128)} %broadcast_in_dim.193.wcol, bf16[256,2048]{1,0:T(8,128)(2,1)} %bitcast.339), custom_call_target="tpu_custom_call" | custom-call | flops 4294967296 | bytes 3145728 | tf_op jit(solution)/shard_map/pallas_call | solution.py:812
  1122.6 32.6 %shard_map.300 = f32[8,256,2816]{2,1,0:T(8,128)} custom-call(s32[25]{0:T(128)} %concatenate.163.sc, bf16[256,4096]{1,0:T(8,128)(2,1)} %shard_map.299.xs, bf16[256,2816]{1,0:T(8,128)(2,1)} %get-tuple-element.29.d.refs_0_, bf16[256,2816]{1,0:T(8,128)(2,1)} %get-tuple-element.28.d.refs_1_, bf16[256,2816]{1,0:T(8,128)(2,1)} %collective-permute-done.70.d.refs_2_, ...), custom_call_target="tpu_custom_call" | custom-call | flops 11811160064 | bytes 46137344 | tf_op jit(solution)/shard_map/pallas_call | solution.py:825
  1165.2 20.9 %shard_map.298 = f32[8,256,512]{2,1,0:T(8,128)} custom-call(s32[5]{0:T(128)} %pad_add_fusion.1.sc, bf16[4,256,512]{2,1,0:T(8,128)(2,1)} %bitcast.341, s32[4,512,2]{2,1,0:T(8,128)} %bitcast.310, f32[4,512,2]{2,1,0:T(8,128)} %bitcast.323, bf16[512,512]{1,0:T(8,128)(2,1)} %get-tuple-element.25.om.att.refs_3_, bf16[512,512]{1,0:T(8,128)(2,1)} %copy-done.56, ...), custom_call_target="tpu_custom_call" | custom-call | flops 5368709120 | bytes 8388608 | tf_op jit(solution)/shard_map/pallas_call | solution.py:849
  1201.0 27.2 %reshape.392 = f32[8,256,2,1408]{3,2,1,0:T(2,128)} reshape(f32[8,256,2816]{2,1,0:T(8,128)} %shard_map.300) | data formatting | bytes 46137344 | tf_op jit(solution)/shard_map/reshape | solution.py:839
  1228.2 16.3 %copy.1146 = f32[8,256,2,1408]{3,2,0,1:T(2,128)} copy(f32[8,256,2,1408]{3,2,1,0:T(2,128)} %reshape.392) | data formatting | bytes 46137344 | tf_op jit(solution)/shard_map/reshape | solution.py:839
  1278.5 13.3 collective-permute-done.108
  1299.9 22.2 %shard_map.297 = (f32[8,256,512]{2,1,0:T(8,128)}, f32[2,256,512]{2,1,0:T(8,128)}) custom-call(s32[5]{0:T(128)} %pad_add_fusion.1.sc, bf16[4,256,512]{2,1,0:T(8,128)(2,1)} %bitcast.340, s32[4,512,2]{2,1,0:T(8,128)} %bitcast.315, f32[4,512,2]{2,1,0:T(8,128)} %bitcast.324, bf16[512,1024]{1,0:T(8,128)(2,1)} %get-tuple-element.34.gm.refs_3_, ...), custom_call_target="tpu_custom_call" | custom-call | flops 5368709120 | bytes 12582912 | tf_op jit(solution)/shard_map/pallas_call | solution.py:849
  (738 shorter events, 812.7 us)
Async XLA Ops:
  8.3 59.9 %all-to-all-start = ((bf16[8,64,768]{2,1,0:T(8,128)(2,1)}), bf16[8,64,768]{2,1,0:T(8,128)(2,1)S(1)}, u32[]{:S(2)}, u32[]{:S(2)}) async-start(bf16[8,64,768]{2,1,0:T(8,128)(2,1)} %reshape.367), calls=%async_computation | async-start | bytes 1572864 | tf_op jit(solution)/shard_map/all_to_all | solution.py:469
  14.7 114.1 %collective-permute-start.10 = (bf16[2,256]{1,0:T(2,128)(2,1)}, bf16[2,256]{1,0:T(2,128)(2,1)S(1)}, u32[]{:S(2)}, u32[]{:S(2)}) collective-permute-start(bf16[2,256]{1,0:T(2,128)(2,1)} %pad_maximum_fusion.5), channel_id=1, source_target_pairs={{0,4},{4,0},{8,12},{12,8},{16,20},{20,16},{24,28},{28,24},{1,5},{5... | collective-permute-start | bytes 3080 | tf_op jit(solution)/shard_map/ppermute | solution.py:390
  23.7 121.0 %collective-permute-start.11 = (bf16[8,256,256]{2,1,0:T(8,128)(2,1)S(1)}, bf16[8,256,256]{2,1,0:T(8,128)(2,1)S(1)}, u32[]{:S(2)}, u32[]{:S(2)}) collective-permute-start(bf16[8,256,256]{2,1,0:T(8,128)(2,1)S(1)} %get-tuple-element.174.wt), channel_id=1, source_target_pairs={{0,4},{4,0},{8,12},{12,8},{16,20},{20,16},{24,28},{28,24},{1,5},{5... | collective-permute-start | bytes 3145736 | tf_op jit(solution)/shard_map/ppermute | solution.py:390
  69.3 60.7 %collective-permute-start.2 = (bf16[512,512]{0,1:T(8,128)(2,1)}, bf16[512,512]{0,1:T(8,128)(2,1)}, u32[]{:S(2)}, u32[]{:S(2)}) collective-permute-start(bf16[512,512]{0,1:T(8,128)(2,1)} %copy.1113), channel_id=1, source_target_pairs={{0,3},{1,2},{2,1},{3,0},{4,7},{5,6},{6,5},{7,4},{8,11},{9,10},{10,... | collective-permute-start | bytes 1572872 | tf_op jit(solution)/shard_map/ppermute | solution.py:390
  72.9 57.0 %collective-permute-start.1 = (bf16[512,512]{0,1:T(8,128)(2,1)}, bf16[512,512]{0,1:T(8,128)(2,1)}, u32[]{:S(2)}, u32[]{:S(2)}) collective-permute-start(bf16[512,512]{0,1:T(8,128)(2,1)} %copy.1113), channel_id=1, source_target_pairs={{0,2},{1,3},{2,0},{3,1},{4,6},{5,7},{6,4},{7,5},{8,10},{9,11},{10,... | collective-permute-start | bytes 1572872 | tf_op jit(solution)/shard_map/ppermute | solution.py:390
  72.9 56.5 %collective-permute-start = (bf16[512,512]{0,1:T(8,128)(2,1)}, bf16[512,512]{0,1:T(8,128)(2,1)}, u32[]{:S(2)}, u32[]{:S(2)}) collective-permute-start(bf16[512,512]{0,1:T(8,128)(2,1)} %copy.1113), channel_id=1, source_target_pairs={{0,1},{1,0},{2,3},{3,2},{4,5},{5,4},{6,7},{7,6},{8,9},{9,8},{10,11... | collective-permute-start | bytes 1572872 | tf_op jit(solution)/shard_map/ppermute | solution.py:390
  136.2 275.6 %collective-permute-start.36 = (bf16[8,256,2816]{2,1,0:T(8,128)(2,1)}, bf16[8,256,2816]{2,1,0:T(8,128)(2,1)}, u32[]{:S(2)}, u32[]{:S(2)}) collective-permute-start(bf16[8,256,2816]{2,1,0:T(8,128)(2,1)} %copy.1110.wm.w), channel_id=1, source_target_pairs={{0,4},{4,0},{8,12},{12,8},{16,20},{20,16},{24,28},{28,24},{1,5},{5... | collective-permute-start | bytes 34603016 | tf_op jit(solution)/shard_map/ppermute | solution.py:390
  150.4 67.0 %collective-permute-start.3 = (f32[8,2048]{1,0:T(8,128)S(1)}, f32[8,2048]{1,0:T(8,128)S(1)}, u32[]{:S(2)}, u32[]{:S(2)}) collective-permute-start(f32[8,2048]{1,0:T(8,128)S(1)} %convolution_bitcast_fusion.1), channel_id=1, source_target_pairs={{0,4},{4,0},{8,12},{12,8},{16,20},{20,16},{24,28},{28,24},{1,5},{5... | collective-permute-start | bytes 196616 | tf_op jit(solution)/shard_map/ppermute | solution.py:390
  243.8 110.2 %collective-permute-start.40 = (bf16[8,256,1408]{2,1,0:T(8,128)(2,1)}, bf16[8,256,1408]{2,1,0:T(8,128)(2,1)}, u32[]{:S(2)}, u32[]{:S(2)}) collective-permute-start(bf16[8,256,1408]{2,1,0:T(8,128)(2,1)} %bitcast.245), channel_id=1, source_target_pairs={{0,4},{4,0},{8,12},{12,8},{16,20},{20,16},{24,28},{28,24},{1,5},{5... | collective-permute-start | bytes 17301512 | tf_op jit(solution)/shard_map/ppermute | solution.py:390
  405.1 104.4 %collective-permute-start.43 = (bf16[256,1408]{1,0:T(8,128)(2,1)}, bf16[256,1408]{1,0:T(8,128)(2,1)}, u32[]{:S(2)}, u32[]{:S(2)}) collective-permute-start(bf16[256,1408]{1,0:T(8,128)(2,1)} %add_convert_fusion.7), channel_id=1, source_target_pairs={{0,8},{4,12},{8,0},{12,4},{16,24},{20,28},{24,16},{28,20},{1,9},{5... | collective-permute-start | bytes 2162696 | tf_op jit(solution)/shard_map/ppermute | solution.py:390
  408.4 130.4 %collective-permute-start.52 = (bf16[256,1408]{1,0:T(8,128)(2,1)}, bf16[256,1408]{1,0:T(8,128)(2,1)}, u32[]{:S(2)}, u32[]{:S(2)}) collective-permute-start(bf16[256,1408]{1,0:T(8,128)(2,1)} %add_convert_fusion.5), channel_id=1, source_target_pairs={{0,16},{4,20},{8,24},{12,28},{16,0},{20,4},{24,8},{28,12},{1,17},{... | collective-permute-start | bytes 2162696 | tf_op jit(solution)/shard_map/ppermute | solution.py:390
  428.4 57.6 %collective-permute-start.37 = (bf16[256,2816]{1,0:T(8,128)(2,1)}, bf16[256,2816]{1,0:T(8,128)(2,1)}, u32[]{:S(2)}, u32[]{:S(2)}) collective-permute-start(bf16[256,2816]{1,0:T(8,128)(2,1)} %shard_map.235), channel_id=1, source_target_pairs={{0,16},{4,20},{8,24},{12,28},{16,0},{20,4},{24,8},{28,12},{1,17},{... | collective-permute-start | bytes 4325384 | tf_op jit(solution)/shard_map/ppermute | solution.py:390
  579.4 100.8 %collective-permute-start.70 = (bf16[256,2816]{1,0:T(8,128)(2,1)}, bf16[256,2816]{1,0:T(8,128)(2,1)}, u32[]{:S(2)}, u32[]{:S(2)}) collective-permute-start(bf16[256,2816]{1,0:T(8,128)(2,1)} %get-tuple-element.29.d.refs_0_), channel_id=1, source_target_pairs={{0,8},{4,12},{8,0},{12,4},{16,24},{20,28},{24,16},{28,20},{1,9},{5... | collective-permute-start | bytes 4325384 | tf_op jit(solution)/shard_map/ppermute | solution.py:390
  584.7 96.9 %collective-permute-start.74 = (bf16[256,2816]{1,0:T(8,128)(2,1)}, bf16[256,2816]{1,0:T(8,128)(2,1)}, u32[]{:S(2)}, u32[]{:S(2)}) collective-permute-start(bf16[256,2816]{1,0:T(8,128)(2,1)} %get-tuple-element.29.d.refs_0_), channel_id=1, source_target_pairs={{0,16},{4,20},{8,24},{12,28},{16,0},{20,4},{24,8},{28,12},{1,17},{... | collective-permute-start | bytes 4325384 | tf_op jit(solution)/shard_map/ppermute | solution.py:390
  585.6 94.0 %collective-permute-start.67 = (bf16[256,2816]{1,0:T(8,128)(2,1)}, bf16[256,2816]{1,0:T(8,128)(2,1)}, u32[]{:S(2)}, u32[]{:S(2)}) collective-permute-start(bf16[256,2816]{1,0:T(8,128)(2,1)} %get-tuple-element.28.d.refs_1_), channel_id=1, source_target_pairs={{0,16},{4,20},{8,24},{12,28},{16,0},{20,4},{24,8},{28,12},{1,17},{... | collective-permute-start | bytes 4325384 | tf_op jit(solution)/shard_map/ppermute | solution.py:390
  587.6 70.9 %collective-permute-start.54 = (bf16[256,1408]{1,0:T(8,128)(2,1)}, bf16[256,1408]{1,0:T(8,128)(2,1)}, u32[]{:S(2)}, u32[]{:S(2)}) collective-permute-start(bf16[256,1408]{1,0:T(8,128)(2,1)} %collective-permute-done.53.d.refs_2_), channel_id=1, source_target_pairs={{0,16},{4,20},{8,24},{12,28},{16,0},{20,4},{24,8},{28,12},{1,17},{... | collective-permute-start | bytes 2162696 | tf_op jit(solution)/shard_map/ppermute | solution.py:390
  600.2 99.5 %collective-permute-start.76 = (bf16[256,2816]{1,0:T(8,128)(2,1)}, bf16[256,2816]{1,0:T(8,128)(2,1)}, u32[]{:S(2)}, u32[]{:S(2)}) collective-permute-start(bf16[256,2816]{1,0:T(8,128)(2,1)} %get-tuple-element.28.d.refs_1_), channel_id=1, source_target_pairs={{0,8},{4,12},{8,0},{12,4},{16,24},{20,28},{24,16},{28,20},{1,9},{5... | collective-permute-start | bytes 4325384 | tf_op jit(solution)/shard_map/ppermute | solution.py:390
  707.2 112.1 %collective-permute-start.78 = (bf16[256,2816]{1,0:T(8,128)(2,1)}, bf16[256,2816]{1,0:T(8,128)(2,1)S(1)}, u32[]{:S(2)}, u32[]{:S(2)}) collective-permute-start(bf16[256,2816]{1,0:T(8,128)(2,1)} %collective-permute-done.70.d.refs_2_), channel_id=1, source_target_pairs={{0,4},{4,0},{8,12},{12,8},{16,20},{20,16},{24,28},{28,24},{1,5},{5... | collective-permute-start | bytes 4325384 | tf_op jit(solution)/shard_map/ppermute | solution.py:390
  708.7 132.9 %collective-permute-start.75 = (bf16[256,2816]{1,0:T(8,128)(2,1)}, bf16[256,2816]{1,0:T(8,128)(2,1)S(1)}, u32[]{:S(2)}, u32[]{:S(2)}) collective-permute-start(bf16[256,2816]{1,0:T(8,128)(2,1)} %collective-permute-done.74.d.refs_4_), channel_id=1, source_target_pairs={{0,4},{4,0},{8,12},{12,8},{16,20},{20,16},{24,28},{28,24},{1,5},{5... | collective-permute-start | bytes 4325384 | tf_op jit(solution)/shard_map/ppermute | solution.py:390
  714.1 129.2 %collective-permute-start.77 = (bf16[256,2816]{1,0:T(8,128)(2,1)}, bf16[256,2816]{1,0:T(8,128)(2,1)}, u32[]{:S(2)}, u32[]{:S(2)}) collective-permute-start(bf16[256,2816]{1,0:T(8,128)(2,1)} %collective-permute-done.76.d.refs_3_), channel_id=1, source_target_pairs={{0,4},{4,0},{8,12},{12,8},{16,20},{20,16},{24,28},{28,24},{1,5},{5... | collective-permute-start | bytes 4325384 | tf_op jit(solution)/shard_map/ppermute | solution.py:390
  715.6 127.8 %collective-permute-start.69 = (bf16[256,2816]{1,0:T(8,128)(2,1)}, bf16[256,2816]{1,0:T(8,128)(2,1)}, u32[]{:S(2)}, u32[]{:S(2)}) collective-permute-start(bf16[256,2816]{1,0:T(8,128)(2,1)} %collective-permute-done.68.d.refs_7_), channel_id=1, source_target_pairs={{0,4},{4,0},{8,12},{12,8},{16,20},{20,16},{24,28},{28,24},{1,5},{5... | collective-permute-start | bytes 4325384 | tf_op jit(solution)/shard_map/ppermute | solution.py:390
  723.5 136.0 %collective-permute-start.72 = (bf16[256,2816]{1,0:T(8,128)(2,1)}, bf16[256,2816]{1,0:T(8,128)(2,1)}, u32[]{:S(2)}, u32[]{:S(2)}) collective-permute-start(bf16[256,2816]{1,0:T(8,128)(2,1)} %collective-permute-done.71.d.refs_6_), channel_id=1, source_target_pairs={{0,4},{4,0},{8,12},{12,8},{16,20},{20,16},{24,28},{28,24},{1,5},{5... | collective-permute-start | bytes 4325384 | tf_op jit(solution)/shard_map/ppermute | solution.py:390
  819.3 65.2 %collective-permute-start.56 = (bf16[256,1408]{1,0:T(8,128)(2,1)}, bf16[256,1408]{1,0:T(8,128)(2,1)}, u32[]{:S(2)}, u32[]{:S(2)}) collective-permute-start(bf16[256,1408]{1,0:T(8,128)(2,1)} %collective-permute-done.44.d.refs_5_), channel_id=1, source_target_pairs={{0,4},{4,0},{8,12},{12,8},{16,20},{20,16},{24,28},{28,24},{1,5},{5... | collective-permute-start | bytes 2162696 | tf_op jit(solution)/shard_map/ppermute | solution.py:390
  859.5 58.2 %collective-permute-start.55 = (bf16[256,1408]{1,0:T(8,128)(2,1)}, bf16[256,1408]{1,0:T(8,128)(2,1)}, u32[]{:S(2)}, u32[]{:S(2)}) collective-permute-start(bf16[256,1408]{1,0:T(8,128)(2,1)} %collective-permute-done.54.d.refs_6_), channel_id=1, source_target_pairs={{0,4},{4,0},{8,12},{12,8},{16,20},{20,16},{24,28},{28,24},{1,5},{5... | collective-permute-start | bytes 2162696 | tf_op jit(solution)/shard_map/ppermute | solution.py:390
  917.7 120.6 %collective-permute-start.93 = (bf16[8,256,256]{2,1,0:T(8,128)(2,1)S(1)}, bf16[8,256,256]{2,1,0:T(8,128)(2,1)S(1)}, u32[]{:S(2)}, u32[]{:S(2)}) collective-permute-start(bf16[8,256,256]{2,1,0:T(8,128)(2,1)S(1)} %copy-done.4), channel_id=1, source_target_pairs={{0,4},{4,0},{8,12},{12,8},{16,20},{20,16},{24,28},{28,24},{1,5},{5... | collective-permute-start | bytes 3145736 | tf_op jit(solution)/shard_map/ppermute | solution.py:390
  968.7 67.2 %collective-permute-start.92 = (bf16[2048,256]{0,1:T(8,128)(2,1)S(1)}, bf16[2048,256]{0,1:T(8,128)(2,1)}, u32[]{:S(2)}, u32[]{:S(2)}) collective-permute-start(bf16[2048,256]{0,1:T(8,128)(2,1)S(1)} %get-tuple-element.179), channel_id=1, source_target_pairs={{0,4},{4,0},{8,12},{12,8},{16,20},{20,16},{24,28},{28,24},{1,5},{5... | collective-permute-start | bytes 3145736 | tf_op jit(solution)/shard_map/ppermute | solution.py:390
  1114.2 74.1 %collective-permute-start.100 = (bf16[512,1024]{1,0:T(8,128)(2,1)S(1)}, bf16[512,1024]{1,0:T(8,128)(2,1)S(1)}, u32[]{:S(2)}, u32[]{:S(2)}) collective-permute-start(bf16[512,1024]{1,0:T(8,128)(2,1)S(1)} %copy-done.39), channel_id=1, source_target_pairs={{0,24},{4,28},{8,16},{12,20},{16,8},{20,12},{24,0},{28,4},{1,25},{... | collective-permute-start | bytes 3145736 | tf_op jit(solution)/shard_map/ppermute | solution.py:390
  1115.6 72.9 %collective-permute-start.102 = (bf16[512,1024]{1,0:T(8,128)(2,1)S(1)}, bf16[512,1024]{1,0:T(8,128)(2,1)}, u32[]{:S(2)}, u32[]{:S(2)}) collective-permute-start(bf16[512,1024]{1,0:T(8,128)(2,1)S(1)} %copy-done.39), channel_id=1, source_target_pairs={{0,16},{4,20},{8,24},{12,28},{16,0},{20,4},{24,8},{28,12},{1,17},{... | collective-permute-start | bytes 3145736 | tf_op jit(solution)/shard_map/ppermute | solution.py:390
  1156.3 88.3 %collective-permute-start.106 = (bf16[512,1024]{1,0:T(8,128)(2,1)S(1)}, bf16[512,1024]{1,0:T(8,128)(2,1)}, u32[]{:S(2)}, u32[]{:S(2)}) collective-permute-start(bf16[512,1024]{1,0:T(8,128)(2,1)S(1)} %copy-done.39), channel_id=1, source_target_pairs={{0,4},{4,0},{8,12},{12,8},{16,20},{20,16},{24,28},{28,24},{1,5},{5... | collective-permute-start | bytes 3145736 | tf_op jit(solution)/shard_map/ppermute | solution.py:390
  1165.2 85.5 %collective-permute-start.105 = (bf16[512,1024]{1,0:T(8,128)(2,1)}, bf16[512,1024]{1,0:T(8,128)(2,1)}, u32[]{:S(2)}, u32[]{:S(2)}) collective-permute-start(bf16[512,1024]{1,0:T(8,128)(2,1)} %collective-permute-done.104.gm.refs_5_), channel_id=1, source_target_pairs={{0,4},{4,0},{8,12},{12,8},{16,20},{20,16},{24,28},{28,24},{1,5},{5... | collective-permute-start | bytes 3145736 | tf_op jit(solution)/shard_map/ppermute | solution.py:390
  1188.2 72.6 %collective-permute-start.101 = (bf16[512,1024]{1,0:T(8,128)(2,1)S(1)}, bf16[512,1024]{1,0:T(8,128)(2,1)}, u32[]{:S(2)}, u32[]{:S(2)}) collective-permute-start(bf16[512,1024]{1,0:T(8,128)(2,1)S(1)} %collective-permute-done.100.gm.refs_9_), channel_id=1, source_target_pairs={{0,4},{4,0},{8,12},{12,8},{16,20},{20,16},{24,28},{28,24},{1,5},{5... | collective-permute-start | bytes 3145736 | tf_op jit(solution)/shard_map/ppermute | solution.py:390
  1188.5 67.3 %collective-permute-start.103 = (bf16[512,1024]{1,0:T(8,128)(2,1)}, bf16[512,1024]{1,0:T(8,128)(2,1)}, u32[]{:S(2)}, u32[]{:S(2)}) collective-permute-start(bf16[512,1024]{1,0:T(8,128)(2,1)} %collective-permute-done.102.gm.refs_7_), channel_id=1, source_target_pairs={{0,4},{4,0},{8,12},{12,8},{16,20},{20,16},{24,28},{28,24},{1,5},{5... | collective-permute-start | bytes 3145736 | tf_op jit(solution)/shard_map/ppermute | solution.py:390
  (185 other events, 4694.8 us)

commit v2 on v1

v2 whole, which is shorter than its diff:
```python
import functools

import jax
import jax.numpy as jnp
from jax import lax
from jax.experimental import pallas as pl
from jax.experimental.pallas import tpu as pltpu
from jax.sharding import PartitionSpec as P

D = 2048
HEADS = 16
HD = 128
E_A = 8
E_F = 8
FF = 5632
DOCS = 3

norm_eps = 1e-06
rope_base = 10000.0
masked_score = -1e30

BF = jnp.bfloat16
F32 = jnp.float32
VMEM_CAP = 60 * 1024 * 1024
PER_US = 1.1e9


def dot(a, b):
    return lax.dot_general(a, b, (((1,), (0,)), ((), ())), preferred_element_type=F32)


def dot_nt(a, b):
    return lax.dot_general(a, b, (((1,), (1,)), ((), ())), preferred_element_type=F32)


def dot_tn(a, b):
    return lax.dot_general(a, b, (((0,), (0,)), ((), ())), preferred_element_type=F32)


def spec(shape, index=None):
    if index is not None:
        return pl.BlockSpec(shape, index)
    zeros = (0,) * len(shape)
    return pl.BlockSpec(shape, lambda *_: zeros, pipeline_mode=pl.Buffered(1))


def call(chain, body, sc, grid, in_specs, out_specs, out_shape, scratch=(), aliases=None, us=5):
    single = not isinstance(out_shape, (list, tuple))
    out_specs, out_shape = ([out_specs], [out_shape]) if single else (list(out_specs), list(out_shape))
    out_specs = [pl.BlockSpec(v.block_shape, v.index_map) for v in out_specs]
    anywhere = pl.BlockSpec(memory_space=pl.ANY)

    def go(*operands, carry=()):
        waits = [v for v in chain if not any(v is u for u in operands) and not any(v is u for u in carry)]
        n_in, n_extra, n_out, n_carry = len(operands), len(waits) + len(carry), len(out_shape), len(carry)

        def kernel_body(first, *refs):
            outs = refs[n_in + n_extra :]
            body(first, *refs[:n_in], *outs[:n_out], *outs[n_out + n_carry :])

        alias = dict(aliases or {})
        for i in range(n_carry):
            alias[1 + n_in + len(waits) + i] = n_out + i
        out = pl.pallas_call(
            kernel_body,
            out_shape=out_shape + [jax.ShapeDtypeStruct(v.shape, v.dtype) for v in carry],
            grid_spec=pltpu.PrefetchScalarGridSpec(
                num_scalar_prefetch=1,
                grid=grid,
                in_specs=list(in_specs) + [anywhere] * n_extra,
                out_specs=out_specs + [anywhere] * n_carry,
                scratch_shapes=list(scratch),
            ),
            input_output_aliases=alias,
            compiler_params=pltpu.CompilerParams(
                dimension_semantics=("arbitrary",) * len(grid), vmem_limit_bytes=VMEM_CAP
            ),
            cost_estimate=pl.CostEstimate(flops=int(us * PER_US), bytes_accessed=0, transcendentals=0),
        )(sc, *operands, *waits, *carry)
        chain[:] = out[:1]
        result = out[0] if single else out[:n_out]
        return (result, *out[n_out:]) if carry else result

    return go


def proj_body(n_extra, width, n, sc, route, xo, xt, *refs):
    wm, wt = refs[0], refs[1]
    outs, tile = refs[-3:-1], refs[-1]
    a, b = xo[...], xt[...]
    r0, r1 = route[:, 0:1], route[:, 1:2]
    acc0 = jnp.zeros((a.shape[0], width), F32)
    acc1 = acc0
    for e in range(E_A):
        r = dot(a, wm[e]) + dot(b, wt[e])
        acc0 = jnp.where(r0 == e, r, acc0)
        acc1 = jnp.where(r1 == e, r, acc1)
    tile[:, 0:width] = acc0.astype(BF)
    tile[:, width : 2 * width] = acc1.astype(BF)
    for i in range(n_extra):
        r = dot(a, wm[E_A + i]) + dot(b, wt[E_A + i])
        tile[:, (2 + i) * width : (3 + i) * width] = r.astype(BF)
    for i in range(n):

        @pl.when(pl.program_id(0) == i)
        def _():
            outs[i // (n // 2)][i % (n // 2)] = tile[...]


def rotate(u, cosf, sinf):
    return u * cosf + pltpu.roll(u, HD // 2, 1) * sinf


def unrotate(u, cosf, sinf):
    return u * cosf - pltpu.roll(u, HD // 2, 1) * sinf


def add_halves(refs):
    a0, a1, b0, b1 = refs
    top = a0[...].astype(F32) + a1[...].astype(F32)
    low = b0[...].astype(F32) + b1[...].astype(F32)
    return jnp.concatenate((top, low), axis=0)


def allowed_pairs(doc_col, doc_row):
    n = doc_col.shape[0]
    t = lax.broadcasted_iota(jnp.int32, (n, n), 0)
    u = lax.broadcasted_iota(jnp.int32, (n, n), 1)
    return (doc_col[...] == doc_row[...]) & (u <= t) & (doc_col[...] < DOCS)


def attend_body(hc, sc, a0, a1, b0, b1, doc_col, doc_row, cosr, sinr, qkv, out, lse):
    width = hc * HD
    u = add_halves((a0, a1, b0, b1))
    cosf, sinf = cosr[...], sinr[...]
    ok = allowed_pairs(doc_col, doc_row)
    for h in range(hc):
        at = 2 * width + h * HD
        k = rotate(u[:, at : at + HD], cosf, sinf).astype(BF)
        v = u[:, at + width : at + width + HD].astype(BF)
        qkv[:, at : at + HD] = k
        qkv[:, at + width : at + width + HD] = v
        for j in range(2):
            lo = j * width + h * HD
            q = rotate(u[:, lo : lo + HD], cosf, sinf).astype(BF)
            qkv[:, lo : lo + HD] = q
            s = jnp.where(ok, dot_nt(q, k) * (HD**-0.5), masked_score)
            m = jnp.max(s, axis=1, keepdims=True)
            p = jnp.where(ok, jnp.exp(s - m), 0.0)
            total = jnp.sum(p, axis=1, keepdims=True)
            total = jnp.where(total > 0, total, 1.0)
            out[:, lo : lo + HD] = (dot(p.astype(BF), v) / total).astype(BF)
            lse[:, 2 * h + j : 2 * h + j + 1] = m + jnp.log(total)


def attend_back_body(hc, sc, a0, a1, b0, b1, qkv, att, lse, gates, doc_col, doc_row, cosr, sinr, grads, dgate):
    width = hc * HD
    u = add_halves((a0, a1, b0, b1))
    cosf, sinf = cosr[...], sinr[...]
    ok = allowed_pairs(doc_col, doc_row)
    keep = (doc_col[...] < DOCS).astype(F32)
    dg = [jnp.zeros((u.shape[0], 1), F32) for _ in range(2)]
    for h in range(hc):
        at = 2 * width + h * HD
        k = qkv[:, at : at + HD]
        v = qkv[:, at + width : at + width + HD]
        dk = jnp.zeros((u.shape[0], HD), F32)
        dv = dk
        for j in range(2):
            lo = j * width + h * HD
            q = qkv[:, lo : lo + HD]
            o = att[:, lo : lo + HD].astype(F32)
            raw = u[:, lo : lo + HD]
            dg[j] = dg[j] + jnp.sum(raw * o, axis=1, keepdims=True)
            do = (raw * (gates[:, j : j + 1] * keep)).astype(BF)
            delta = jnp.sum(do.astype(F32) * o, axis=1, keepdims=True)
            s = dot_nt(q, k) * (HD**-0.5)
            p = jnp.where(ok, jnp.exp(s - lse[:, 2 * h + j : 2 * h + j + 1]), 0.0)
            ds = (p * (dot_nt(do, v) - delta)).astype(BF)
            dq = dot(ds, k) * (HD**-0.5)
            grads[:, lo : lo + HD] = unrotate(dq, cosf, sinf).astype(BF)
            dk = dk + dot_tn(ds, q)
            dv = dv + dot_tn(p.astype(BF), do)
        grads[:, at : at + HD] = unrotate(dk * (HD**-0.5), cosf, sinf).astype(BF)
        grads[:, at + width : at + width + HD] = dv.astype(BF)
    dgate[...] = jnp.zeros_like(dgate)
    dgate[:, 0:1] = dg[0]
    dgate[:, 1:2] = dg[1]


def chosen(hot0, hot1, a, b, e):
    return a * hot0[e] + b * hot1[e]


def one_hots(route):
    return [[jnp.where(route[:, j : j + 1] == e, 1.0, 0.0).astype(BF) for e in range(E_A)] for j in range(2)]


def gated(vals, gates, width):
    a = (vals[:, 0:width].astype(F32) * gates[:, 0:1]).astype(BF)
    b = (vals[:, width : 2 * width].astype(F32) * gates[:, 1:2]).astype(BF)
    return a, b


def att_out_body(width, sc, route, gates, om, ot, wm, wt, prev, out):
    acc = jnp.zeros(out.shape[1:], F32)
    hot0, hot1 = one_hots(route)
    am, bm = gated(om, gates, width)
    at, bt = gated(ot, gates, width)
    for e in range(E_A):
        acc += dot_nt(chosen(hot0, hot1, am, bm, e), wm[e])
        acc += dot_nt(chosen(hot0, hot1, at, bt, e), wt[e])
    out[0] = acc.astype(BF)


def att_in_back_body(width, sc, route, gm, gt, wm, wt, prev, out):
    acc = jnp.zeros(out.shape[1:], F32)
    hot0, hot1 = one_hots(route)
    am, bm = gm[:, 0:width], gm[:, width : 2 * width]
    at, bt = gt[:, 0:width], gt[:, width : 2 * width]
    for e in range(E_A):
        acc += dot_nt(chosen(hot0, hot1, am, bm, e), wm[e])
        acc += dot_nt(chosen(hot0, hot1, at, bt, e), wt[e])
    for i in range(2):
        lo = (2 + i) * width
        acc += dot_nt(gm[:, lo : lo + width], wm[E_A + i]) + dot_nt(gt[:, lo : lo + width], wt[E_A + i])
    out[0] = acc.astype(BF)


def att_weight_body(width, n, with_gates, extra, sc, *refs):
    xt, route, gates = refs[0], refs[1], refs[2]
    pieces = refs[3 : 3 + 2 * n]
    out = refs[3 + 2 * n]
    out2 = refs[4 + 2 * n] if extra else None
    vals = refs[-1]
    seq = route.shape[1]
    half = pl.program_id(0)
    e = pl.program_id(1)
    for side in range(2):

        @pl.when((half == side) & (e == 0))
        def _():
            for k in range(n):
                piece = pieces[2 * k + side]
                if with_gates:
                    a, b = gated(piece, gates[sc[k]], width)
                else:
                    a, b = piece[:, 0:width], piece[:, width : 2 * width]
                vals[k, :, 0:width] = a
                vals[k, :, width : 2 * width] = b
            if extra:
                for i in range(2):
                    lo = (2 + i) * width
                    acc = jnp.zeros((xt.shape[1], width), F32)
                    for k in range(n):
                        acc += dot(xt[sc[k]], pieces[2 * k + side][:, lo : lo + width])
                    out2[:, i, :] = acc

    acc = jnp.zeros((xt.shape[1], width), F32)
    for k in range(n):
        r = route[sc[k]]
        hot0 = jnp.where(r[:, 0:1] == e, 1.0, 0.0).astype(BF)
        hot1 = jnp.where(r[:, 1:2] == e, 1.0, 0.0).astype(BF)
        sel = vals[k, :, 0:width] * hot0 + vals[k, :, width : 2 * width] * hot1
        acc += dot(xt[sc[k]], sel)
    for i in range(E_A):

        @pl.when(e == i)
        def _():
            out[:, i, :] = acc


def row_chunks(rows):
    step = min(rows, 1024)
    return [(i, step) for i in range(0, rows, step)]


def group_proj_body(n, parts, base, sc, pos, xo, xt, wm, wt, *refs):
    outs, xs = refs[:parts], refs[parts]
    i = pl.program_id(0)
    steps = pl.num_programs(0)
    ts = outs[0].shape[1]
    dc = xo.shape[1]
    at = base + n + i
    tile, e, kind = sc[at], sc[at + steps], sc[at + 2 * steps]
    p0 = sc[base + tile]

    @pl.when(kind == 2)
    def _():
        a = jnp.zeros((ts, dc), F32)
        b = a
        for lo, m in row_chunks(xo.shape[0]):
            ids = p0 + lax.broadcasted_iota(jnp.int32, (ts, m), 0)
            hot = (pos[0:1, lo : lo + m] == ids) | (pos[1:2, lo : lo + m] == ids)
            hot = jnp.where(hot, 1.0, 0.0).astype(BF)
            a = a + dot(hot, xo[lo : lo + m, :])
            b = b + dot(hot, xt[lo : lo + m, :])
        xs[:, 0:dc] = a.astype(BF)
        xs[:, dc : 2 * dc] = b.astype(BF)

    rows = p0 + lax.broadcasted_iota(jnp.int32, (ts, 1), 0)
    for t in range(n):
        out, at = outs[t // (n // parts)], t % (n // parts)

        @pl.when((kind == 2) & (tile == t))
        def _():
            out[at] = (dot(xs[:, 0:dc], wm[0]) + dot(xs[:, dc : 2 * dc], wt[0])).astype(BF)

        @pl.when((kind == 1) & (tile == t))
        def _():
            r = dot(xs[:, 0:dc], wm[0]) + dot(xs[:, dc : 2 * dc], wt[0])
            out[at] = jnp.where(rows >= sc[base + n + 3 * steps + e], r, out[at].astype(F32)).astype(BF)


def middle_body(fl, sc, pos, rowv, *refs):
    gu, da = refs[0:4], refs[4:6]
    dgu, act, tok = refs[6:]
    ts = gu[0].shape[0]
    rows = pos.shape[1]
    half = pl.program_id(0)
    p0 = sc[half]
    inv = jnp.zeros((ts, 1), F32)
    gate = inv
    for lo, n in row_chunks(rows):
        ids = p0 + lax.broadcasted_iota(jnp.int32, (ts, n), 0)
        is0 = pos[0:1, lo : lo + n] == ids
        is1 = pos[1:2, lo : lo + n] == ids
        inv += jnp.sum(jnp.where(is0 | is1, rowv[0:1, lo : lo + n], 0.0), axis=1, keepdims=True)
        picked = jnp.where(is0, rowv[1:2, lo : lo + n], jnp.where(is1, rowv[2:3, lo : lo + n], 0.0))
        gate += jnp.sum(picked, axis=1, keepdims=True)

    def work(g0, g1, d):
        dpf = jnp.zeros((ts, 128), F32)
        dn = dpf
        step = 128
        for lo in range(0, fl, step):
            gt = (g0[:, lo : lo + step].astype(F32) + g1[:, lo : lo + step].astype(F32)) * inv
            up = (g0[:, fl + lo : fl + lo + step].astype(F32) + g1[:, fl + lo : fl + lo + step].astype(F32)) * inv
            raw = d[:, lo : lo + step].astype(F32)
            sg = 1.0 / (1.0 + jnp.exp(-gt))
            silu = gt * sg
            a = silu * up
            act[0, :, lo : lo + step] = (a * gate).astype(BF)
            da = raw * gate
            dgt = da * up * (sg + silu * (1.0 - sg))
            dup = da * silu
            dgu[0, :, lo : lo + step] = (dgt * inv).astype(BF)
            dgu[0, :, fl + lo : fl + lo + step] = (dup * inv).astype(BF)
            dpf += raw * a
            dn += dgt * gt + dup * up
        dpf = jnp.sum(dpf, axis=1, keepdims=True)
        dn = jnp.sum(dn, axis=1, keepdims=True)
        for lo, n in row_chunks(rows):
            ids = p0 + lax.broadcasted_iota(jnp.int32, (ts, n), 0)
            is0 = pos[0:1, lo : lo + n] == ids
            is1 = pos[1:2, lo : lo + n] == ids
            t0 = jnp.sum(jnp.where(is0, dpf, 0.0), axis=0, keepdims=True)
            t1 = jnp.sum(jnp.where(is1, dpf, 0.0), axis=0, keepdims=True)
            t2 = jnp.sum(jnp.where(is0 | is1, dn, 0.0), axis=0, keepdims=True)
            new = jnp.concatenate((t0, t1, t2, jnp.zeros((5, n), F32)), axis=0)
            tok[:, lo : lo + n] = new + jnp.where(half == 0, 0.0, tok[:, lo : lo + n])

    for h in range(2):

        @pl.when(half == h)
        def _():
            work(*gu[2 * h : 2 * h + 2], da[h])


def piece_of(arrays, place):
    i, h = place
    return arrays[i][...] if h is None else arrays[i][h]


def group_back_body(where, base, sc, posc, *refs):
    n = len(where)
    arrays, (w, prev, out, dh) = refs[:-4], refs[-4:]
    i = pl.program_id(0)
    steps = pl.num_programs(0)
    ts = dh.shape[0] // n
    at = base + n + i
    tile, e, kind = sc[at], sc[at + steps], sc[at + 2 * steps]
    p0 = sc[base + tile]
    rows = p0 + lax.broadcasted_iota(jnp.int32, (ts, 1), 0)
    for t in range(n):

        @pl.when((kind == 2) & (tile == t))
        def _():
            dh[t * ts : (t + 1) * ts, :] = dot_nt(piece_of(arrays, where[t]), w[0])

        @pl.when((kind == 1) & (tile == t))
        def _():
            r = dot_nt(piece_of(arrays, where[t]), w[0])
            old = dh[t * ts : (t + 1) * ts, :]
            dh[t * ts : (t + 1) * ts, :] = jnp.where(rows >= sc[base + n + 3 * steps + e], r, old)

    @pl.when(i == steps - 1)
    def _():
        for lo, m in row_chunks(out.shape[0]):
            acc = prev[lo : lo + m, :]
            for t in range(n):
                ids = sc[base + t] + lax.broadcasted_iota(jnp.int32, (m, ts), 1)
                hot = (posc[lo : lo + m, 0:1] == ids) | (posc[lo : lo + m, 1:2] == ids)
                acc = acc + dot(jnp.where(hot, 1.0, 0.0).astype(BF), dh[t * ts : (t + 1) * ts, :].astype(BF))
            out[lo : lo + m, :] = acc


def sort_t_body(sc, pos, x, out):
    p0 = sc[pl.program_id(0)]
    ts = out.shape[1]
    acc = jnp.zeros((ts, x.shape[1]), F32)
    for lo, m in row_chunks(x.shape[0]):
        ids = p0 + lax.broadcasted_iota(jnp.int32, (ts, m), 0)
        hot = (pos[0:1, lo : lo + m] == ids) | (pos[1:2, lo : lo + m] == ids)
        acc += dot(jnp.where(hot, 1.0, 0.0).astype(BF), x[lo : lo + m, :])
    out[...] = jnp.transpose(acc).astype(BF)


def group_weight_body(where, fl, sc, xs, *refs):
    n = len(where)
    arrays, (out, acc) = refs[:-2], refs[-2:]
    ts = xs.shape[1] // n
    e = pl.program_id(0)
    lo, hi = sc[n + e], sc[n + e + 1]
    acc[...] = jnp.zeros_like(acc)
    for i in range(n):
        p0 = sc[i]

        @pl.when((p0 < hi) & (p0 + ts > lo))
        def _():
            ids = p0 + lax.broadcasted_iota(jnp.int32, (1, ts), 1)
            ok = jnp.where((ids >= lo) & (ids < hi), 1.0, 0.0).astype(BF)
            acc[...] += dot(xs[:, i * ts : (i + 1) * ts] * ok, piece_of(arrays, where[i]))

    if len(out.shape) == 4:
        real = out.shape[3]
        out[:, 0, 0, :] = acc[:, 0:real]
        out[:, 0, 1, :] = acc[:, fl : fl + real]
    else:
        for i in range(E_F):

            @pl.when(e == i)
            def _():
                out[:, i, :] = acc[:, 0 : out.shape[2]]


def hold_body(sc, out):
    out[...] = jnp.zeros_like(out)


def add_body(sc, x, got, out):
    out[...] = x[...] + got[...]


def join_body(axis, n, sc, *refs):
    size = refs[0].shape[axis]
    for k in range(n):
        if axis:
            refs[n][:, k * size : (k + 1) * size] = refs[k][...]
        else:
            refs[n][k * size : (k + 1) * size, :] = refs[k][...]


def join_scaled_body(n, sc, gain, *refs):
    size = refs[0].shape[0]
    for k in range(n):
        v = refs[k][...]
        refs[n][k * size : (k + 1) * size, :] = v
        refs[n + 1][k * size : (k + 1) * size, :] = (v.astype(F32) * gain[...]).astype(BF)


def pairs_body(sc, a0, a1, b0, b1, a, b):
    a[...] = (a0[...].astype(F32) + a1[...].astype(F32)).astype(BF)
    b[...] = (b0[...].astype(F32) + b1[...].astype(F32)).astype(BF)


def total_body(n, sc, *refs):
    total = refs[0][...].astype(F32)
    for v in refs[1:n]:
        total = total + v[...].astype(F32)
    refs[n][...] = total
    refs[n + 1][...] = total.astype(BF)


def step_body(sc, *refs):
    for h in range(2):
        refs[4 + h][...] = (refs[2 * h][...].astype(F32) + refs[2 * h + 1][...].astype(F32)).astype(BF)


def middle_grad_body(n, sc, dy, y1, dlf, coef, rf, gf, *refs):
    i = pl.program_id(0)
    dy1, dh2 = refs[n:]
    router = dot_tn(dlf[...], rf[...])

    def work(part):
        total = part[...].astype(F32) + router
        dy1[...] = (dy[...].astype(F32) + total * gf[...] - y1[...].astype(F32) * coef[...]).astype(BF)

        @pl.when(i == 0)
        def _():
            dh2[...] = total

    for k in range(n):

        @pl.when(i == k)
        def _():
            work(refs[k])


def prep_gate_up_body(fl, sc, w, out):
    real = w.shape[3]
    for e in range(E_F):
        for j in range(2):
            out[e, :, j * fl : j * fl + real] = w[:, e, j, :].astype(BF)
            if real != fl:
                out[e, :, j * fl + real : (j + 1) * fl] = jnp.zeros((w.shape[0], fl - real), BF)


def prep_down_body(fl, sc, w, out):
    real = w.shape[2]
    out[:, :, 0:real] = jnp.swapaxes(w[...].astype(BF), 0, 1)
    if real != fl:
        out[:, :, real:fl] = jnp.zeros((E_F, w.shape[0], fl - real), BF)


def per_device(
    inputs,
    cotangent,
    doc_lengths,
    att_routes,
    ffn_routes,
    kv_weight,
    query_weight,
    output_weight,
    att_router,
    att_gain,
    gate_up_weight,
    down_weight,
    ffn_router,
    ffn_gain,
):
    n_ctx = lax.axis_size("ctx")
    n_z = lax.axis_size("fsdp")
    c = lax.axis_index("ctx")
    f = lax.axis_index("fsdp")
    n_chip = n_ctx // 2
    chip, core = c // 2, c % 2
    tok = inputs.shape[1]
    seq = tok * n_ctx
    dc = D // n_ctx
    rows = n_z * seq
    hc = HEADS // n_z // 2
    width = hc * HD
    half = seq // 2
    fl_real = FF // n_z
    fl = -(-fl_real // 128) * 128
    ts = 2 * rows // n_ctx // 2
    assert n_chip == n_z

    chain = []
    launch = functools.partial(call, chain)

    def swap(x, axis, k, n):
        return lax.ppermute(x, axis, [(i, i ^ k) for i in range(n)])

    def core_swap(x):
        return swap(x, "ctx", 1, n_ctx)

    def chip_swap(x, k):
        return swap(x, "ctx", 2 * k, n_ctx)

    def z_swap(x, k):
        return swap(x, "fsdp", k, n_z)

    chip_bits = [1 << i for i in range(n_chip.bit_length() - 1)]
    z_bits = [1 << i for i in range(n_z.bit_length() - 1)]

    def z_gather(x):
        return [x] + [z_swap(x, k) for k in range(1, n_z)]

    def z_send(pieces):
        return [pieces[0]] + [z_swap(pieces[k], k) for k in range(1, n_z)]

    def z_total(got, *others):
        got = [*got, *others]
        return launch(
            functools.partial(total_body, len(got)),
            jnp.zeros((1,), jnp.int32),
            (1,),
            [spec((seq, dc))] * len(got),
            [spec((seq, dc))] * 2,
            [jax.ShapeDtypeStruct((seq, dc), F32), jax.ShapeDtypeStruct((seq, dc), BF)],
            us=1.5,
        )(*got)

    def mark(*values):
        chain.extend(values)

    one = jnp.zeros((1,), jnp.int32)

    def hold(*vals):
        out = launch(
            hold_body, one, (1,), [], spec((8, 128)), jax.ShapeDtypeStruct((8, 128), F32), us=0.5
        )(carry=vals)
        return list(out[1:])

    def join(vals, axis):
        m, n = vals[0].shape
        shape = (m, len(vals) * n) if axis else (len(vals) * m, n)
        return launch(
            functools.partial(join_body, axis, len(vals)),
            one,
            (1,),
            [spec((m, n))] * len(vals),
            spec(shape),
            jax.ShapeDtypeStruct(shape, vals[0].dtype),
            us=1.5,
        )(*vals)

    def join_scaled(vals, gain):
        m, n = vals[0].shape
        shape = (len(vals) * m, n)
        return launch(
            functools.partial(join_scaled_body, len(vals)),
            one,
            (1,),
            [spec((1, n))] + [spec((m, n))] * len(vals),
            [spec(shape)] * 2,
            [jax.ShapeDtypeStruct(shape, BF)] * 2,
            us=2,
        )(gain, *vals)

    class Small:
        def __init__(self, x, hops):
            self.x = x
            self.todo = [
                (kind, b)
                for kind in hops
                for b in {"c": [1], "x": [2 * b for b in chip_bits], "z": z_bits, "g": z_bits}[kind]
            ]
            self.send()

        def send(self):
            kind, b = self.todo[0]
            axis, n = ("ctx", n_ctx) if kind in "cx" else ("fsdp", n_z)
            self.got = swap(self.x, axis, b, n)

        def step(self):
            if not self.todo:
                return
            kind, _ = self.todo.pop(0)
            if kind == "g":
                self.x = join([self.x, self.got], 1)
            else:
                m = self.x.shape
                self.x = launch(
                    add_body,
                    one,
                    (1,),
                    [spec(m)] * 2,
                    spec(m),
                    jax.ShapeDtypeStruct(m, F32),
                    us=0.5,
                )(self.x, self.got)
            if self.todo:
                self.send()

        def finish(self):
            while self.todo:
                self.step()
            return self.x

    orders = (chip_bits, chip_bits[::-1])

    def kept(order):
        ks = [0]
        for b in reversed(order[1:]):
            ks = ks + [k ^ b for k in ks]
        return ks

    late = [(k, h) for h in range(2) for k in kept(orders[h])]
    early = [(k ^ orders[h][0], h) for k, h in late]
    groups = (early, late, early + late)

    def send_first(tiles):
        return [chip_swap(tiles[h], orders[h][0]) for h in range(2)]

    def send_next(keep, got, step):
        n, m, cols = keep[0].shape

        def add(first):
            some = spec((1, m, cols), lambda i, sc: (i + first, 0, 0))
            part = spec((1, m, cols), lambda i, sc: (i, 0, 0))
            return launch(
                step_body,
                one,
                (n // 2,),
                [some] * 4,
                [part] * 2,
                [jax.ShapeDtypeStruct((n // 2, m, cols), BF)] * 2,
                us=n * m * cols * 4e-6,
            )(keep[0], got[0], keep[1], got[1])

        left = add(n // 2)
        sent = [chip_swap(left[h], orders[h][step]) for h in range(2)]
        return add(0), sent

    def finish_reduce(keep, got, step):
        while keep[0].shape[0] > 1:
            keep, got = send_next(keep, got, step)
            step += 1
        return [v[0] for h in range(2) for v in (keep[h], got[h])]

    def rel(x):
        return jnp.take(x, f ^ jnp.arange(n_z, dtype=jnp.int32), axis=0)

    x_loc = inputs[0].astype(F32)
    ends = jnp.cumsum(doc_lengths, axis=1)
    my_pos = c * tok + jnp.arange(tok, dtype=jnp.int32)
    my_ends = lax.dynamic_slice_in_dim(ends, f, 1, 0)
    my_keep = (my_pos < my_ends[0, DOCS - 1]).astype(F32)[:, None]
    inv1_loc = lax.rsqrt(jnp.mean(x_loc * x_loc, axis=1, keepdims=True) + norm_eps)
    n1_loc = x_loc * inv1_loc
    dy_loc = cotangent[0].astype(F32) * my_keep
    payload = jnp.stack((n1_loc.astype(BF), dy_loc.astype(BF), inputs[0]), axis=1)
    payload = payload.reshape(tok, 3, n_ctx, dc).transpose(2, 0, 1, 3).reshape(n_ctx, tok, 3 * dc)
    payload = lax.all_to_all(payload, "ctx", 0, 0, tiled=True).reshape(seq, 3 * dc)
    n1_own, dy_own, x_own = payload[:, :dc], payload[:, dc : 2 * dc], payload[:, 2 * dc :]

    routes = jnp.concatenate((att_routes, ffn_routes), axis=2)[None]
    for b in [1] + [2 * v for v in chip_bits]:
        routes = jnp.concatenate((routes, swap(routes, "ctx", b, n_ctx)), axis=0)
    routes = jnp.take(routes, c ^ jnp.arange(n_ctx, dtype=jnp.int32), axis=0).reshape(seq, n_z, 4)
    routes = rel(jnp.transpose(routes, (1, 0, 2))).reshape(rows, 4)
    route_row = jnp.transpose(routes)
    att_route3 = routes[:, :2].reshape(n_z, seq, 2)
    experts = jnp.arange(E_F, dtype=jnp.int32)

    def split_halves(w):
        mine = lax.dynamic_slice_in_dim(w, core * width, width, 2)
        theirs = lax.dynamic_slice_in_dim(w, (1 - core) * width, width, 2)
        return mine, theirs, core_swap(theirs)

    def e_major(w):
        return jnp.transpose(w.astype(BF), (1, 0, 2))

    qk_weight = jnp.concatenate((e_major(query_weight), e_major(kv_weight)), axis=0)
    wqk_m, wqk_t, wqk_x = split_halves(qk_weight)
    small = jnp.concatenate((att_gain[None], ffn_gain[None]), axis=0)
    small_t = core_swap(small.astype(BF)).astype(F32)
    small = small.astype(BF).astype(F32)
    ga, gf, ga_t, gf_t = small[0:1], small[1:2], small_t[0:1], small_t[1:2]
    ra, rf = att_router.astype(BF), ffn_router.astype(BF)

    def row_logits(router, hidden):
        return lax.dot_general(router, hidden, (((0,), (1,)), ((), ())), preferred_element_type=F32)

    def gates_of(logits, route2):
        picked = jnp.sum(jnp.where(route2[:, None, :] == experts[None, :, None], logits[None], 0.0), axis=1)
        return jax.nn.softmax(picked, axis=0)

    n1 = z_gather(n1_own)
    la = Small(row_logits(ra, (n1_own.astype(F32) * ga).astype(BF)), "cxg")
    step = 32
    mark(n1_own)
    wg, dy_own = launch(
        functools.partial(prep_gate_up_body, fl),
        jnp.zeros((1,), jnp.int32),
        (dc // step,),
        [spec((step, E_F, 2, fl_real), lambda i, sc: (i, 0, 0, 0))],
        spec((E_F, step, 2 * fl), lambda i, sc: (0, i, 0)),
        jax.ShapeDtypeStruct((E_F, dc, 2 * fl), BF),
            us=26,
    )(gate_up_weight, carry=(dy_own,))
    n1, h1 = join_scaled(n1, ga)
    n1_t = core_swap(n1)
    wg_x = core_swap(wg)
    dy = dy_own
    dy_got = z_swap(dy, z_bits[0])
    h1_x = (n1_t.astype(F32) * ga_t).astype(BF)
    def project(xo, xt, weights, n_extra, g):
        cols = (2 + n_extra) * width
        group = groups[g]
        n = len(group)
        at = lambda i, sc: (sc[i], 0)
        return launch(
            functools.partial(proj_body, n_extra, width, n),
            jnp.stack([2 * (chip ^ k) + h for k, h in group]),
            (n,),
            [spec((half, 4), at), spec((half, dc), at), spec((half, dc), at)] + [spec(w.shape) for w in weights],
            [spec((n // 2, half, cols))] * 2,
            [jax.ShapeDtypeStruct((n // 2, half, cols), BF)] * 2,
            [pltpu.VMEM((half, cols), BF)],
            us=8 if n_extra else 7,
        )(routes, xo, xt, *weights)

    def prep_down():
        return launch(
            functools.partial(prep_down_body, fl),
            jnp.zeros((1,), jnp.int32),
            (dc // step,),
            [spec((step, E_F, fl_real), lambda i, sc: (i, 0, 0))],
            spec((E_F, step, fl), lambda i, sc: (0, i, 0)),
            jax.ShapeDtypeStruct((E_F, dc, fl), BF),
                us=9.5,
        )(down_weight)

    la.step()
    tiles = project(h1, h1_x, (wqk_m, wqk_x), 2, 0)
    la.step()
    sent = send_first(tiles)
    dy = join([dy, dy_got], 0)
    dy_got = z_swap(dy, z_bits[1])
    keep = project(h1, h1_x, (wqk_m, wqk_x), 2, 1)
    for b in z_bits[2:]:
        dy = join([dy, dy_got], 0)
        dy_got = z_swap(dy, b)
    dy_all = join([dy, dy_got], 0)
    la.step()

    hot = (route_row[2:4, None, :] == experts[None, :, None]).astype(F32)
    blocks = rows // 128
    hot_b = hot.reshape(2 * E_F, blocks, 128)
    lane = jnp.arange(128)
    tri = (lane[:, None] < lane[None, :]).astype(BF)
    before = jnp.einsum("anl,lm->anm", hot_b.astype(BF), tri, preferred_element_type=F32)
    totals = jnp.sum(hot_b, axis=2)
    lane_b = jnp.arange(blocks)
    tri_b = (lane_b[:, None] < lane_b[None, :]).astype(BF)
    before_b = jnp.dot(totals.astype(BF), tri_b, preferred_element_type=F32)
    rank = (before + before_b[:, :, None]).reshape(2, E_F, rows)
    counts = jnp.sum(totals, axis=1).reshape(2, E_F)
    per_expert = counts[0] + counts[1]
    off = jnp.sum(jnp.where(experts[:, None] > experts[None, :], per_expert[None, :], 0.0), axis=1)
    base = jnp.stack((off, off + counts[0]))
    pos_row = jnp.sum(hot * (base[:, :, None] + rank), axis=1).astype(jnp.int32)
    pos_col = jnp.transpose(pos_row)
    offsets = jnp.concatenate((off, jnp.sum(per_expert)[None])).astype(jnp.int32)

    def start_of(k, other, h):
        return 2 * ts * (2 * (chip ^ k) + (core ^ other)) + h * ts

    def tile_scalars(table):
        ks, others, hs = (jnp.array([[t[i] for t in row] for row in table], jnp.int32) for i in range(3))
        p0 = start_of(ks, others, hs)
        n = p0.shape[1]
        first = jnp.sum((offsets[1:] <= p0[..., None]).astype(jnp.int32), axis=2)
        last = jnp.sum((offsets[1:] <= p0[..., None] + ts - 1).astype(jnp.int32), axis=2)
        count = last - first + 1
        lower = jnp.arange(n)[:, None] >= jnp.arange(n)[None, :]
        upto = jnp.sum(jnp.where(lower, count[:, None, :], 0), axis=2)
        v = jnp.arange(n + E_F - 1, dtype=jnp.int32)
        tile = jnp.minimum(jnp.sum((upto[:, None, :] <= v[:, None]).astype(jnp.int32), axis=2), n - 1)
        mine = tile[:, :, None] == jnp.arange(n)
        begin_v = jnp.sum(jnp.where(mine, (upto - count)[:, None, :], 0), axis=2)
        first_v = jnp.sum(jnp.where(mine, first[:, None, :], 0), axis=2)
        last_v = jnp.sum(jnp.where(mine, last[:, None, :], 0), axis=2)
        e = jnp.minimum(first_v + v - begin_v, last_v)
        kind = jnp.where(v < upto[:, -1:], jnp.where(v == begin_v, 2, 1), 0)
        ends = jnp.broadcast_to(offsets, (len(table), E_F + 1))
        return jnp.concatenate((p0, tile, e, kind, ends), axis=1).astype(jnp.int32)

    proj_scalars = tile_scalars([[(k, 0, h) for k, h in group] for group in groups[:2]])
    all_scalars = tile_scalars([[(k, 0, h) for k, h in groups[2]]]).reshape(-1)
    back_table = [[(k, other, h) for other in range(2) for h in range(2)] for k in range(n_chip)]
    n_pieces = 4 * n_chip
    starts_all = start_of(*(jnp.array([t[i] for row in back_table for t in row], jnp.int32) for i in range(3)))
    weight_scalars = jnp.concatenate((starts_all, offsets))
    proj_length = proj_scalars.shape[1]
    proj_scalars = proj_scalars.reshape(-1)

    def group_proj(xo, xt, wm, wx, g):
        m = wm.shape[2]
        n = len(groups[g])
        steps = n + E_F - 1
        lo = g * proj_length if g < 2 else 0
        parts = 2 if g < 2 else 4
        by_expert = spec((1, dc, m), lambda i, sc: (sc[lo + n + steps + i], 0, 0))
        return launch(
            functools.partial(group_proj_body, n, parts, lo),
            proj_scalars if g < 2 else all_scalars,
            (steps,),
            [spec((2, rows)), spec((rows, dc)), spec((rows, dc)), by_expert, by_expert],
            [spec((n // parts, ts, m))] * parts,
            [jax.ShapeDtypeStruct((n // parts, ts, m), BF)] * parts,
            [pltpu.VMEM((ts, 2 * dc), BF)],
            us=17 if m > fl else 27,
        )(pos_row, xo, xt, wm, wx)

    def sort_t(x):
        return launch(
            sort_t_body,
            starts_all,
            (n_pieces,),
            [spec((2, rows)), spec((rows, dc))],
            spec((dc, ts), lambda i, sc: (0, i)),
            jax.ShapeDtypeStruct((dc, 2 * rows), BF),
            us=13,
        )(pos_row, x)

    if keep[0].shape[0] > 1:
        keep, sent = send_next(keep, sent, 1)
    wd = prep_down()
    wd_x = core_swap(wd)
    dy_x = core_swap(dy_all)
    la.step()
    qkv_parts = finish_reduce(keep, sent, 2)

    s_abs = f ^ chip
    positions = jnp.arange(seq, dtype=jnp.int32)
    my_ends = lax.dynamic_index_in_dim(ends, s_abs, 0, keepdims=False)
    my_starts = my_ends - lax.dynamic_index_in_dim(doc_lengths, s_abs, 0, keepdims=False)
    doc_one = jnp.sum((positions[:, None] >= my_ends).astype(jnp.int32), axis=1)
    begin = jnp.sum(jnp.where(doc_one[:, None] == jnp.arange(DOCS, dtype=jnp.int32), my_starts, 0), axis=1)
    doc_col, doc_row = doc_one[:, None], doc_one[None, :]
    halves = jnp.arange(HD // 2, dtype=F32)
    angles = (positions - begin).astype(F32)[:, None] * (rope_base ** (-2.0 * halves / HD))[None, :]
    cos, sin = jnp.cos(angles), jnp.sin(angles)
    cosf = jnp.concatenate((cos, cos), axis=1)
    sinf = jnp.concatenate((-sin, sin), axis=1)

    qkv, ao, lse = launch(
        functools.partial(attend_body, hc),
        one,
        (1,),
        [spec((half, 4 * width))] * 4 + [spec((seq, 1)), spec((1, seq)), spec((seq, HD)), spec((seq, HD))],
        [spec((seq, 4 * width)), spec((seq, 2 * width)), spec((seq, 128))],
        [
            jax.ShapeDtypeStruct((seq, 4 * width), BF),
            jax.ShapeDtypeStruct((seq, 2 * width), BF),
            jax.ShapeDtypeStruct((seq, 128), F32),
        ],
            us=7,
    )(*qkv_parts, doc_col, doc_row, cosf, sinf)

    ao_m = [ao] + [chip_swap(ao, k) for k in range(1, n_chip)]
    ao_t = [core_swap(ao)]
    wo_m, wo_t, wo_x = split_halves(e_major(output_weight))
    la.step()
    (wg_x,) = hold(wg_x)
    da_all = group_proj(dy_all, dy_x, wd, wd_x, 2)
    da_tiles, da_keep = da_all[:2], da_all[2:]
    ao_m = [ao] + hold(*ao_m[1:])
    ao_t += [core_swap(v) for v in ao_m[1:]]
    pa = gates_of(la.finish(), route_row[0:2])
    pa3 = jnp.transpose(pa).reshape(n_z, seq, 2)

    def into_stream(body, k, streams, vals, weights, buf, us, cols, carry=()):
        sc = jnp.reshape(chip ^ k, (1,))
        by_stream = [spec((pl.squeezed, seq, 2), lambda i, sc: (sc[0], 0, 0))] * len(streams)
        n_in = len(streams) + 2 + len(weights)
        return launch(
            body,
            sc,
            (1,),
            by_stream
            + [spec((seq, cols))] * 2
            + [spec(w.shape) for w in weights]
            + [pl.BlockSpec(memory_space=pl.ANY)],
            spec((1, seq, dc), lambda i, sc: (sc[0], 0, 0)),
            jax.ShapeDtypeStruct((n_z, seq, dc), BF),
            aliases={n_in + 1: 0},
            us=us,
        )(*streams, *vals, *weights, buf, carry=carry)

    buf = jnp.zeros((n_z, seq, dc), BF)
    for k in range(n_chip):
        buf = into_stream(
            functools.partial(att_out_body, width),
            k,
            (att_route3, pa3),
            (ao_m[k], ao_t[k]),
            (wo_m, wo_t),
            buf,
            4.3,
            2 * width,
            da_tiles if k == n_chip - 1 else (),
        )
    buf, *da_tiles = buf
    y1_sent = z_send([buf[k] for k in range(n_z)])
    da_sent = send_first(da_tiles)
    y1, y1_own = z_total(y1_sent, x_own)

    y1_got = z_gather(y1_own)
    y1_f = y1_own.astype(F32)
    stat = jnp.concatenate(
        (
            row_logits(rf, (y1_f * gf).astype(BF)),
            jnp.sum(y1_f * y1_f, axis=1)[None],
            jnp.zeros((7, seq), F32),
        ),
        axis=0,
    )
    stat = Small(stat, "cxg")
    if da_keep[0].shape[0] > 1:
        da_keep, da_sent = send_next(da_keep, da_sent, 1)
    for _ in range(1 + len(chip_bits)):
        stat.step()
    y1_low, yg = join_scaled(y1_got, gf)
    yg_x = (core_swap(y1_low).astype(F32) * gf_t).astype(BF)

    gu_tiles = group_proj(yg, yg_x, wg, wg_x, 0)
    gu_sent = send_first(gu_tiles)
    da_parts = finish_reduce(da_keep, da_sent, 2)
    da_parts = launch(
        pairs_body,
        one,
        (1,),
        [spec((ts, fl))] * 4,
        [spec((ts, fl))] * 2,
        [jax.ShapeDtypeStruct((ts, fl), BF)] * 2,
        us=3,
    )(*da_parts)
    gu_keep = group_proj(yg, yg_x, wg, wg_x, 1)
    stat.step()
    yg_s = sort_t(yg)
    dy_s = sort_t(dy_all)
    if gu_keep[0].shape[0] > 1:
        gu_keep, gu_sent = send_next(gu_keep, gu_sent, 1)
    stat = stat.finish()
    inv2 = lax.rsqrt(stat[8:9] / D + norm_eps)
    lf = stat[0:E_F] * inv2
    pf = gates_of(lf, route_row[2:4])
    rowv = jnp.concatenate((inv2, pf, jnp.zeros((5, rows), F32)), axis=0)
    gu_parts = finish_reduce(gu_keep, gu_sent, 2)

    by_half = lambda n: spec((1, ts, n), lambda h, sc: (h, 0, 0))
    dgu, act, tok_sum = launch(
        functools.partial(middle_body, fl),
        jnp.stack([start_of(0, 0, h) for h in range(2)]),
        (2,),
        [spec((2, rows)), spec((8, rows))] + [spec((ts, 2 * fl))] * 4 + [spec((ts, fl))] * 2,
        [by_half(2 * fl), by_half(fl), spec((8, rows))],
        [
            jax.ShapeDtypeStruct((2, ts, 2 * fl), BF),
            jax.ShapeDtypeStruct((2, ts, fl), BF),
            jax.ShapeDtypeStruct((8, rows), F32),
        ],
            us=13,
    )(pos_row, rowv, *gu_parts, *da_parts)

    def router_back(dgate, gates, route2):
        dlog = gates * (dgate - jnp.sum(gates * dgate, axis=0, keepdims=True))
        return jnp.sum(jnp.where(route2[:, None, :] == experts[None, :, None], dlog[:, None, :], 0.0), axis=0)

    near = list(chip_bits)
    far = [k for k in range(1, n_chip) if k not in near]

    def gather_near(own):
        return {0: own} | {b: chip_swap(own, b) for b in near}

    def gather_far(got):
        result = {}
        for h in range(2):
            have = {k: got[k][h] for k in got}
            seen = orders[h][0]
            for b in orders[h][1:]:
                for k in [k for k in list(have) if k and not k & ~seen]:
                    have[k ^ b] = result[k ^ b, h] = chip_swap(have[k], b)
                seen |= b
        return result

    def whole(v):
        w = core_swap(v)
        return [(v, 0), (v, 1), (w, 0), (w, 1)]

    def apart(got, k):
        mine = [got[k, h] for h in range(2)]
        return [(v, None) for v in mine] + [(core_swap(v), None) for v in mine]

    def arrays_of(pieces):
        arrays, where = [], []
        for v, h in pieces:
            i = next((i for i, u in enumerate(arrays) if u is v), None)
            if i is None:
                i = len(arrays)
                arrays.append(v)
            where.append((i, h))
        return arrays, tuple(where)

    back_groups = ([0], near, far)
    back_scalars = [tile_scalars([[t for k in ks for t in back_table[k]]]).reshape(-1) for ks in back_groups]

    def group_back(g, pieces, w, acc, carry=()):
        m = w.shape[2]
        arrays, where = arrays_of([v for k in back_groups[g] for v in pieces[k]])
        n = len(where)
        steps = n + E_F - 1
        return launch(
            functools.partial(group_back_body, where, 0),
            back_scalars[g],
            (steps,),
            [spec((rows, 2))]
            + [spec(v.shape) for v in arrays]
            + [spec((1, dc, m), lambda i, sc: (sc[n + steps + i], 0, 0)), spec((rows, dc))],
            spec((rows, dc)),
            jax.ShapeDtypeStruct((rows, dc), F32),
            [pltpu.VMEM((n * ts, dc), F32)],
            aliases={3 + len(arrays): 0},
            us=3.4 * n if m > fl else 2.8 * n,
        )(pos_col, *arrays, w, acc, carry=carry)

    def group_weight(xs, pieces, out, out_spec):
        arrays, where = arrays_of([v for k in range(n_chip) for v in pieces[k]])
        m = arrays[0].shape[-1]
        return launch(
            functools.partial(group_weight_body, where, fl),
            weight_scalars,
            (E_F,),
            [spec((dc, 2 * rows))] + [spec(v.shape) for v in arrays],
            out_spec,
            out,
            [pltpu.VMEM((dc, m), F32)],
            us=30 if m > fl else 24,
        )(xs, *arrays)

    dgu_pieces = {0: whole(dgu)}
    act_x = core_swap(act)
    dgu_got = gather_near(dgu)

    tok_sum = Small(rel(tok_sum.reshape(8, n_z, seq).transpose(1, 0, 2)[:, :3]).reshape(n_z * 3, seq), "czx")
    for _ in range(len(z_bits)):
        tok_sum.step()

    dh2 = group_back(0, dgu_pieces, wg, jnp.zeros((rows, dc), F32))
    act_pieces = {0: [(act, 0), (act, 1), (act_x, 0), (act_x, 1)]}
    ffn = group_back(0, act_pieces, wd, jnp.zeros((rows, dc), F32))
    got = hold(*[dgu_got[b] for b in near])
    for b, v in zip(near, got):
        dgu_got[b] = v
        dgu_pieces[b] = whole(v)
    tok_sum.step()
    dgu_far = gather_far({b: dgu_got[b] for b in near})
    dh2, act = group_back(1, dgu_pieces, wg, dh2, carry=(act,))
    act_pieces[0] = [(act, 0), (act, 1), (act_x, 0), (act_x, 1)]
    tok_sum.step()
    dgu_far = dict(zip(dgu_far, hold(*dgu_far.values())))
    for k in far:
        dgu_pieces[k] = apart(dgu_far, k)
    act_got = gather_near(act)
    dh2 = group_back(2, dgu_pieces, wg, dh2)
    dh2_sent = z_send([dh2[k * seq : (k + 1) * seq].astype(BF) for k in range(n_z)])
    gate_up_grad = group_weight(
        yg_s,
        dgu_pieces,
        jax.ShapeDtypeStruct((dc, E_F, 2, fl_real), F32),
        spec((dc, 1, 2, fl_real), lambda e, sc: (0, e, 0, 0)),
    )
    _, dh2 = z_total(dh2_sent)
    dh2_got = z_gather(dh2)
    got = hold(*[act_got[b] for b in near])
    for b, v in zip(near, got):
        act_got[b] = v
        act_pieces[b] = whole(v)
    act_far = gather_far({b: act_got[b] for b in near})
    ffn = group_back(1, act_pieces, wd, ffn)
    act_far = dict(zip(act_far, hold(*act_far.values())))
    for k in far:
        act_pieces[k] = apart(act_far, k)
    tok_sum = rel(tok_sum.finish().reshape(n_z, 3, seq)).transpose(1, 0, 2).reshape(3, rows)
    dlf = router_back(tok_sum[0:2], pf, route_row[2:4])
    m2 = (tok_sum[2:3] + jnp.sum(dlf * lf, axis=0, keepdims=True)) / D
    dlf_inv = (dlf * inv2).astype(BF)
    by_row = lambda n: spec((seq, n), lambda i, sc: (i, 0))
    dy1_low, dh2_own = launch(
        functools.partial(middle_grad_body, n_z),
        jnp.zeros((1,), jnp.int32),
        (n_z,),
        [by_row(dc), by_row(dc), spec((E_F, seq), lambda i, sc: (0, i)), by_row(1), spec((E_F, dc)), spec((1, dc))]
        + [spec((seq, dc))] * n_z,
        [by_row(dc), spec((seq, dc))],
        [jax.ShapeDtypeStruct((rows, dc), BF), jax.ShapeDtypeStruct((seq, dc), F32)],
        us=4,
    )(dy_all, y1_low, dlf_inv, jnp.transpose(m2 * inv2 * inv2), jnp.transpose(rf), gf, *dh2_got)
    dy1_x = core_swap(dy1_low)

    tiles = project(dy1_low, dy1_x, (wo_m, wo_x), 0, 0)
    sent = send_first(tiles)
    keep = project(dy1_low, dy1_x, (wo_m, wo_x), 0, 1)
    if keep[0].shape[0] > 1:
        keep, sent = send_next(keep, sent, 1)

    def att_weight(xt, with_gates, extra, mine, theirs, cols):
        pieces = [v for pair in zip(mine, theirs) for v in pair]
        sc = jnp.concatenate((chip ^ jnp.arange(n_chip, dtype=jnp.int32), core[None]))
        at = lambda i, e, sc: (0, 0, sc[n_chip] ^ i)
        outs = [E_A] + ([2] if extra else [])
        return launch(
            functools.partial(att_weight_body, width, n_chip, with_gates, extra),
            sc,
            (2, E_A),
            [spec(xt.shape), spec((n_z, seq, 2)), spec((n_z, seq, 2))] + [spec((seq, cols))] * len(pieces),
            [spec((dc, n, width), at) for n in outs],
            [jax.ShapeDtypeStruct((dc, n, 2 * width), F32) for n in outs],
            [pltpu.VMEM((n_chip, seq, 2 * width), BF)],
            us=20,
        )(xt, att_route3, pa3, *pieces)

    def stream_t(v):
        return jnp.transpose(v.reshape(n_z, seq, dc), (0, 2, 1))

    ffn = group_back(2, act_pieces, wd, ffn)
    dao_parts = finish_reduce(keep, sent, 2)

    pa_one = lax.dynamic_index_in_dim(pa3, chip, 0, keepdims=False)
    grads, dgate = launch(
        functools.partial(attend_back_body, hc),
        one,
        (1,),
        [spec((half, 2 * width))] * 4
        + [spec((seq, 4 * width)), spec((seq, 2 * width)), spec((seq, 128)), spec((seq, 2))]
        + [spec((seq, 1)), spec((1, seq)), spec((seq, HD)), spec((seq, HD))],
        [spec((seq, 4 * width)), spec((seq, 128))],
        [jax.ShapeDtypeStruct((seq, 4 * width), BF), jax.ShapeDtypeStruct((seq, 128), F32)],
            us=7,
    )(*dao_parts, qkv, ao, lse, pa_one, doc_col, doc_row, cosf, sinf)
    g_m = [grads] + [chip_swap(grads, k) for k in range(1, n_chip)]
    g_t = [core_swap(grads)]
    dpa = jnp.zeros((n_z, 2, seq), F32)
    dpa = lax.dynamic_update_slice(dpa, jnp.transpose(dgate[:, :2])[None], (s_abs, 0, 0))
    dpa = Small(dpa.reshape(n_z * 2, seq), "czx")
    ffn_sent = z_send([ffn[k * seq : (k + 1) * seq].astype(BF) for k in range(n_z)])
    down_grad = group_weight(
        dy_s,
        act_pieces,
        jax.ShapeDtypeStruct((dc, E_F, fl_real), F32),
        spec((dc, E_F, fl_real)),
    )
    ffn = z_total(ffn_sent, y1)[1]
    for _ in range(1 + len(z_bits)):
        dpa.step()
    g_m = [grads] + hold(*g_m[1:])
    dpa.step()
    g_t += [core_swap(v) for v in g_m[1:]]

    def to_rows(v):
        n = v.shape[1] // dc
        v = lax.all_to_all(v.reshape(n_ctx, tok, n * dc), "ctx", 0, 0, tiled=True)
        v = v.reshape(n_ctx, tok, n, dc).transpose(2, 1, 0, 3)
        return v.reshape(n, tok, D)

    buf = jnp.zeros((n_z, seq, dc), BF)
    for k in range(n_chip):
        buf = into_stream(
            functools.partial(att_in_back_body, width),
            k,
            (att_route3,),
            (g_m[k], g_t[k]),
            (wqk_m, wqk_t),
            buf,
            5,
            4 * width,
        )
        if k == 0:
            dpa.finish()
    dpa = lax.dynamic_index_in_dim(dpa.finish().reshape(n_z, 2, seq), f, 0, keepdims=False)
    dh1_sent = z_send([buf[k] for k in range(n_z)])
    query_grad, kv_grad = att_weight(stream_t(h1), False, True, g_m, g_t, 4 * width)
    dh1, _ = z_total(dh1_sent)
    dla = router_back(dpa, pa[:, :seq], route_row[0:2, :seq]).astype(BF)
    dh1 = dh1 + lax.dot_general(dla, ra, (((0,), (1,)), ((), ())), preferred_element_type=F32)
    back_col = jnp.concatenate(((dh1 * ga).astype(BF), dy1_low[:seq]), axis=1)

    back = to_rows(jnp.concatenate((back_col, ffn), axis=1))
    outputs, back = back[2:], back[:2].astype(F32)
    input_grad = back[1] + inv1_loc * (back[0] - n1_loc * jnp.mean(back[0] * n1_loc, axis=1, keepdims=True))
    input_grad = input_grad.astype(BF)[None]

    mark(back_col)
    (output_grad,) = att_weight(stream_t(dy1_low), True, False, ao_m, ao_t, 2 * width)

    own = slice(0, seq)
    tail = jnp.concatenate(
        (
            jnp.dot(dla, h1[own], preferred_element_type=F32),
            jnp.dot(dlf_inv[:, own], yg[own], preferred_element_type=F32),
            jnp.sum(dh1 * n1_own.astype(F32), axis=0, keepdims=True),
            jnp.sum(dh2_own * y1_f, axis=0, keepdims=True),
            jnp.zeros((6, dc), F32),
        ),
        axis=0,
    )
    tail = Small(tail, "z").finish()
    att_router_grad = jnp.transpose(tail[0:E_A])
    ffn_router_grad = jnp.transpose(tail[E_A : E_A + E_F])
    att_gain_grad = tail[E_A + E_F]
    ffn_gain_grad = tail[E_A + E_F + 1]

    return (
        outputs,
        input_grad,
        kv_grad,
        query_grad,
        output_grad,
        att_router_grad,
        att_gain_grad,
        gate_up_grad,
        down_grad,
        ffn_router_grad,
        ffn_gain_grad,
    )


def solution(mesh):
    in_specs = (
        P("fsdp", "ctx", None),
        P("fsdp", "ctx", None),
        P(),
        P("ctx", None, None),
        P("ctx", None, None),
        P("ctx", None, "fsdp"),
        P("ctx", None, "fsdp"),
        P("ctx", None, "fsdp"),
        P("ctx", None),
        P("ctx"),
        P("ctx", None, None, "fsdp"),
        P("ctx", None, "fsdp"),
        P("ctx", None),
        P("ctx"),
    )
    out_specs = (
        P("fsdp", "ctx", None),
        P("fsdp", "ctx", None),
        P("ctx", None, "fsdp"),
        P("ctx", None, "fsdp"),
        P("ctx", None, "fsdp"),
        P("ctx", None),
        P("ctx"),
        P("ctx", None, None, "fsdp"),
        P("ctx", None, "fsdp"),
        P("ctx", None),
        P("ctx"),
    )
    return jax.shard_map(
        per_device, mesh=mesh, in_specs=in_specs, out_specs=out_specs, check_vma=False
    )
```

time: 1360 us -> 934 us (0.69)
  local copies, waits for them, and re-layouts: 232 us -> 103 us
  Pallas kernels: 600 us -> 479 us
  waiting for transfers between devices: 253 us -> 178 us
  other arithmetic: 105 us -> 38 us
    pallas_call x82 -> x79, Pallas kernels: 600 us -> 479 us  [go(): pl.pallas_call(kernel_body, out_shape=out_shape + [jax.ShapeDtypeStruct(v...]
    reshape x5 -> x6, local copies, waits for them, and re-layouts: 80.8 us -> 2.47 us  [the longest x1 0.77 us: per_device(): tok_sum.finish().reshape(n_z, 3, seq)]
    ppermute x117 -> x105, waiting for transfers between devices: 253 us -> 178 us  [swap(): return lax.ppermute(x, axis, [(i, i ^ k) for i in range(n)])]
    convert_element_type x23 -> x3, other arithmetic: 29.2 us -> 2.67 us  [the longest x1 2.4 us: per_device(): h1_x = (n1_t.astype(F32) * ga_t).astype(BF)]
    unnamed x225 -> x315, local copies, waits for them, and re-layouts: 72.8 us -> 49.3 us
    concatenate x13 -> x9, other arithmetic: 27.5 us -> 4.17 us  [the longest x1 1.66 us: per_device(): jnp.concatenate((e_major(query_weight), e_major(kv_weight)), axis=0)]
    ppermute x117 -> x105, starting transfers between devices: 108 us -> 106 us  [swap(): return lax.ppermute(x, axis, [(i, i ^ k) for i in range(n)])]
  transfers between devices with their start and end apart: 120 -> 107, of which waited for: 30 -> 29; matrix products, arithmetic and copies ran while one was open for 24% -> 10% of each run, Pallas kernels for 44% -> 49%
where the time goes in v2:
time: 934 us; the launch traced here: 920 us
  Pallas kernels  479 us (51%)
  waiting for transfers between devices  178 us (19%)
  starting transfers between devices  115 us (12%)
  local copies, waits for them, and re-layouts  103 us (11%)
  other arithmetic  38 us (4%)
    pallas_call x79, Pallas kernels, go(): pl.pallas_call(kernel_body, out_shape=out_shape + [jax.ShapeDtypeStruct(v...  479 us
    ppermute x105, waiting for transfers between devices, swap(): return lax.ppermute(x, axis, [(i, i ^ k) for i in range(n)])  178 us
    ppermute x105, starting transfers between devices, swap(): return lax.ppermute(x, axis, [(i, i ^ k) for i in range(n)])  106 us
    unnamed x315, local copies, waits for them, and re-layouts  49.3 us
  transfers between devices with their start and end apart: 107, of which 29 were waited for; matrix products, arithmetic and copies ran while one was open for 10% of the time, Pallas kernels for 49%

profile of v2, /device:TPU:0, one launch (start us, length us, event | category | flops | bytes accessed | tf_op | source)
XLA Modules:
  0.0 920.4 jit_solution(1479994044160729772)
XLA Ops:
  33.1 26.0 %shard_map.383 = (bf16[8,256,2816]{2,1,0:T(8,128)(2,1)}, bf16[512,256]{1,0:T(8,128)(2,1)}) custom-call(s32[1]{0:T(128)} %constant.81.clone.1.first, f32[256,8,2,1408]{3,2,1,0:T(2,128)} %refs_0_.2, bf16[512,256]{1,0:T(8,128)(2,1)} %get-tuple-element.247.refs_1_, bf16[512,256]{1,0:T(8,128)(2,1)} %get-tuple-element.246.refs_2_), custom_call_target="tpu_custom_call", output_to_operand_aliasing={{1}: (3, {})} | custom-call | flops 28600000512 | tf_op jit(solution)/shard_map/pallas_call | solution.py:64
  67.5 8.8 collective-permute-done.5.refs_2_
  77.8 8.2 collective-permute-done.6.refs_3_
  102.9 7.9 shard_map.386
  120.0 7.9 shard_map.389
  127.9 15.7 %collective-permute-done.12.refs_1_ = bf16[1024,256]{1,0:T(8,128)(2,1)S(1)} collective-permute-done((bf16[1024,256]{1,0:T(8,128)(2,1)}, bf16[1024,256]{1,0:T(8,128)(2,1)S(1)}, u32[]{:S(2)}, u32[]{:S(2)}) %collective-permute-start.12) | collective-permute-done | bytes 524320 | tf_op jit(solution)/shard_map/ppermute | solution.py:564
  154.8 9.4 %shard_map.394.refs_2_.refs_3_.refs_5_ = bf16[8,256,1408]{2,1,0:T(8,128)(2,1)} custom-call(s32[1]{0:T(128)} %constant.81.clone.1.first, f32[256,8,1408]{2,1,0:T(8,128)} %refs_0_.3, bf16[1,256,1024]{2,1,0:T(8,128)(2,1)} %get-tuple-element.107.refs_1_), custom_call_target="tpu_custom_call" | custom-call | flops 10449999872 | tf_op jit(solution)/shard_map/pallas_call | solution.py:64
  185.7 7.2 shard_map.396
  199.5 21.7 %shard_map.399 = (bf16[2,256,1408]{2,1,0:T(8,128)(2,1)}, bf16[2,256,1408]{2,1,0:T(8,128)(2,1)}, bf16[2,256,1408]{2,1,0:T(8,128)(2,1)}, bf16[2,256,1408]{2,1,0:T(8,128)(2,1)}) custom-call(s32[62]{0:T(128)} %bitcast.349, s32[2,2048]{1,0:T(2,128)} %convert_element_type.346.refs_0_, bf16[2048,256]{1,0:T(8,128)(2,1)} %shard_map.390.refs_2_.refs_1_.refs_0_, ...), custom_call_target="tpu_custom_call" | custom-call | flops 29699999744 | tf_op jit(solution)/shard_map/pallas_call | solution.py:64
  256.1 7.6 collective-permute-done.30.refs_1_
  263.7 11.3 %collective-permute-done.31.refs_2_ = bf16[512,256]{1,0:T(8,128)(2,1)S(1)} collective-permute-done((bf16[512,256]{1,0:T(8,128)(2,1)S(1)}, bf16[512,256]{1,0:T(8,128)(2,1)S(1)}, u32[]{:S(2)}, u32[]{:S(2)}) %collective-permute-start.31) | collective-permute-done | bytes 262176 | tf_op jit(solution)/shard_map/ppermute | solution.py:564
  318.1 16.8 %shard_map.412 = (bf16[2,256,2816]{2,1,0:T(8,128)(2,1)}, bf16[2,256,2816]{2,1,0:T(8,128)(2,1)}) custom-call(s32[92]{0:T(128)} %reshape.2244.first, s32[2,2048]{1,0:T(2,128)} %convert_element_type.346.refs_0_, bf16[2048,256]{1,0:T(8,128)(2,1)} %get-tuple-element.129.refs_1_, bf16[2048,256]{1,0:T(8,128)(2,1)} %multiply_convert_fusion.refs_2_, ...), custom_call_target="tpu_custom_call" | custom-call | flops 18699999232 | tf_op jit(solution)/shard_map/pallas_call | solution.py:64
  339.3 15.4 %shard_map.414 = (bf16[2,256,2816]{2,1,0:T(8,128)(2,1)}, bf16[2,256,2816]{2,1,0:T(8,128)(2,1)}) custom-call(s32[92]{0:T(128)} %reshape.2244.first, s32[2,2048]{1,0:T(2,128)} %convert_element_type.346.refs_0_, bf16[2048,256]{1,0:T(8,128)(2,1)} %get-tuple-element.129.refs_1_, bf16[2048,256]{1,0:T(8,128)(2,1)} %multiply_convert_fusion.refs_2_, ...), custom_call_target="tpu_custom_call" | custom-call | flops 18699999232 | tf_op jit(solution)/shard_map/pallas_call | solution.py:64
  357.7 13.0 %shard_map.416.refs_2_.refs_0_ = bf16[256,4096]{1,0:T(8,128)(2,1)} custom-call(s32[16]{0:T(128)} %multiply_add_fusion.2.first, s32[2,2048]{1,0:T(2,128)} %convert_element_type.346.refs_0_, bf16[2048,256]{1,0:T(8,128)(2,1)} %get-tuple-element.129.refs_1_, f32[16,1024]{1,0:T(8,128)} %shard_map.415.refs_2_.refs_0_), custom_call_target="tpu_custom_call" | custom-call | flops 14300000256 | tf_op jit(solution)/shard_map/pallas_call | solution.py:64
  370.6 13.0 %shard_map.417.refs_4_.refs_0_ = bf16[256,4096]{1,0:T(8,128)(2,1)} custom-call(s32[16]{0:T(128)} %multiply_add_fusion.2.first, s32[2,2048]{1,0:T(2,128)} %convert_element_type.346.refs_0_, bf16[2048,256]{1,0:T(8,128)(2,1)} %shard_map.390.refs_2_.refs_1_.refs_0_, bf16[256,4096]{1,0:T(8,128)(2,1)} %shard_map.416.refs_2_.refs_0_), custom_call_target="tpu_custom_call" | custom-call | flops 14300000256 | tf_op jit(solution)/shard_map/pallas_call | solution.py:64
  383.7 15.5 %collective-permute-done.46.refs_1_ = bf16[2,256,2816]{2,1,0:T(8,128)(2,1)S(1)} collective-permute-done((bf16[2,256,2816]{2,1,0:T(8,128)(2,1)}, bf16[2,256,2816]{2,1,0:T(8,128)(2,1)S(1)}, u32[]{:S(2)}, u32[]{:S(2)}) %collective-permute-start.46) | collective-permute-done | bytes 2883616 | tf_op jit(solution)/shard_map/ppermute | solution.py:564
  416.9 21.1 %collective-permute-done.48 = bf16[1,256,2816]{2,1,0:T(8,128)(2,1)S(1)} collective-permute-done((bf16[1,256,2816]{2,1,0:T(8,128)(2,1)}, bf16[1,256,2816]{2,1,0:T(8,128)(2,1)S(1)}, u32[]{:S(2)}, u32[]{:S(2)}) %collective-permute-start.48) | collective-permute-done | bytes 1441824 | tf_op jit(solution)/shard_map/ppermute | solution.py:564
  437.9 8.9 collective-permute-done.49
  446.8 12.4 %shard_map.421 = (bf16[2,256,2816]{2,1,0:T(8,128)(2,1)}, bf16[2,256,1408]{2,1,0:T(8,128)(2,1)}, f32[8,2048]{1,0:T(8,128)}) custom-call(s32[2]{0:T(128)} %pad_add_fusion.5.first, s32[2,2048]{1,0:T(2,128)} %convert_element_type.346.refs_0_, f32[8,2048]{1,0:T(8,128)} %maximum_maximum_fusion.refs_1_, bf16[256,2816]{1,0:T(8,128)(2,1)} %bitcast.355, ...), custom_call_target="tpu_custom_call" | custom-call | flops 14300000256 | tf_op jit(solution)/shard_map/pallas_call | solution.py:64
  474.3 13.0 %shard_map.424.refs_5_.refs_6_ = f32[2048,256]{1,0:T(8,128)} custom-call(s32[46]{0:T(128)} %bitcast.350, s32[2048,2]{1,0:T(8,128)} %bitcast.306, bf16[2,256,2816]{2,1,0:T(8,128)(2,1)} %get-tuple-element.144.refs_2_.refs_1_, bf16[2,256,2816]{2,1,0:T(8,128)(2,1)} %collective-permute-done.54.refs_2_, ...), custom_call_target="tpu_custom_call", output_to_operand_aliasing={{}: (5, {})} | custom-call | flops 14960000000 | tf_op jit(solution)/shard_map/pallas_call | solution.py:64
  488.8 10.8 %shard_map.425.refs_0_.refs_6_ = f32[2048,256]{1,0:T(8,128)} custom-call(s32[46]{0:T(128)} %bitcast.351, s32[2048,2]{1,0:T(8,128)} %bitcast.307, bf16[2,256,1408]{2,1,0:T(8,128)(2,1)} %get-tuple-element.145.refs_1_.refs_8_, bf16[2,256,1408]{2,1,0:T(8,128)(2,1)} %collective-permute-done.53.refs_2_, ...), custom_call_target="tpu_custom_call", output_to_operand_aliasing={{}: (5, {})} | custom-call | flops 12320000000 | tf_op jit(solution)/shard_map/pallas_call | solution.py:64
  499.6 27.8 %collective-permute-done.55.refs_1_ = bf16[2,256,2816]{2,1,0:T(8,128)(2,1)S(1)} collective-permute-done((bf16[2,256,2816]{2,1,0:T(8,128)(2,1)}, bf16[2,256,2816]{2,1,0:T(8,128)(2,1)S(1)}, u32[]{:S(2)}, u32[]{:S(2)}) %collective-permute-start.55) | collective-permute-done | bytes 2883616 | tf_op jit(solution)/shard_map/ppermute | solution.py:564
  545.3 22.8 %shard_map.428 = (f32[2048,256]{1,0:T(8,128)}, bf16[2,256,1408]{2,1,0:T(8,128)(2,1)}) custom-call(s32[62]{0:T(128)} %bitcast.347, s32[2048,2]{1,0:T(8,128)} %bitcast.308, bf16[2,256,2816]{2,1,0:T(8,128)(2,1)} %get-tuple-element.147.refs_1_.refs_3_, ...), custom_call_target="tpu_custom_call", output_to_operand_aliasing={{0}: (7, {}), {1}: (9, {})} | custom-call | flops 29920000000 | tf_op jit(solution)/shard_map/pallas_call | solution.py:64
  583.8 13.6 %shard_map.431.refs_11_ = f32[2048,256]{1,0:T(8,128)} custom-call(s32[46]{0:T(128)} %bitcast.345, s32[2048,2]{1,0:T(8,128)} %bitcast.309, bf16[256,2816]{1,0:T(8,128)(2,1)} %get-tuple-element.150.refs_1_.refs_7_, bf16[256,2816]{1,0:T(8,128)(2,1)} %get-tuple-element.151.refs_2_.refs_8_, ...), custom_call_target="tpu_custom_call", output_to_operand_aliasing={{}: (7, {})} | custom-call | flops 14960000000 | tf_op jit(solution)/shard_map/pallas_call | solution.py:64
  604.2 29.8 %shard_map.432.refs_4_ = f32[256,8,2,1408]{3,2,1,0:T(2,128)} custom-call(s32[25]{0:T(128)} %pad_add_fusion.6.first, bf16[256,4096]{1,0:T(8,128)(2,1)} %shard_map.416.refs_2_.refs_0_, bf16[2,256,2816]{2,1,0:T(8,128)(2,1)} %get-tuple-element.144.refs_2_.refs_1_, bf16[2,256,2816]{2,1,0:T(8,128)(2,1)} %collective-permute-done.54.refs_2_, ...), custom_call_target="tpu_custom_call" | custom-call | flops 32999999488 | tf_op jit(solution)/shard_map/pallas_call | solution.py:64
  645.6 18.3 %shard_map.435.refs_0_.refs_6_ = f32[2048,256]{1,0:T(8,128)} custom-call(s32[62]{0:T(128)} %bitcast.348, s32[2048,2]{1,0:T(8,128)} %bitcast.310, bf16[2,256,1408]{2,1,0:T(8,128)(2,1)} %get-tuple-element.155.refs_1_.refs_3_, bf16[2,256,1408]{2,1,0:T(8,128)(2,1)} %collective-permute-done.70.refs_2_.refs_4_, ...), custom_call_target="tpu_custom_call", output_to_operand_aliasing={{}: (7, {})} | custom-call | flops 24640000000 | tf_op jit(solution)/shard_map/pallas_call | solution.py:64
  674.7 10.6 %collective-permute-done.75.refs_8_ = bf16[512,256]{1,0:T(8,128)(2,1)S(1)} collective-permute-done((bf16[512,256]{1,0:T(8,128)(2,1)S(1)}, bf16[512,256]{1,0:T(8,128)(2,1)S(1)}, u32[]{:S(2)}, u32[]{:S(2)}) %collective-permute-start.75) | collective-permute-done | bytes 262176 | tf_op jit(solution)/shard_map/ppermute | solution.py:564
  727.5 11.6 %shard_map.443.refs_12_ = f32[2048,256]{1,0:T(8,128)} custom-call(s32[46]{0:T(128)} %bitcast.346, s32[2048,2]{1,0:T(8,128)} %bitcast.311, bf16[256,1408]{1,0:T(8,128)(2,1)} %get-tuple-element.170.refs_1_.refs_7_, bf16[256,1408]{1,0:T(8,128)(2,1)} %get-tuple-element.171.refs_2_.refs_8_, bf16[256,1408]{1,0:T(8,128)(2,1)} %copy-done.99, ...), custom_call_target="tpu_custom_call", output_to_operand_aliasing={{}: (7, {})} | custom-call | flops 12320000000 | tf_op jit(solution)/shard_map/pallas_call | solution.py:64
  746.7 7.2 shard_map.444
  757.4 24.3 %shard_map.445.refs_5_ = f32[256,8,1408]{2,1,0:T(8,128)} custom-call(s32[25]{0:T(128)} %pad_add_fusion.6.first, bf16[256,4096]{1,0:T(8,128)(2,1)} %shard_map.417.refs_4_.refs_0_, bf16[2,256,1408]{2,1,0:T(8,128)(2,1)} %get-tuple-element.154.refs_1_, bf16[2,256,1408]{2,1,0:T(8,128)(2,1)} %collective-permute-done.53.refs_2_, ...), custom_call_target="tpu_custom_call" | custom-call | flops 26400000000 | tf_op jit(solution)/shard_map/pallas_call | solution.py:64
  849.4 21.3 %shard_map.457 = (f32[256,8,512]{2,1,0:T(8,128)}, f32[256,2,512]{2,1,0:T(2,128)}) custom-call(s32[5]{0:T(128)} %pad_add_fusion.7.first, bf16[4,256,512]{2,1,0:T(8,128)(2,1)} %bitcast.312, s32[4,512,2]{2,1,0:T(8,128)} %bitcast.281, f32[4,512,2]{2,1,0:T(8,128)} %bitcast.303, bf16[512,1024]{1,0:T(8,128)(2,1)} %get-tuple-element.173.refs_11_.refs_1_.refs_3_, ...), custom_call_target="tpu_custom_call" | custom-call | flops 22000001024 | tf_op jit(solution)/shard_map/pallas_call | solution.py:64
  883.9 18.7 %shard_map.459.refs_2_ = f32[256,8,512]{2,1,0:T(8,128)} custom-call(s32[5]{0:T(128)} %pad_add_fusion.7.first, bf16[4,256,512]{2,1,0:T(8,128)(2,1)} %bitcast.313, s32[4,512,2]{2,1,0:T(8,128)} %bitcast.282, f32[4,512,2]{2,1,0:T(8,128)} %bitcast.304, bf16[512,512]{1,0:T(8,128)(2,1)} %get-tuple-element.113.refs_2_.refs_5_.refs_3_, bf16[512,512]{1,0:T(8,128)(2,1)} %copy-done.101, ...), custom_call_target="tpu_custom_call" | custom-call | flops 22000001024 | tf_op jit(solution)/shard_map/pallas_call | solution.py:64
  (797 shorter events, 440.1 us)
Async XLA Ops:
  13.6 53.6 %collective-permute-start.10 = (bf16[2,256]{1,0:T(2,128)(2,1)S(1)}, bf16[2,256]{1,0:T(2,128)(2,1)S(1)}, u32[]{:S(2)}, u32[]{:S(2)}) collective-permute-start(bf16[2,256]{1,0:T(2,128)(2,1)S(1)} %pad_maximum_fusion.4), channel_id=1, source_target_pairs={{0,4},{4,0},{8,12},{12,8},{16,20},{20,16},{24,28},{28,24},{1,5},{5... | collective-permute-start | bytes 3080 | tf_op jit(solution)/shard_map/ppermute | solution.py:564
  14.2 47.1 %collective-permute-start = (s32[1,64,4,4]{1,3,2,0:T(4,128)S(1)}, s32[1,64,4,4]{1,3,2,0:T(4,128)S(1)}, u32[]{:S(2)}, u32[]{:S(2)}) collective-permute-start(s32[1,64,4,4]{1,3,2,0:T(4,128)S(1)} %add_bitcast_fusion), channel_id=1, source_target_pairs={{0,4},{4,0},{8,12},{12,8},{16,20},{20,16},{24,28},{28,24},{1,5},{5... | collective-permute-start | bytes 12296 | tf_op jit(solution)/shard_map/ppermute | solution.py:564
  59.1 137.4 %collective-permute-start.22 = (bf16[8,256,2816]{2,1,0:T(8,128)(2,1)}, bf16[8,256,2816]{2,1,0:T(8,128)(2,1)}, u32[]{:S(2)}, u32[]{:S(2)}) collective-permute-start(bf16[8,256,2816]{2,1,0:T(8,128)(2,1)} %get-tuple-element.99.refs_5_.refs_3_), channel_id=1, source_target_pairs={{0,4},{4,0},{8,12},{12,8},{16,20},{20,16},{24,28},{28,24},{1,5},{5... | collective-permute-start | bytes 34603016 | tf_op jit(solution)/shard_map/ppermute | solution.py:564
  67.5 35.4 %collective-permute-start.11 = (bf16[10,256,256]{2,1,0:T(8,128)(2,1)}, bf16[10,256,256]{2,1,0:T(8,128)(2,1)}, u32[]{:S(2)}, u32[]{:S(2)}) collective-permute-start(bf16[10,256,256]{2,1,0:T(8,128)(2,1)} %get-tuple-element.221.refs_4_), channel_id=1, source_target_pairs={{0,4},{4,0},{8,12},{12,8},{16,20},{20,16},{24,28},{28,24},{1,5},{5... | collective-permute-start | bytes 3932168 | tf_op jit(solution)/shard_map/ppermute | solution.py:564
  110.8 37.8 %collective-permute-start.15 = (bf16[2,256,1024]{2,1,0:T(8,128)(2,1)}, bf16[2,256,1024]{2,1,0:T(8,128)(2,1)S(1)}, u32[]{:S(2)}, u32[]{:S(2)}) collective-permute-start(bf16[2,256,1024]{2,1,0:T(8,128)(2,1)} %get-tuple-element.102.refs_2_), channel_id=1, source_target_pairs={{0,8},{4,12},{8,0},{12,4},{16,24},{20,28},{24,16},{28,20},{1,9},{5... | collective-permute-start | bytes 3145736 | tf_op jit(solution)/shard_map/ppermute | solution.py:564
  114.4 32.3 %collective-permute-start.13 = (f32[8,512]{1,0:T(8,128)}, f32[8,512]{1,0:T(8,128)S(1)}, u32[]{:S(2)}, u32[]{:S(2)}) collective-permute-start(f32[8,512]{1,0:T(8,128)} %shard_map.387.refs_2_.refs_0_), channel_id=1, source_target_pairs={{0,16},{4,20},{8,24},{12,28},{16,0},{20,4},{24,8},{28,12},{1,17},{... | collective-permute-start | bytes 49160 | tf_op jit(solution)/shard_map/ppermute | solution.py:564
  115.8 32.8 %collective-permute-start.16 = (bf16[2,256,1024]{2,1,0:T(8,128)(2,1)}, bf16[2,256,1024]{2,1,0:T(8,128)(2,1)}, u32[]{:S(2)}, u32[]{:S(2)}) collective-permute-start(bf16[2,256,1024]{2,1,0:T(8,128)(2,1)} %get-tuple-element.105), channel_id=1, source_target_pairs={{0,16},{4,20},{8,24},{12,28},{16,0},{20,4},{24,8},{28,12},{1,17},{... | collective-permute-start | bytes 3145736 | tf_op jit(solution)/shard_map/ppermute | solution.py:564
  164.2 35.3 %collective-permute-start.21 = (bf16[8,256,1408]{2,1,0:T(8,128)(2,1)}, bf16[8,256,1408]{2,1,0:T(8,128)(2,1)}, u32[]{:S(2)}, u32[]{:S(2)}) collective-permute-start(bf16[8,256,1408]{2,1,0:T(8,128)(2,1)} %shard_map.394.refs_2_.refs_3_.refs_5_), channel_id=1, source_target_pairs={{0,4},{4,0},{8,12},{12,8},{16,20},{20,16},{24,28},{28,24},{1,5},{5... | collective-permute-start | bytes 17301512 | tf_op jit(solution)/shard_map/ppermute | solution.py:564
  247.2 39.4 %collective-permute-start.37 = (bf16[2,256,1408]{2,1,0:T(8,128)(2,1)}, bf16[2,256,1408]{2,1,0:T(8,128)(2,1)S(1)}, u32[]{:S(2)}, u32[]{:S(2)}) collective-permute-start(bf16[2,256,1408]{2,1,0:T(8,128)(2,1)} %get-tuple-element.122), channel_id=1, source_target_pairs={{0,8},{4,12},{8,0},{12,4},{16,24},{20,28},{24,16},{28,20},{1,9},{5... | collective-permute-start | bytes 4325384 | tf_op jit(solution)/shard_map/ppermute | solution.py:564
  247.8 38.9 %collective-permute-start.38 = (bf16[2,256,1408]{2,1,0:T(8,128)(2,1)}, bf16[2,256,1408]{2,1,0:T(8,128)(2,1)}, u32[]{:S(2)}, u32[]{:S(2)}) collective-permute-start(bf16[2,256,1408]{2,1,0:T(8,128)(2,1)} %get-tuple-element.124), channel_id=1, source_target_pairs={{0,16},{4,20},{8,24},{12,28},{16,0},{20,4},{24,8},{28,12},{1,17},{... | collective-permute-start | bytes 4325384 | tf_op jit(solution)/shard_map/ppermute | solution.py:564
  315.8 39.0 %collective-permute-start.41 = (f32[16,512]{1,0:T(8,128)S(1)}, f32[16,512]{1,0:T(8,128)S(1)}, u32[]{:S(2)}, u32[]{:S(2)}) collective-permute-start(f32[16,512]{1,0:T(8,128)S(1)} %copy-done.124), channel_id=1, source_target_pairs={{0,1},{1,0},{2,3},{3,2},{4,5},{5,4},{6,7},{7,6},{8,9},{9,8},{10,11... | collective-permute-start | bytes 98312 | tf_op jit(solution)/shard_map/ppermute | solution.py:564
  334.9 64.3 %collective-permute-start.46 = (bf16[2,256,2816]{2,1,0:T(8,128)(2,1)}, bf16[2,256,2816]{2,1,0:T(8,128)(2,1)S(1)}, u32[]{:S(2)}, u32[]{:S(2)}) collective-permute-start(bf16[2,256,2816]{2,1,0:T(8,128)(2,1)} %get-tuple-element.133.refs_4_), channel_id=1, source_target_pairs={{0,8},{4,12},{8,0},{12,4},{16,24},{20,28},{24,16},{28,20},{1,9},{5... | collective-permute-start | bytes 8650760 | tf_op jit(solution)/shard_map/ppermute | solution.py:564
  334.9 64.6 %collective-permute-start.47 = (bf16[2,256,2816]{2,1,0:T(8,128)(2,1)}, bf16[2,256,2816]{2,1,0:T(8,128)(2,1)}, u32[]{:S(2)}, u32[]{:S(2)}) collective-permute-start(bf16[2,256,2816]{2,1,0:T(8,128)(2,1)} %get-tuple-element.137), channel_id=1, source_target_pairs={{0,16},{4,20},{8,24},{12,28},{16,0},{20,4},{24,8},{28,12},{1,17},{... | collective-permute-start | bytes 8650760 | tf_op jit(solution)/shard_map/ppermute | solution.py:564
  356.8 54.6 %collective-permute-start.45 = (f32[16,1024]{1,0:T(8,128)}, f32[16,1024]{1,0:T(8,128)S(1)}, u32[]{:S(2)}, u32[]{:S(2)}) collective-permute-start(f32[16,1024]{1,0:T(8,128)} %shard_map.415.refs_2_.refs_0_), channel_id=1, source_target_pairs={{0,2},{1,3},{2,0},{3,1},{4,6},{5,7},{6,4},{7,5},{8,10},{9,11},{10,... | collective-permute-start | bytes 196616 | tf_op jit(solution)/shard_map/ppermute | solution.py:564
  405.3 32.6 %collective-permute-start.48 = (bf16[1,256,2816]{2,1,0:T(8,128)(2,1)}, bf16[1,256,2816]{2,1,0:T(8,128)(2,1)S(1)}, u32[]{:S(2)}, u32[]{:S(2)}) collective-permute-start(bf16[1,256,2816]{2,1,0:T(8,128)(2,1)} %get-tuple-element.138.refs_4_), channel_id=1, source_target_pairs={{0,16},{4,20},{8,24},{12,28},{16,0},{20,4},{24,8},{28,12},{1,17},{... | collective-permute-start | bytes 4325384 | tf_op jit(solution)/shard_map/ppermute | solution.py:564
  414.5 32.3 %collective-permute-start.49 = (bf16[1,256,2816]{2,1,0:T(8,128)(2,1)S(1)}, bf16[1,256,2816]{2,1,0:T(8,128)(2,1)}, u32[]{:S(2)}, u32[]{:S(2)}) collective-permute-start(bf16[1,256,2816]{2,1,0:T(8,128)(2,1)S(1)} %copy-done.96), channel_id=1, source_target_pairs={{0,8},{4,12},{8,0},{12,4},{16,24},{20,28},{24,16},{28,20},{1,9},{5... | collective-permute-start | bytes 4325384 | tf_op jit(solution)/shard_map/ppermute | solution.py:564
  462.8 64.6 %collective-permute-start.55 = (bf16[2,256,2816]{2,1,0:T(8,128)(2,1)}, bf16[2,256,2816]{2,1,0:T(8,128)(2,1)S(1)}, u32[]{:S(2)}, u32[]{:S(2)}) collective-permute-start(bf16[2,256,2816]{2,1,0:T(8,128)(2,1)} %get-tuple-element.144.refs_2_.refs_1_), channel_id=1, source_target_pairs={{0,8},{4,12},{8,0},{12,4},{16,24},{20,28},{24,16},{28,20},{1,9},{5... | collective-permute-start | bytes 8650760 | tf_op jit(solution)/shard_map/ppermute | solution.py:564
  464.0 64.5 %collective-permute-start.56 = (bf16[2,256,2816]{2,1,0:T(8,128)(2,1)}, bf16[2,256,2816]{2,1,0:T(8,128)(2,1)}, u32[]{:S(2)}, u32[]{:S(2)}) collective-permute-start(bf16[2,256,2816]{2,1,0:T(8,128)(2,1)} %get-tuple-element.144.refs_2_.refs_1_), channel_id=1, source_target_pairs={{0,16},{4,20},{8,24},{12,28},{16,0},{20,4},{24,8},{28,12},{1,17},{... | collective-permute-start | bytes 8650760 | tf_op jit(solution)/shard_map/ppermute | solution.py:564
  541.2 32.3 %collective-permute-start.61 = (bf16[256,2816]{1,0:T(8,128)(2,1)}, bf16[256,2816]{1,0:T(8,128)(2,1)S(1)}, u32[]{:S(2)}, u32[]{:S(2)}) collective-permute-start(bf16[256,2816]{1,0:T(8,128)(2,1)} %slice_bitcast_fusion.1), channel_id=1, source_target_pairs={{0,16},{4,20},{8,24},{12,28},{16,0},{20,4},{24,8},{28,12},{1,17},{... | collective-permute-start | bytes 4325384 | tf_op jit(solution)/shard_map/ppermute | solution.py:564
  581.2 55.8 %collective-permute-start.68 = (bf16[2,256,1408]{2,1,0:T(8,128)(2,1)}, bf16[2,256,1408]{2,1,0:T(8,128)(2,1)S(1)}, u32[]{:S(2)}, u32[]{:S(2)}) collective-permute-start(bf16[2,256,1408]{2,1,0:T(8,128)(2,1)} %get-tuple-element.154.refs_1_), channel_id=1, source_target_pairs={{0,8},{4,12},{8,0},{12,4},{16,24},{20,28},{24,16},{28,20},{1,9},{5... | collective-permute-start | bytes 4325384 | tf_op jit(solution)/shard_map/ppermute | solution.py:564
  582.0 55.0 %collective-permute-start.69 = (bf16[2,256,1408]{2,1,0:T(8,128)(2,1)}, bf16[2,256,1408]{2,1,0:T(8,128)(2,1)S(1)}, u32[]{:S(2)}, u32[]{:S(2)}) collective-permute-start(bf16[2,256,1408]{2,1,0:T(8,128)(2,1)} %get-tuple-element.154.refs_1_), channel_id=1, source_target_pairs={{0,16},{4,20},{8,24},{12,28},{16,0},{20,4},{24,8},{28,12},{1,17},{... | collective-permute-start | bytes 4325384 | tf_op jit(solution)/shard_map/ppermute | solution.py:564
  599.8 34.2 %collective-permute-start.65 = (bf16[512,256]{1,0:T(8,128)(2,1)S(1)}, bf16[512,256]{1,0:T(8,128)(2,1)S(1)}, u32[]{:S(2)}, u32[]{:S(2)}) collective-permute-start(bf16[512,256]{1,0:T(8,128)(2,1)S(1)} %get-tuple-element.237), channel_id=1, source_target_pairs={{0,1},{1,0},{2,3},{3,2},{4,5},{5,4},{6,7},{7,6},{8,9},{9,8},{10,11... | collective-permute-start | bytes 786440 | tf_op jit(solution)/shard_map/ppermute | solution.py:564
  600.7 33.3 %collective-permute-start.66 = (bf16[512,256]{1,0:T(8,128)(2,1)S(1)}, bf16[512,256]{1,0:T(8,128)(2,1)}, u32[]{:S(2)}, u32[]{:S(2)}) collective-permute-start(bf16[512,256]{1,0:T(8,128)(2,1)S(1)} %get-tuple-element.236), channel_id=1, source_target_pairs={{0,2},{1,3},{2,0},{3,1},{4,6},{5,7},{6,4},{7,5},{8,10},{9,11},{10,... | collective-permute-start | bytes 786440 | tf_op jit(solution)/shard_map/ppermute | solution.py:564
  601.8 32.2 %collective-permute-start.67 = (bf16[512,256]{1,0:T(8,128)(2,1)S(1)}, bf16[512,256]{1,0:T(8,128)(2,1)}, u32[]{:S(2)}, u32[]{:S(2)}) collective-permute-start(bf16[512,256]{1,0:T(8,128)(2,1)S(1)} %get-tuple-element.235), channel_id=1, source_target_pairs={{0,3},{1,2},{2,1},{3,0},{4,7},{5,6},{6,5},{7,4},{8,11},{9,10},{10,... | collective-permute-start | bytes 786440 | tf_op jit(solution)/shard_map/ppermute | solution.py:564
  639.6 57.9 %collective-permute-start.78 = (bf16[8,256,256]{2,1,0:T(8,128)(2,1)}, bf16[8,256,256]{2,1,0:T(8,128)(2,1)}, u32[]{:S(2)}, u32[]{:S(2)}) collective-permute-start(bf16[8,256,256]{2,1,0:T(8,128)(2,1)} %get-tuple-element.223.refs_5_), channel_id=1, source_target_pairs={{0,4},{4,0},{8,12},{12,8},{16,20},{20,16},{24,28},{28,24},{1,5},{5... | collective-permute-start | bytes 3145736 | tf_op jit(solution)/shard_map/ppermute | solution.py:564
  741.6 40.1 %collective-permute-start.86 = (bf16[512,256]{1,0:T(8,128)(2,1)S(1)}, bf16[512,256]{1,0:T(8,128)(2,1)S(1)}, u32[]{:S(2)}, u32[]{:S(2)}) collective-permute-start(bf16[512,256]{1,0:T(8,128)(2,1)S(1)} %get-tuple-element.233), channel_id=1, source_target_pairs={{0,1},{1,0},{2,3},{3,2},{4,5},{5,4},{6,7},{7,6},{8,9},{9,8},{10,11... | collective-permute-start | bytes 786440 | tf_op jit(solution)/shard_map/ppermute | solution.py:564
  745.9 38.3 %collective-permute-start.87 = (bf16[512,256]{1,0:T(8,128)(2,1)S(1)}, bf16[512,256]{1,0:T(8,128)(2,1)S(1)}, u32[]{:S(2)}, u32[]{:S(2)}) collective-permute-start(bf16[512,256]{1,0:T(8,128)(2,1)S(1)} %get-tuple-element.232), channel_id=1, source_target_pairs={{0,2},{1,3},{2,0},{3,1},{4,6},{5,7},{6,4},{7,5},{8,10},{9,11},{10,... | collective-permute-start | bytes 786440 | tf_op jit(solution)/shard_map/ppermute | solution.py:564
  753.9 58.2 %collective-permute-start.91 = (bf16[512,1024]{1,0:T(8,128)(2,1)}, bf16[512,1024]{1,0:T(8,128)(2,1)S(1)}, u32[]{:S(2)}, u32[]{:S(2)}) collective-permute-start(bf16[512,1024]{1,0:T(8,128)(2,1)} %get-tuple-element.173.refs_11_.refs_1_.refs_3_), channel_id=1, source_target_pairs={{0,8},{4,12},{8,0},{12,4},{16,24},{20,28},{24,16},{28,20},{1,9},{5... | collective-permute-start | bytes 3145736 | tf_op jit(solution)/shard_map/ppermute | solution.py:564
  755.0 57.2 %collective-permute-start.92 = (bf16[512,1024]{1,0:T(8,128)(2,1)}, bf16[512,1024]{1,0:T(8,128)(2,1)}, u32[]{:S(2)}, u32[]{:S(2)}) collective-permute-start(bf16[512,1024]{1,0:T(8,128)(2,1)} %get-tuple-element.173.refs_11_.refs_1_.refs_3_), channel_id=1, source_target_pairs={{0,16},{4,20},{8,24},{12,28},{16,0},{20,4},{24,8},{28,12},{1,17},{... | collective-permute-start | bytes 3145736 | tf_op jit(solution)/shard_map/ppermute | solution.py:564
  755.0 57.2 %collective-permute-start.93 = (bf16[512,1024]{1,0:T(8,128)(2,1)}, bf16[512,1024]{1,0:T(8,128)(2,1)}, u32[]{:S(2)}, u32[]{:S(2)}) collective-permute-start(bf16[512,1024]{1,0:T(8,128)(2,1)} %get-tuple-element.173.refs_11_.refs_1_.refs_3_), channel_id=1, source_target_pairs={{0,24},{4,28},{8,16},{12,20},{16,8},{20,12},{24,0},{28,4},{1,25},{... | collective-permute-start | bytes 3145736 | tf_op jit(solution)/shard_map/ppermute | solution.py:564
  784.2 34.0 %collective-permute-start.97 = (bf16[512,1024]{1,0:T(8,128)(2,1)}, bf16[512,1024]{1,0:T(8,128)(2,1)}, u32[]{:S(2)}, u32[]{:S(2)}) collective-permute-start(bf16[512,1024]{1,0:T(8,128)(2,1)} %get-tuple-element.173.refs_11_.refs_1_.refs_3_), channel_id=1, source_target_pairs={{0,4},{4,0},{8,12},{12,8},{16,20},{20,16},{24,28},{28,24},{1,5},{5... | collective-permute-start | bytes 3145736 | tf_op jit(solution)/shard_map/ppermute | solution.py:564
  880.1 34.0 %all-to-all-start.1 = ((bf16[8,64,768]{2,1,0:T(8,128)(2,1)}), bf16[8,64,768]{2,1,0:T(8,128)(2,1)S(1)}, u32[]{:S(2)}, u32[]{:S(2)}) async-start(bf16[8,64,768]{2,1,0:T(8,128)(2,1)} %bitcast.125), calls=%async_computation.1 | async-start | bytes 1572864 | tf_op jit(solution)/shard_map/all_to_all | solution.py:1238
  (227 other events, 2555.0 us)

commit v3 on v2

--- a/solution.py
+++ b/solution.py
@@ -597,6 +597,20 @@
         chain.extend(values)
 
     one = jnp.zeros((1,), jnp.int32)
+    always = doc_lengths[0, 0] > 0
+
+    def window(work, *args):
+        outer = list(chain)
+
+        def inside(tokens, args):
+            chain[:] = tokens
+            return work(*args)
+
+        shapes = jax.eval_shape(inside, outer, args)
+        nothing = lambda tokens, args: jax.tree.map(lambda v: jnp.zeros(v.shape, v.dtype), shapes)
+        out = lax.cond(always, inside, nothing, outer, args)
+        chain[:] = jax.tree.leaves(out)[:1]
+        return out
 
     def hold(*vals):
         out = launch(
@@ -724,31 +738,31 @@
     dy_loc = cotangent[0].astype(F32) * my_keep
     payload = jnp.stack((n1_loc.astype(BF), dy_loc.astype(BF), inputs[0]), axis=1)
     payload = payload.reshape(tok, 3, n_ctx, dc).transpose(2, 0, 1, 3).reshape(n_ctx, tok, 3 * dc)
+    def split_halves(w):
+        mine = lax.dynamic_slice_in_dim(w, core * width, width, 2)
+        theirs = lax.dynamic_slice_in_dim(w, (1 - core) * width, width, 2)
+        return mine, theirs, core_swap(theirs)
+
+    def e_major(w):
+        return jnp.transpose(w.astype(BF), (1, 0, 2))
+
     payload = lax.all_to_all(payload, "ctx", 0, 0, tiled=True).reshape(seq, 3 * dc)
-    n1_own, dy_own, x_own = payload[:, :dc], payload[:, dc : 2 * dc], payload[:, 2 * dc :]
-
+    qk_weight = jnp.concatenate((e_major(query_weight), e_major(kv_weight)), axis=0)
     routes = jnp.concatenate((att_routes, ffn_routes), axis=2)[None]
     for b in [1] + [2 * v for v in chip_bits]:
         routes = jnp.concatenate((routes, swap(routes, "ctx", b, n_ctx)), axis=0)
     routes = jnp.take(routes, c ^ jnp.arange(n_ctx, dtype=jnp.int32), axis=0).reshape(seq, n_z, 4)
+    small = jnp.concatenate((att_gain[None], ffn_gain[None]), axis=0).astype(BF)
+    small_t = core_swap(small).astype(F32)
+    small = small.astype(F32)
+    wqk_m, wqk_t, wqk_x = split_halves(qk_weight)
+    n1_own, dy_own, x_own = payload[:, :dc], payload[:, dc : 2 * dc], payload[:, 2 * dc :]
+
     routes = rel(jnp.transpose(routes, (1, 0, 2))).reshape(rows, 4)
     route_row = jnp.transpose(routes)
     att_route3 = routes[:, :2].reshape(n_z, seq, 2)
     experts = jnp.arange(E_F, dtype=jnp.int32)
 
-    def split_halves(w):
-        mine = lax.dynamic_slice_in_dim(w, core * width, width, 2)
-        theirs = lax.dynamic_slice_in_dim(w, (1 - core) * width, width, 2)
-        return mine, theirs, core_swap(theirs)
-
-    def e_major(w):
-        return jnp.transpose(w.astype(BF), (1, 0, 2))
-
-    qk_weight = jnp.concatenate((e_major(query_weight), e_major(kv_weight)), axis=0)
-    wqk_m, wqk_t, wqk_x = split_halves(qk_weight)
-    small = jnp.concatenate((att_gain[None], ffn_gain[None]), axis=0)
-    small_t = core_swap(small.astype(BF)).astype(F32)
-    small = small.astype(BF).astype(F32)
     ga, gf, ga_t, gf_t = small[0:1], small[1:2], small_t[0:1], small_t[1:2]
     ra, rf = att_router.astype(BF), ffn_router.astype(BF)
 
@@ -759,24 +773,28 @@
         picked = jnp.sum(jnp.where(route2[:, None, :] == experts[None, :, None], logits[None], 0.0), axis=1)
         return jax.nn.softmax(picked, axis=0)
 
-    n1 = z_gather(n1_own)
     la = Small(row_logits(ra, (n1_own.astype(F32) * ga).astype(BF)), "cxg")
     step = 32
-    mark(n1_own)
-    wg, dy_own = launch(
-        functools.partial(prep_gate_up_body, fl),
-        jnp.zeros((1,), jnp.int32),
-        (dc // step,),
-        [spec((step, E_F, 2, fl_real), lambda i, sc: (i, 0, 0, 0))],
-        spec((E_F, step, 2 * fl), lambda i, sc: (0, i, 0)),
-        jax.ShapeDtypeStruct((E_F, dc, 2 * fl), BF),
+
+    def first_window(n1_own, dy_own, gate_up_weight):
+        n1 = z_gather(n1_own)
+        dy_got = z_swap(dy_own, z_bits[0])
+        wg = launch(
+            functools.partial(prep_gate_up_body, fl),
+            jnp.zeros((1,), jnp.int32),
+            (dc // step,),
+            [spec((step, E_F, 2, fl_real), lambda i, sc: (i, 0, 0, 0))],
+            spec((E_F, step, 2 * fl), lambda i, sc: (0, i, 0)),
+            jax.ShapeDtypeStruct((E_F, dc, 2 * fl), BF),
             us=26,
-    )(gate_up_weight, carry=(dy_own,))
-    n1, h1 = join_scaled(n1, ga)
+        )(gate_up_weight)
+        n1, h1 = join_scaled(n1, ga)
+        return n1, h1, join([dy_own, dy_got], 0), wg
+
+    mark(routes, wqk_x, small_t)
+    n1, h1, dy, wg = window(first_window, n1_own, dy_own, gate_up_weight)
     n1_t = core_swap(n1)
     wg_x = core_swap(wg)
-    dy = dy_own
-    dy_got = z_swap(dy, z_bits[0])
     h1_x = (n1_t.astype(F32) * ga_t).astype(BF)
     def project(xo, xt, weights, n_extra, g):
         cols = (2 + n_extra) * width
@@ -808,39 +826,10 @@
     la.step()
     tiles = project(h1, h1_x, (wqk_m, wqk_x), 2, 0)
     la.step()
-    sent = send_first(tiles)
-    dy = join([dy, dy_got], 0)
-    dy_got = z_swap(dy, z_bits[1])
-    keep = project(h1, h1_x, (wqk_m, wqk_x), 2, 1)
-    for b in z_bits[2:]:
-        dy = join([dy, dy_got], 0)
-        dy_got = z_swap(dy, b)
-    dy_all = join([dy, dy_got], 0)
-    la.step()
-
-    hot = (route_row[2:4, None, :] == experts[None, :, None]).astype(F32)
-    blocks = rows // 128
-    hot_b = hot.reshape(2 * E_F, blocks, 128)
-    lane = jnp.arange(128)
-    tri = (lane[:, None] < lane[None, :]).astype(BF)
-    before = jnp.einsum("anl,lm->anm", hot_b.astype(BF), tri, preferred_element_type=F32)
-    totals = jnp.sum(hot_b, axis=2)
-    lane_b = jnp.arange(blocks)
-    tri_b = (lane_b[:, None] < lane_b[None, :]).astype(BF)
-    before_b = jnp.dot(totals.astype(BF), tri_b, preferred_element_type=F32)
-    rank = (before + before_b[:, :, None]).reshape(2, E_F, rows)
-    counts = jnp.sum(totals, axis=1).reshape(2, E_F)
-    per_expert = counts[0] + counts[1]
-    off = jnp.sum(jnp.where(experts[:, None] > experts[None, :], per_expert[None, :], 0.0), axis=1)
-    base = jnp.stack((off, off + counts[0]))
-    pos_row = jnp.sum(hot * (base[:, :, None] + rank), axis=1).astype(jnp.int32)
-    pos_col = jnp.transpose(pos_row)
-    offsets = jnp.concatenate((off, jnp.sum(per_expert)[None])).astype(jnp.int32)
-
     def start_of(k, other, h):
         return 2 * ts * (2 * (chip ^ k) + (core ^ other)) + h * ts
 
-    def tile_scalars(table):
+    def tile_scalars(table, offsets):
         ks, others, hs = (jnp.array([[t[i] for t in row] for row in table], jnp.int32) for i in range(3))
         p0 = start_of(ks, others, hs)
         n = p0.shape[1]
@@ -860,14 +849,41 @@
         ends = jnp.broadcast_to(offsets, (len(table), E_F + 1))
         return jnp.concatenate((p0, tile, e, kind, ends), axis=1).astype(jnp.int32)
 
-    proj_scalars = tile_scalars([[(k, 0, h) for k, h in group] for group in groups[:2]])
-    all_scalars = tile_scalars([[(k, 0, h) for k, h in groups[2]]]).reshape(-1)
+    near = list(chip_bits)
+    far = [k for k in range(1, n_chip) if k not in near]
+    back_groups = ([0], near, far)
     back_table = [[(k, other, h) for other in range(2) for h in range(2)] for k in range(n_chip)]
     n_pieces = 4 * n_chip
-    starts_all = start_of(*(jnp.array([t[i] for row in back_table for t in row], jnp.int32) for i in range(3)))
-    weight_scalars = jnp.concatenate((starts_all, offsets))
-    proj_length = proj_scalars.shape[1]
-    proj_scalars = proj_scalars.reshape(-1)
+    def places():
+        hot = (route_row[2:4, None, :] == experts[None, :, None]).astype(F32)
+        blocks = rows // 128
+        hot_b = hot.reshape(2 * E_F, blocks, 128)
+        lane = jnp.arange(128)
+        tri = (lane[:, None] < lane[None, :]).astype(BF)
+        before = jnp.einsum("anl,lm->anm", hot_b.astype(BF), tri, preferred_element_type=F32)
+        totals = jnp.sum(hot_b, axis=2)
+        lane_b = jnp.arange(blocks)
+        tri_b = (lane_b[:, None] < lane_b[None, :]).astype(BF)
+        before_b = jnp.dot(totals.astype(BF), tri_b, preferred_element_type=F32)
+        rank = (before + before_b[:, :, None]).reshape(2, E_F, rows)
+        counts = jnp.sum(totals, axis=1).reshape(2, E_F)
+        per_expert = counts[0] + counts[1]
+        off = jnp.sum(jnp.where(experts[:, None] > experts[None, :], per_expert[None, :], 0.0), axis=1)
+        base = jnp.stack((off, off + counts[0]))
+        pos_row = jnp.sum(hot * (base[:, :, None] + rank), axis=1).astype(jnp.int32)
+        pos_col = jnp.transpose(pos_row)
+        offsets = jnp.concatenate((off, jnp.sum(per_expert)[None])).astype(jnp.int32)
+        proj_scalars = tile_scalars([[(k, 0, h) for k, h in group] for group in groups[:2]], offsets)
+        all_scalars = tile_scalars([[(k, 0, h) for k, h in groups[2]]], offsets).reshape(-1)
+        starts_all = start_of(*(jnp.array([t[i] for row in back_table for t in row], jnp.int32) for i in range(3)))
+        weight_scalars = jnp.concatenate((starts_all, offsets))
+        back_scalars = [
+            tile_scalars([[t for k in ks for t in back_table[k]]], offsets).reshape(-1) for ks in back_groups
+        ]
+        return pos_row, pos_col, proj_scalars.reshape(-1), all_scalars, back_scalars, starts_all, weight_scalars
+
+    n_tile = len(groups[0])
+    proj_length = 4 * n_tile + 3 * (E_F - 1) + E_F + 1
 
     def group_proj(xo, xt, wm, wx, g):
         m = wm.shape[2]
@@ -898,13 +914,26 @@
             us=13,
         )(pos_row, x)
 
-    if keep[0].shape[0] > 1:
-        keep, sent = send_next(keep, sent, 1)
-    wd = prep_down()
-    wd_x = core_swap(wd)
-    dy_x = core_swap(dy_all)
+    def query_window(tiles, dy):
+        sent = send_first(tiles)
+        for b in z_bits[1:-1]:
+            dy = join([dy, z_swap(dy, b)], 0)
+        dy_got = z_swap(dy, z_bits[-1])
+        keep = project(h1, h1_x, (wqk_m, wqk_x), 2, 1)
+        wd = prep_down()
+        return sent, keep, wd, dy, dy_got
+
+    def sum_window(sent, keep, wd, dy, dy_got):
+        if keep[0].shape[0] > 1:
+            keep, sent = send_next(keep, sent, 1)
+        dy = join([dy, dy_got], 0)
+        wd_x, dy_x = core_swap(wd), core_swap(dy)
+        return finish_reduce(keep, sent, 2), dy, dy_x, wd_x, places()
+
+    sent, keep, wd, dy, dy_got = window(query_window, tiles, dy)
     la.step()
-    qkv_parts = finish_reduce(keep, sent, 2)
+    qkv_parts, dy_all, dy_x, wd_x, at_places = window(sum_window, sent, keep, wd, dy, dy_got)
+    pos_row, pos_col, proj_scalars, all_scalars, back_scalars, starts_all, weight_scalars = at_places
 
     s_abs = f ^ chip
     positions = jnp.arange(seq, dtype=jnp.int32)
@@ -937,7 +966,6 @@
     ao_t = [core_swap(ao)]
     wo_m, wo_t, wo_x = split_halves(e_major(output_weight))
     la.step()
-    (wg_x,) = hold(wg_x)
     da_all = group_proj(dy_all, dy_x, wd, wd_x, 2)
     da_tiles, da_keep = da_all[:2], da_all[2:]
     ao_m = [ao] + hold(*ao_m[1:])
@@ -1043,8 +1071,6 @@
         dlog = gates * (dgate - jnp.sum(gates * dgate, axis=0, keepdims=True))
         return jnp.sum(jnp.where(route2[:, None, :] == experts[None, :, None], dlog[:, None, :], 0.0), axis=0)
 
-    near = list(chip_bits)
-    far = [k for k in range(1, n_chip) if k not in near]
 
     def gather_near(own):
         return {0: own} | {b: chip_swap(own, b) for b in near}
@@ -1078,8 +1104,6 @@
             where.append((i, h))
         return arrays, tuple(where)
 
-    back_groups = ([0], near, far)
-    back_scalars = [tile_scalars([[t for k in ks for t in back_table[k]]]).reshape(-1) for ks in back_groups]
 
     def group_back(g, pieces, w, acc, carry=()):
         m = w.shape[2]
@@ -1111,7 +1135,7 @@
             out_spec,
             out,
             [pltpu.VMEM((dc, m), F32)],
-            us=30 if m > fl else 24,
+            us=30 if m > fl else 0.1,
         )(xs, *arrays)
 
     dgu_pieces = {0: whole(dgu)}
@@ -1119,18 +1143,16 @@
     dgu_got = gather_near(dgu)
 
     tok_sum = Small(rel(tok_sum.reshape(8, n_z, seq).transpose(1, 0, 2)[:, :3]).reshape(n_z * 3, seq), "czx")
-    for _ in range(len(z_bits)):
-        tok_sum.step()
-
+    tok_sum.step()
     dh2 = group_back(0, dgu_pieces, wg, jnp.zeros((rows, dc), F32))
     act_pieces = {0: [(act, 0), (act, 1), (act_x, 0), (act_x, 1)]}
+    tok_sum.step()
     ffn = group_back(0, act_pieces, wd, jnp.zeros((rows, dc), F32))
+    tok_sum.step()
     got = hold(*[dgu_got[b] for b in near])
+    dgu_far = gather_far(dict(zip(near, got)))
     for b, v in zip(near, got):
-        dgu_got[b] = v
         dgu_pieces[b] = whole(v)
-    tok_sum.step()
-    dgu_far = gather_far({b: dgu_got[b] for b in near})
     dh2, act = group_back(1, dgu_pieces, wg, dh2, carry=(act,))
     act_pieces[0] = [(act, 0), (act, 1), (act_x, 0), (act_x, 1)]
     tok_sum.step()
@@ -1139,24 +1161,27 @@
         dgu_pieces[k] = apart(dgu_far, k)
     act_got = gather_near(act)
     dh2 = group_back(2, dgu_pieces, wg, dh2)
-    dh2_sent = z_send([dh2[k * seq : (k + 1) * seq].astype(BF) for k in range(n_z)])
-    gate_up_grad = group_weight(
-        yg_s,
-        dgu_pieces,
-        jax.ShapeDtypeStruct((dc, E_F, 2, fl_real), F32),
-        spec((dc, 1, 2, fl_real), lambda e, sc: (0, e, 0, 0)),
-    )
-    _, dh2 = z_total(dh2_sent)
-    dh2_got = z_gather(dh2)
-    got = hold(*[act_got[b] for b in near])
-    for b, v in zip(near, got):
-        act_got[b] = v
+    def first_back_window(dh2):
+        sent = z_send([dh2[k * seq : (k + 1) * seq].astype(BF) for k in range(n_z)])
+        gate_up_grad = group_weight(
+            yg_s,
+            dgu_pieces,
+            jax.ShapeDtypeStruct((dc, E_F, 2, fl_real), F32),
+            spec((dc, 1, 2, fl_real), lambda e, sc: (0, e, 0, 0)),
+        )
+        return z_total(sent)[1], gate_up_grad
+
+    dh2, gate_up_grad = window(first_back_window, dh2)
+    act_got = hold(*[act_got[b] for b in near])
+    for b, v in zip(near, act_got):
         act_pieces[b] = whole(v)
-    act_far = gather_far({b: act_got[b] for b in near})
-    ffn = group_back(1, act_pieces, wd, ffn)
-    act_far = dict(zip(act_far, hold(*act_far.values())))
-    for k in far:
-        act_pieces[k] = apart(act_far, k)
+    act_far = gather_far(dict(zip(near, act_got)))
+
+    def second_back_window(dh2, ffn):
+        got = z_gather(dh2)
+        return group_back(1, act_pieces, wd, ffn), got
+
+    ffn, dh2_got = window(second_back_window, dh2, ffn)
     tok_sum = rel(tok_sum.finish().reshape(n_z, 3, seq)).transpose(1, 0, 2).reshape(3, rows)
     dlf = router_back(tok_sum[0:2], pf, route_row[2:4])
     m2 = (tok_sum[2:3] + jnp.sum(dlf * lf, axis=0, keepdims=True)) / D
@@ -1175,8 +1200,9 @@
     dy1_x = core_swap(dy1_low)
 
     tiles = project(dy1_low, dy1_x, (wo_m, wo_x), 0, 0)
-    sent = send_first(tiles)
-    keep = project(dy1_low, dy1_x, (wo_m, wo_x), 0, 1)
+    sent, keep = window(
+        lambda tiles: (send_first(tiles), project(dy1_low, dy1_x, (wo_m, wo_x), 0, 1)), tiles
+    )
     if keep[0].shape[0] > 1:
         keep, sent = send_next(keep, sent, 1)
 
@@ -1199,6 +1225,9 @@
     def stream_t(v):
         return jnp.transpose(v.reshape(n_z, seq, dc), (0, 2, 1))
 
+    act_far = dict(zip(act_far, hold(*act_far.values())))
+    for k in far:
+        act_pieces[k] = apart(act_far, k)
     ffn = group_back(2, act_pieces, wd, ffn)
     dao_parts = finish_reduce(keep, sent, 2)
 
@@ -1214,22 +1243,24 @@
         [jax.ShapeDtypeStruct((seq, 4 * width), BF), jax.ShapeDtypeStruct((seq, 128), F32)],
             us=7,
     )(*dao_parts, qkv, ao, lse, pa_one, doc_col, doc_row, cosf, sinf)
-    g_m = [grads] + [chip_swap(grads, k) for k in range(1, n_chip)]
-    g_t = [core_swap(grads)]
     dpa = jnp.zeros((n_z, 2, seq), F32)
     dpa = lax.dynamic_update_slice(dpa, jnp.transpose(dgate[:, :2])[None], (s_abs, 0, 0))
     dpa = Small(dpa.reshape(n_z * 2, seq), "czx")
-    ffn_sent = z_send([ffn[k * seq : (k + 1) * seq].astype(BF) for k in range(n_z)])
-    down_grad = group_weight(
-        dy_s,
-        act_pieces,
-        jax.ShapeDtypeStruct((dc, E_F, fl_real), F32),
-        spec((dc, E_F, fl_real)),
-    )
-    ffn = z_total(ffn_sent, y1)[1]
-    for _ in range(1 + len(z_bits)):
-        dpa.step()
-    g_m = [grads] + hold(*g_m[1:])
+    def grads_window(grads, ffn):
+        got = [chip_swap(grads, k) for k in range(1, n_chip)]
+        own = core_swap(grads)
+        ffn_sent = z_swap(ffn[rows // 2 :], z_bits[-1])
+        down_grad = group_weight(
+            dy_s,
+            act_pieces,
+            jax.ShapeDtypeStruct((dc, E_F, fl_real), F32),
+            spec((dc, E_F, fl_real)),
+        )
+        return got, own, ffn_sent, down_grad
+
+    ffn = ffn.astype(BF)
+    g_m, own_t, ffn_sent, down_grad = window(grads_window, grads, ffn)
+    g_m, g_t = [grads, *g_m], [own_t]
     dpa.step()
     g_t += [core_swap(v) for v in g_m[1:]]
 
@@ -1251,12 +1282,30 @@
             5,
             4 * width,
         )
+        dpa.step()
         if k == 0:
-            dpa.finish()
+            for b in z_bits[-2::-1]:
+                n = ffn_sent.shape[0] // 2
+                both = [spec((n, dc), lambda i, sc: (i, 0))] * 2
+                ffn, _ = launch(
+                    functools.partial(total_body, 2),
+                    one,
+                    (2,),
+                    both,
+                    both,
+                    [jax.ShapeDtypeStruct((2 * n, dc), F32), jax.ShapeDtypeStruct((2 * n, dc), BF)],
+                    us=2,
+                )(ffn, ffn_sent)[::-1]
+                ffn_sent = z_swap(ffn[n:], b)
     dpa = lax.dynamic_index_in_dim(dpa.finish().reshape(n_z, 2, seq), f, 0, keepdims=False)
-    dh1_sent = z_send([buf[k] for k in range(n_z)])
-    query_grad, kv_grad = att_weight(stream_t(h1), False, True, g_m, g_t, 4 * width)
-    dh1, _ = z_total(dh1_sent)
+    ffn = z_total([ffn[:seq], ffn_sent], y1)[1]
+
+    def last_window(buf):
+        sent = z_send([buf[k] for k in range(n_z)])
+        query_grad, kv_grad = att_weight(stream_t(h1), False, True, g_m, g_t, 4 * width)
+        return z_total(sent)[0], query_grad, kv_grad
+
+    dh1, query_grad, kv_grad = window(last_window, buf)
     dla = router_back(dpa, pa[:, :seq], route_row[0:2, :seq]).astype(BF)
     dh1 = dh1 + lax.dot_general(dla, ra, (((0,), (1,)), ((), ())), preferred_element_type=F32)
     back_col = jnp.concatenate(((dh1 * ga).astype(BF), dy1_low[:seq]), axis=1)

time: 934 us -> 884 us (0.946)
  Pallas kernels: 479 us -> 457 us
  local copies, waits for them, and re-layouts: 103 us -> 91.9 us
  waiting for transfers between devices: 178 us -> 168 us
    pallas_call x79 -> x78, Pallas kernels: 479 us -> 457 us  [go(): pl.pallas_call(kernel_body, out_shape=out_shape + [jax.ShapeDtypeStruct(v...]
    unnamed x315 -> x241, local copies, waits for them, and re-layouts: 49.3 us -> 36 us
    ppermute x105 -> x104, waiting for transfers between devices: 178 us -> 168 us  [swap(): return lax.ppermute(x, axis, [(i, i ^ k) for i in range(n)])]
    ppermute x105 -> x104, starting transfers between devices: 106 us -> 101 us  [swap(): return lax.ppermute(x, axis, [(i, i ^ k) for i in range(n)])]
  transfers between devices with their start and end apart: 107 -> 106, of which waited for: 29 -> 28; matrix products, arithmetic and copies ran while one was open for 10% -> 10% of each run, Pallas kernels for 49% -> 49%
where the time goes in v3:
time: 884 us; the launch traced here: 871 us
  Pallas kernels  457 us (52%)
  waiting for transfers between devices  168 us (19%)
  starting transfers between devices  109 us (12%)
  local copies, waits for them, and re-layouts  91.9 us (10%)
  other arithmetic  34.9 us (4%)
    pallas_call x78, Pallas kernels, go(): pl.pallas_call(kernel_body, out_shape=out_shape + [jax.ShapeDtypeStruct(v...  457 us
    ppermute x104, waiting for transfers between devices, swap(): return lax.ppermute(x, axis, [(i, i ^ k) for i in range(n)])  168 us
    ppermute x104, starting transfers between devices, swap(): return lax.ppermute(x, axis, [(i, i ^ k) for i in range(n)])  101 us
    unnamed x241, local copies, waits for them, and re-layouts  36 us
  transfers between devices with their start and end apart: 106, of which 28 were waited for; matrix products, arithmetic and copies ran while one was open for 10% of the time, Pallas kernels for 49%

profile of v3, /device:TPU:0, one launch (start us, length us, event | category | flops | bytes accessed | tf_op | source)
XLA Modules:
  0.0 871.0 jit_solution(749062719276561926)
XLA Ops:
  35.5 35.9 %conditional.8 = (bf16[2048,256]{1,0:T(8,128)(2,1)}, bf16[2048,256]{1,0:T(8,128)(2,1)S(1)}, bf16[1024,256]{1,0:T(8,128)(2,1)S(1)}, bf16[8,256,2816]{2,1,0:T(8,128)(2,1)}) conditional(s32[]{:T(128)} %bitcast.57, () %tuple.78, (bf16[512,256]{1,0:T(8,128)(2,1)S(1)}, f32[256,8,2,1408]{3,2,1,0:T(2,128)}, s32[2048,4]{1,0:T(8,128)S(1)}, ...), branch_computations={%region_2.3_spmd, %region_3.4_spmd} | conditional | flops 32450000896 | bytes 14155816 | solution.py:611
  41.3 25.8 %branch_1_fun.15.refs_5_ = bf16[8,256,2816]{2,1,0:T(8,128)(2,1)} custom-call(s32[1]{0:T(128)} %constant.101.clone.first, f32[256,8,2,1408]{3,2,1,0:T(2,128)} %get-tuple-element.580.refs_0_, s32[2048,4]{1,0:T(8,128)S(1)} %get-tuple-element.223.refs_1_, bf16[10,256,256]{2,1,0:T(8,128)(2,1)} %get-tuple-element.224.refs_2_, f32[2,256]{1,0:T(2,128)S(1)} %get-tuple-element.225.refs_3_), custom_call_target="tpu_custom_call" | custom-call | flops 28600000512 | tf_op jit(solution)/shard_map/cond/branch_1_fun/pallas_call | solution.py:64
  101.0 30.0 %conditional.9 = (bf16[2,256,1024]{2,1,0:T(8,128)(2,1)}, bf16[2,256,1024]{2,1,0:T(8,128)(2,1)}, bf16[2,256,1024]{2,1,0:T(8,128)(2,1)}, bf16[2,256,1024]{2,1,0:T(...) conditional(s32[]{:T(128)} %bitcast.57, () %tuple.77, ...), branch_computations={%region_4.5_spmd, %region_5.6_spmd} | conditional | flops 19249999872 | bytes 11534628 | solution.py:611
  115.0 9.5 %branch_1_fun.19 = bf16[8,256,1408]{2,1,0:T(8,128)(2,1)} custom-call(s32[1]{0:T(128)} %constant.105.clone.first, f32[256,8,1408]{2,1,0:T(8,128)} %get-tuple-element.582.refs_0_, bf16[2,256,1024]{2,1,0:T(8,128)(2,1)} %get-tuple-element.998.refs_1_), custom_call_target="tpu_custom_call" | custom-call | flops 10449999872 | tf_op jit(solution)/shard_map/cond/branch_1_fun/pallas_call | solution.py:64
  132.4 23.1 %conditional.10 = (bf16[256,1024]{1,0:T(8,128)(2,1)S(1)}, bf16[256,1024]{1,0:T(8,128)(2,1)}, bf16[256,1024]{1,0:T(8,128)(2,1)S(1)}, bf16[256,1024]{1,0:T(8,128)(...) conditional(s32[]{:T(128)} %bitcast.57, () %tuple.76, ...), branch_computations={%region_6.7_spmd, %region_7.48_spmd} | conditional | flops 6272583168 | bytes 37044896 | solution.py:611
  168.3 21.4 %shard_map.406 = (bf16[2,256,1408]{2,1,0:T(8,128)(2,1)}, bf16[2,256,1408]{2,1,0:T(8,128)(2,1)}, bf16[2,256,1408]{2,1,0:T(8,128)(2,1)}, bf16[2,256,1408]{2,1,0:T(8,128)(2,1)}) custom-call(s32[62]{0:T(128)S(1)} %get-tuple-element.485.first, s32[2,2048]{1,0:T(2,128)S(1)} %get-tuple-element.486.refs_0_, bf16[2048,256]{1,0:T(8,128)(2,1)} %get-tuple-element.479.refs_1_.refs_0_, ...), custom_call_target="tpu_custom_call" | custom-call | flops 29699999744 | tf_op jit(solution)/shard_map/pallas_call | solution.py:64
  224.5 8.7 %collective-permute-done.45.refs_1_ = bf16[512,256]{1,0:T(8,128)(2,1)S(1)} collective-permute-done((bf16[512,256]{1,0:T(8,128)(2,1)S(1)}, bf16[512,256]{1,0:T(8,128)(2,1)S(1)}, u32[]{:S(2)}, u32[]{:S(2)}) %collective-permute-start.45) | collective-permute-done | bytes 262176 | tf_op jit(solution)/shard_map/ppermute | solution.py:564
  287.0 15.9 %shard_map.420 = (bf16[2,256,2816]{2,1,0:T(8,128)(2,1)}, bf16[2,256,2816]{2,1,0:T(8,128)(2,1)}) custom-call(s32[92]{0:T(128)S(1)} %get-tuple-element.506.first, s32[2,2048]{1,0:T(2,128)S(1)} %get-tuple-element.486.refs_0_, bf16[2048,256]{1,0:T(8,128)(2,1)} %get-tuple-element.507.refs_1_, bf16[2048,256]{1,0:T(8,128)(2,1)} %multiply_convert_fusion.refs_2_, ...), custom_call_target="tpu_custom_call" | custom-call | flops 18699999232 | tf_op jit(solution)/shard_map/pallas_call | solution.py:64
  309.4 15.0 %shard_map.422 = (bf16[2,256,2816]{2,1,0:T(8,128)(2,1)}, bf16[2,256,2816]{2,1,0:T(8,128)(2,1)}) custom-call(s32[92]{0:T(128)S(1)} %get-tuple-element.506.first, s32[2,2048]{1,0:T(2,128)S(1)} %get-tuple-element.486.refs_0_, bf16[2048,256]{1,0:T(8,128)(2,1)} %get-tuple-element.507.refs_1_, bf16[2048,256]{1,0:T(8,128)(2,1)} %multiply_convert_fusion.refs_2_, ...), custom_call_target="tpu_custom_call" | custom-call | flops 18699999232 | tf_op jit(solution)/shard_map/pallas_call | solution.py:64
  327.5 13.0 %shard_map.424.refs_2_ = bf16[256,4096]{1,0:T(8,128)(2,1)} custom-call(s32[16]{0:T(128)} %get-tuple-element.516.first, s32[2,2048]{1,0:T(2,128)S(1)} %get-tuple-element.486.refs_0_, bf16[2048,256]{1,0:T(8,128)(2,1)} %get-tuple-element.507.refs_1_, f32[16,1024]{1,0:T(8,128)} %shard_map.423.refs_2_.refs_0_), custom_call_target="tpu_custom_call" | custom-call | flops 14300000256 | tf_op jit(solution)/shard_map/pallas_call | solution.py:64
  340.5 12.4 %shard_map.425.refs_4_ = bf16[256,4096]{1,0:T(8,128)(2,1)S(1)} custom-call(s32[16]{0:T(128)} %get-tuple-element.516.first, s32[2,2048]{1,0:T(2,128)S(1)} %get-tuple-element.486.refs_0_, bf16[2048,256]{1,0:T(8,128)(2,1)} %get-tuple-element.479.refs_1_.refs_0_, bf16[256,4096]{1,0:T(8,128)(2,1)} %shard_map.424.refs_2_), custom_call_target="tpu_custom_call" | custom-call | flops 14300000256 | tf_op jit(solution)/shard_map/pallas_call | solution.py:64
  352.9 16.0 %collective-permute-done.62.refs_1_ = bf16[2,256,2816]{2,1,0:T(8,128)(2,1)} collective-permute-done((bf16[2,256,2816]{2,1,0:T(8,128)(2,1)}, bf16[2,256,2816]{2,1,0:T(8,128)(2,1)}, u32[]{:S(2)}, u32[]{:S(2)}) %collective-permute-start.62) | collective-permute-done | bytes 2883616 | tf_op jit(solution)/shard_map/ppermute | solution.py:564
  384.9 23.3 %collective-permute-done.64 = bf16[1,256,2816]{2,1,0:T(8,128)(2,1)S(1)} collective-permute-done((bf16[1,256,2816]{2,1,0:T(8,128)(2,1)}, bf16[1,256,2816]{2,1,0:T(8,128)(2,1)S(1)}, u32[]{:S(2)}, u32[]{:S(2)}) %collective-permute-start.64) | collective-permute-done | bytes 1441824 | tf_op jit(solution)/shard_map/ppermute | solution.py:564
  416.2 12.3 %shard_map.429 = (bf16[2,256,2816]{2,1,0:T(8,128)(2,1)}, bf16[2,256,1408]{2,1,0:T(8,128)(2,1)S(1)}, f32[8,2048]{1,0:T(8,128)}) custom-call(s32[2]{0:T(128)} %pad_add_fusion.8.first, s32[2,2048]{1,0:T(2,128)S(1)} %get-tuple-element.486.refs_0_, f32[8,2048]{1,0:T(8,128)} %maximum_maximum_fusion.refs_1_, bf16[256,2816]{1,0:T(8,128)(2,1)} %bitcast.354, ...), custom_call_target="tpu_custom_call" | custom-call | flops 14300000256 | tf_op jit(solution)/shard_map/pallas_call | solution.py:64
  437.1 11.3 %shard_map.431.refs_2_.refs_6_ = f32[2048,256]{1,0:T(8,128)S(1)} custom-call(s32[46]{0:T(128)S(1)} %copy-done.131, s32[2048,2]{1,0:T(8,128)} %copy-done.20, bf16[2,256,2816]{2,1,0:T(8,128)(2,1)} %get-tuple-element.523.refs_2_.refs_1_, bf16[2,256,2816]{2,1,0:T(8,128)(2,1)} %collective-permute-done.68.refs_2_, ...), custom_call_target="tpu_custom_call", output_to_operand_aliasing={{}: (5, {})} | custom-call | flops 14960000000 | tf_op jit(solution)/shard_map/pallas_call | solution.py:64
  452.8 8.5 shard_map.433.refs_2_
  463.4 30.6 %collective-permute-done.72.refs_1_ = bf16[2,256,2816]{2,1,0:T(8,128)(2,1)} collective-permute-done((bf16[2,256,2816]{2,1,0:T(8,128)(2,1)}, bf16[2,256,2816]{2,1,0:T(8,128)(2,1)}, u32[]{:S(2)}, u32[]{:S(2)}) %collective-permute-start.72) | collective-permute-done | bytes 2883616 | tf_op jit(solution)/shard_map/ppermute | solution.py:564
  504.5 23.7 %shard_map.436 = (f32[2048,256]{1,0:T(8,128)}, bf16[2,256,1408]{2,1,0:T(8,128)(2,1)}) custom-call(s32[62]{0:T(128)S(1)} %copy-done.129, s32[2048,2]{1,0:T(8,128)} %copy-done.20, bf16[2,256,2816]{2,1,0:T(8,128)(2,1)} %get-tuple-element.528.refs_1_, ...), custom_call_target="tpu_custom_call", output_to_operand_aliasing={{0}: (7, {}), {1}: (9, {})} | custom-call | flops 29920000000 | tf_op jit(solution)/shard_map/pallas_call | solution.py:64
  544.1 12.4 %shard_map.439 = f32[2048,256]{1,0:T(8,128)} custom-call(s32[46]{0:T(128)S(1)} %copy-done.133, s32[2048,2]{1,0:T(8,128)} %copy-done.20, bf16[256,2816]{1,0:T(8,128)(2,1)S(1)} %get-tuple-element.533.refs_1_, bf16[256,2816]{1,0:T(8,128)(2,1)} %get-tuple-element.534.refs_2_, bf16[256,2816]{1,0:T(8,128)(2,1)} %copy-done.91, ...), custom_call_target="tpu_custom_call", output_to_operand_aliasing={{}: (7, {})} | custom-call | flops 14960000000 | tf_op jit(solution)/shard_map/pallas_call | solution.py:64
  556.5 38.8 %conditional.11 = (bf16[512,256]{1,0:T(8,128)(2,1)S(1)}, f32[256,8,2,1408]{3,2,1,0:T(2,128)}) conditional(s32[]{:T(128)} %bitcast.57, () %tuple.83, (f32[2048,256]{1,0:T(8,128)}, s32[25]{0:T(128)S(1)}, bf16[256,4096]{1,0:T(8,128)(2,1)}, bf16[2,256,2816]{2,1,0:T(8,128)(2,1)}, bf16[2,256,2816]{2,1,0:T(8,128)(2,1)}, ...), branch_computations={%region_57.59_spmd, %region_58.60_spmd} | conditional | flops 34650525696 | bytes 23330838 | solution.py:611
  563.5 29.3 %branch_1_fun.23.refs_4_ = f32[256,8,2,1408]{3,2,1,0:T(2,128)} custom-call(s32[25]{0:T(128)S(1)} %get-tuple-element.279.first, bf16[256,4096]{1,0:T(8,128)(2,1)} %get-tuple-element.280.refs_0_, bf16[2,256,2816]{2,1,0:T(8,128)(2,1)} %get-tuple-element.281.refs_1_, bf16[2,256,2816]{2,1,0:T(8,128)(2,1)} %get-tuple-element.282.refs_2_, ...), custom_call_target="tpu_custom_call" | custom-call | flops 32999999488 | tf_op jit(solution)/shard_map/cond/branch_1_fun/pallas_call | solution.py:64
  601.0 23.8 %conditional.12 = (f32[2048,256]{1,0:T(8,128)S(1)}, bf16[512,256]{1,0:T(8,128)(2,1)S(1)}, bf16[512,256]{1,0:T(8,128)(2,1)}, bf16[512,256]{1,0:T(8,128)(2,1)}, bf16[512,256]{1,0:T(8,128)(2,1)}) conditional(s32[]{:T(128)} %bitcast.57, () %tuple.82, (s32[62]{0:T(128)S(1)}, s32[2048,2]{0,1:T(2,128)}, bf16[2,256,1408]{2,1,0:T(8,128)(2,1)}, ...), branch_computations={%region_59.61_spmd, %region_60.62_spmd} | conditional | flops 24640000000 | bytes 3702944 | solution.py:611
  607.5 17.3 %branch_1_fun.25 = f32[2048,256]{1,0:T(8,128)S(1)} custom-call(s32[62]{0:T(128)S(1)} %get-tuple-element.292.first, s32[2048,2]{1,0:T(8,128)} %copy.261.refs_0_, bf16[2,256,1408]{2,1,0:T(8,128)(2,1)} %get-tuple-element.294.refs_1_, bf16[2,256,1408]{2,1,0:T(8,128)(2,1)} %get-tuple-element.295.refs_2_, ...), custom_call_target="tpu_custom_call", output_to_operand_aliasing={{}: (7, {})} | custom-call | flops 24640000000 | tf_op jit(solution)/shard_map/cond/branch_1_fun/pallas_call | solution.py:64
  648.6 22.2 %conditional.13 = (bf16[2,256,512]{2,1,0:T(8,128)(2,1)}, bf16[2,256,512]{2,1,0:T(8,128)(2,1)}, bf16[2,256,512]{2,1,0:T(8,128)(2,1)}, bf16[2,256,512]{2,1,0:T(8,128)(2,1)}) conditional(s32[]{:T(128)} %bitcast.57, () %tuple.75, (bf16[2,256,512]{2,1,0:T(8,128)(2,1)}, bf16[2,256,512]{2,1,0:T(8,128)(2,1)}, s32[]{:T(128)}, s32[2048,4]{1,0:T(8,128)S(1)}, ...), branch_computations={%region_64.66_spmd, %region_65.67_spmd} | conditional | flops 7699999744 | bytes 4194532 | solution.py:611
  659.1 11.7 %collective-permute-done.15 = bf16[2,256,512]{2,1,0:T(8,128)(2,1)} collective-permute-done((bf16[2,256,512]{2,1,0:T(8,128)(2,1)}, bf16[2,256,512]{2,1,0:T(8,128)(2,1)}, u32[]{:S(2)}, u32[]{:S(2)}) %collective-permute-start.15) | collective-permute-done | bytes 524320 | tf_op jit(solution)/shard_map/cond/branch_1_fun/ppermute | solution.py:564
  683.1 9.0 %shard_map.447.refs_12_ = f32[2048,256]{1,0:T(8,128)S(1)} custom-call(s32[46]{0:T(128)S(1)} %copy-done.133, s32[2048,2]{1,0:T(8,128)} %copy-done.20, bf16[256,1408]{1,0:T(8,128)(2,1)} %get-tuple-element.559.refs_1_, bf16[256,1408]{1,0:T(8,128)(2,1)} %get-tuple-element.560.refs_2_, bf16[256,1408]{1,0:T(8,128)(2,1)} %copy-done.22, ...), custom_call_target="tpu_custom_call", output_to_operand_aliasing={{}: (7, {})} | custom-call | flops 12320000000 | tf_op jit(solution)/shard_map/pallas_call | solution.py:64
  702.2 51.6 %conditional.14 = (bf16[512,1024]{1,0:T(8,128)(2,1)}, bf16[512,1024]{1,0:T(8,128)(2,1)}, bf16[512,1024]{1,0:T(8,128)(2,1)}, bf16[512,1024]{1,0:T(8,128)(2,1)}, b...) conditional(s32[]{:T(128)} %bitcast.57, () %tuple.74, (bf16[512,1024]{1,0:T(8,128)(2,1)}, ...), branch_computations={%region_66.68_spmd, %region_67.69_spmd} | conditional | flops 110000000 | bytes 19923192 | solution.py:611
  712.0 24.0 %branch_1_fun.27 = f32[256,8,1408]{2,1,0:T(8,128)} custom-call(s32[25]{0:T(128)S(1)} %get-tuple-element.314.first, bf16[256,4096]{1,0:T(8,128)(2,1)} %get-tuple-element.315.refs_0_, bf16[2,256,1408]{2,1,0:T(8,128)(2,1)} %get-tuple-element.316.refs_1_, bf16[2,256,1408]{2,1,0:T(8,128)(2,1)} %get-tuple-element.317.refs_2_, ...), custom_call_target="tpu_custom_call" | custom-call | flops 110000000 | tf_op jit(solution)/shard_map/cond/branch_1_fun/pallas_call | solution.py:64
  736.0 17.4 %collective-permute-done.8 = bf16[512,1024]{1,0:T(8,128)(2,1)} collective-permute-done((bf16[512,1024]{1,0:T(8,128)(2,1)}, bf16[512,1024]{1,0:T(8,128)(2,1)}, u32[]{:S(2)}, u32[]{:S(2)}) %collective-permute-start.8) | collective-permute-done | bytes 1048608 | tf_op jit(solution)/shard_map/cond/branch_1_fun/ppermute | solution.py:564
  797.6 29.7 %conditional.15 = (f32[512,256]{1,0:T(8,128)S(1)}, f32[256,8,512]{2,1,0:T(8,128)}, f32[256,2,512]{2,1,0:T(2,128)}) conditional(s32[]{:T(128)} %bitcast.57, () %tuple.73, (bf16[4,512,256]{2,1,0:T(8,128)(2,1)S(1)}, s32[]{:T(128)}, s32[]{:T(128)}, bf16[2048,256]{1,0:T(8,128)(2,1)S(1)}, s32[4,512,2]{2,1,0:T(8,128)S(1)}, ...), branch_computations={%region_68.70_spmd, %region_69.71_spmd} | conditional | flops 23650000896 | bytes 7405800 | solution.py:611
  805.1 20.2 %branch_1_fun.28 = (f32[256,8,512]{2,1,0:T(8,128)}, f32[256,2,512]{2,1,0:T(2,128)}) custom-call(s32[5]{0:T(128)} %pad_add_fusion.2.first, bf16[4,256,512]{2,1,0:T(8,128)(2,1)} %bitcast.316, s32[4,512,2]{2,1,0:T(8,128)S(1)} %get-tuple-element.330.refs_1_, f32[4,512,2]{2,1,0:T(8,128)S(1)} %copy-done.14, bf16[512,1024]{1,0:T(8,128)(2,1)} %get-tuple-element.332.refs_3_, ...), custom_call_target="tpu_custom_call" | custom-call | flops 22000001024 | tf_op jit(solution)/shard_map/cond/branch_1_fun/pallas_call | solution.py:64
  835.1 18.3 %shard_map.460.refs_2_ = f32[256,8,512]{2,1,0:T(8,128)} custom-call(s32[5]{0:T(128)} %pad_add_fusion.9.first, bf16[4,256,512]{2,1,0:T(8,128)(2,1)} %bitcast.315, s32[4,512,2]{2,1,0:T(8,128)S(1)} %bitcast.291, f32[4,512,2]{2,1,0:T(8,128)} %bitcast.313, bf16[512,512]{1,0:T(8,128)(2,1)} %get-tuple-element.490.refs_2_.refs_5_.refs_3_, ...), custom_call_target="tpu_custom_call" | custom-call | flops 22000001024 | tf_op jit(solution)/shard_map/pallas_call | solution.py:64
  (780 shorter events, 458.7 us)
Async XLA Ops:
  35.5 31.6 %collective-permute-start = (bf16[512,256]{1,0:T(8,128)(2,1)S(1)}, bf16[512,256]{1,0:T(8,128)(2,1)S(1)}, u32[]{:S(2)}, u32[]{:S(2)}) collective-permute-start(bf16[512,256]{1,0:T(8,128)(2,1)S(1)} %get-tuple-element.200.refs_1_), channel_id=1, source_target_pairs={{0,1},{1,0},{2,3},{3,2},{4,5},{5,4},{6,7},{7,6},{8,9},{9,8},{10,11... | collective-permute-start | bytes 786440 | tf_op jit(solution)/shard_map/cond/branch_1_fun/ppermute | solution.py:564
  84.8 202.2 %collective-permute-start.58 = (bf16[8,256,2816]{2,1,0:T(8,128)(2,1)}, bf16[8,256,2816]{2,1,0:T(8,128)(2,1)}, u32[]{:S(2)}, u32[]{:S(2)}) collective-permute-start(bf16[8,256,2816]{2,1,0:T(8,128)(2,1)} %get-tuple-element.508.refs_3_.refs_5_), channel_id=1, source_target_pairs={{0,4},{4,0},{8,12},{12,8},{16,20},{20,16},{24,28},{28,24},{1,5},{5... | collective-permute-start | bytes 34603016 | tf_op jit(solution)/shard_map/ppermute | solution.py:564
  96.2 34.8 %collective-permute-start.35 = (f32[8,512]{1,0:T(8,128)S(1)}, f32[8,512]{1,0:T(8,128)S(1)}, u32[]{:S(2)}, u32[]{:S(2)}) collective-permute-start(f32[8,512]{1,0:T(8,128)S(1)} %shard_map.402.refs_0_), channel_id=1, source_target_pairs={{0,16},{4,20},{8,24},{12,28},{16,0},{20,4},{24,8},{28,12},{1,17},{... | collective-permute-start | bytes 49160 | tf_op jit(solution)/shard_map/ppermute | solution.py:564
  166.4 33.7 %collective-permute-start.44 = (bf16[512,512]{1,0:T(8,128)(2,1)}, bf16[512,512]{1,0:T(8,128)(2,1)}, u32[]{:S(2)}, u32[]{:S(2)}) collective-permute-start(bf16[512,512]{1,0:T(8,128)(2,1)} %get-tuple-element.490.refs_2_.refs_5_.refs_3_), channel_id=1, source_target_pairs={{0,4},{4,0},{8,12},{12,8},{16,20},{20,16},{24,28},{28,24},{1,5},{5... | collective-permute-start | bytes 1572872 | tf_op jit(solution)/shard_map/ppermute | solution.py:564
  217.2 37.8 %collective-permute-start.52 = (bf16[2,256,1408]{2,1,0:T(8,128)(2,1)}, bf16[2,256,1408]{2,1,0:T(8,128)(2,1)S(1)}, u32[]{:S(2)}, u32[]{:S(2)}) collective-permute-start(bf16[2,256,1408]{2,1,0:T(8,128)(2,1)} %get-tuple-element.499), channel_id=1, source_target_pairs={{0,8},{4,12},{8,0},{12,4},{16,24},{20,28},{24,16},{28,20},{1,9},{5... | collective-permute-start | bytes 4325384 | tf_op jit(solution)/shard_map/ppermute | solution.py:564
  218.8 38.6 %collective-permute-start.53 = (bf16[2,256,1408]{2,1,0:T(8,128)(2,1)}, bf16[2,256,1408]{2,1,0:T(8,128)(2,1)S(1)}, u32[]{:S(2)}, u32[]{:S(2)}) collective-permute-start(bf16[2,256,1408]{2,1,0:T(8,128)(2,1)} %get-tuple-element.501), channel_id=1, source_target_pairs={{0,16},{4,20},{8,24},{12,28},{16,0},{20,4},{24,8},{28,12},{1,17},{... | collective-permute-start | bytes 4325384 | tf_op jit(solution)/shard_map/ppermute | solution.py:564
  248.3 30.6 %collective-permute-start.48 = (bf16[512,256]{1,0:T(8,128)(2,1)}, bf16[512,256]{1,0:T(8,128)(2,1)S(1)}, u32[]{:S(2)}, u32[]{:S(2)}) collective-permute-start(bf16[512,256]{1,0:T(8,128)(2,1)} %get-tuple-element.497.refs_1_), channel_id=1, source_target_pairs={{0,1},{1,0},{2,3},{3,2},{4,5},{5,4},{6,7},{7,6},{8,9},{9,8},{10,11... | collective-permute-start | bytes 786440 | tf_op jit(solution)/shard_map/ppermute | solution.py:564
  284.6 39.9 %collective-permute-start.56 = (f32[16,512]{1,0:T(8,128)S(1)}, f32[16,512]{1,0:T(8,128)S(1)}, u32[]{:S(2)}, u32[]{:S(2)}) collective-permute-start(f32[16,512]{1,0:T(8,128)S(1)} %copy-done.108), channel_id=1, source_target_pairs={{0,1},{1,0},{2,3},{3,2},{4,5},{5,4},{6,7},{7,6},{8,9},{9,8},{10,11... | collective-permute-start | bytes 98312 | tf_op jit(solution)/shard_map/ppermute | solution.py:564
  302.9 66.0 %collective-permute-start.62 = (bf16[2,256,2816]{2,1,0:T(8,128)(2,1)}, bf16[2,256,2816]{2,1,0:T(8,128)(2,1)}, u32[]{:S(2)}, u32[]{:S(2)}) collective-permute-start(bf16[2,256,2816]{2,1,0:T(8,128)(2,1)} %get-tuple-element.511.refs_4_), channel_id=1, source_target_pairs={{0,8},{4,12},{8,0},{12,4},{16,24},{20,28},{24,16},{28,20},{1,9},{5... | collective-permute-start | bytes 8650760 | tf_op jit(solution)/shard_map/ppermute | solution.py:564
  305.3 65.0 %collective-permute-start.63 = (bf16[2,256,2816]{2,1,0:T(8,128)(2,1)}, bf16[2,256,2816]{2,1,0:T(8,128)(2,1)}, u32[]{:S(2)}, u32[]{:S(2)}) collective-permute-start(bf16[2,256,2816]{2,1,0:T(8,128)(2,1)} %get-tuple-element.515), channel_id=1, source_target_pairs={{0,16},{4,20},{8,24},{12,28},{16,0},{20,4},{24,8},{28,12},{1,17},{... | collective-permute-start | bytes 8650760 | tf_op jit(solution)/shard_map/ppermute | solution.py:564
  326.5 53.3 %collective-permute-start.61 = (f32[16,1024]{1,0:T(8,128)}, f32[16,1024]{1,0:T(8,128)S(1)}, u32[]{:S(2)}, u32[]{:S(2)}) collective-permute-start(f32[16,1024]{1,0:T(8,128)} %shard_map.423.refs_2_.refs_0_), channel_id=1, source_target_pairs={{0,2},{1,3},{2,0},{3,1},{4,6},{5,7},{6,4},{7,5},{8,10},{9,11},{10,... | collective-permute-start | bytes 196616 | tf_op jit(solution)/shard_map/ppermute | solution.py:564
  374.9 33.2 %collective-permute-start.64 = (bf16[1,256,2816]{2,1,0:T(8,128)(2,1)}, bf16[1,256,2816]{2,1,0:T(8,128)(2,1)S(1)}, u32[]{:S(2)}, u32[]{:S(2)}) collective-permute-start(bf16[1,256,2816]{2,1,0:T(8,128)(2,1)} %get-tuple-element.517.refs_4_), channel_id=1, source_target_pairs={{0,16},{4,20},{8,24},{12,28},{16,0},{20,4},{24,8},{28,12},{1,17},{... | collective-permute-start | bytes 4325384 | tf_op jit(solution)/shard_map/ppermute | solution.py:564
  382.8 33.4 %collective-permute-start.65 = (bf16[1,256,2816]{2,1,0:T(8,128)(2,1)}, bf16[1,256,2816]{2,1,0:T(8,128)(2,1)}, u32[]{:S(2)}, u32[]{:S(2)}) collective-permute-start(bf16[1,256,2816]{2,1,0:T(8,128)(2,1)} %get-tuple-element.520), channel_id=1, source_target_pairs={{0,8},{4,12},{8,0},{12,4},{16,24},{20,28},{24,16},{28,20},{1,9},{5... | collective-permute-start | bytes 4325384 | tf_op jit(solution)/shard_map/ppermute | solution.py:564
  428.7 65.3 %collective-permute-start.72 = (bf16[2,256,2816]{2,1,0:T(8,128)(2,1)}, bf16[2,256,2816]{2,1,0:T(8,128)(2,1)}, u32[]{:S(2)}, u32[]{:S(2)}) collective-permute-start(bf16[2,256,2816]{2,1,0:T(8,128)(2,1)} %get-tuple-element.523.refs_2_.refs_1_), channel_id=1, source_target_pairs={{0,8},{4,12},{8,0},{12,4},{16,24},{20,28},{24,16},{28,20},{1,9},{5... | collective-permute-start | bytes 8650760 | tf_op jit(solution)/shard_map/ppermute | solution.py:564
  429.3 64.9 %collective-permute-start.73 = (bf16[2,256,2816]{2,1,0:T(8,128)(2,1)}, bf16[2,256,2816]{2,1,0:T(8,128)(2,1)}, u32[]{:S(2)}, u32[]{:S(2)}) collective-permute-start(bf16[2,256,2816]{2,1,0:T(8,128)(2,1)} %get-tuple-element.523.refs_2_.refs_1_), channel_id=1, source_target_pairs={{0,16},{4,20},{8,24},{12,28},{16,0},{20,4},{24,8},{28,12},{1,17},{... | collective-permute-start | bytes 8650760 | tf_op jit(solution)/shard_map/ppermute | solution.py:564
  495.3 33.0 %collective-permute-start.71 = (f32[12,512]{1,0:T(8,128)S(1)}, f32[12,512]{1,0:T(8,128)S(1)}, u32[]{:S(2)}, u32[]{:S(2)}) collective-permute-start(f32[12,512]{1,0:T(8,128)S(1)} %copy-done.35), channel_id=1, source_target_pairs={{0,8},{4,12},{8,0},{12,4},{16,24},{20,28},{24,16},{28,20},{1,9},{5... | collective-permute-start | bytes 73736 | tf_op jit(solution)/shard_map/ppermute | solution.py:564
  499.4 33.4 %collective-permute-start.77 = (bf16[256,2816]{1,0:T(8,128)(2,1)}, bf16[256,2816]{1,0:T(8,128)(2,1)S(1)}, u32[]{:S(2)}, u32[]{:S(2)}) collective-permute-start(bf16[256,2816]{1,0:T(8,128)(2,1)} %slice_bitcast_fusion.5), channel_id=1, source_target_pairs={{0,16},{4,20},{8,24},{12,28},{16,0},{20,4},{24,8},{28,12},{1,17},{... | collective-permute-start | bytes 4325384 | tf_op jit(solution)/shard_map/ppermute | solution.py:564
  503.4 33.2 %collective-permute-start.78 = (bf16[256,2816]{1,0:T(8,128)(2,1)}, bf16[256,2816]{1,0:T(8,128)(2,1)}, u32[]{:S(2)}, u32[]{:S(2)}) collective-permute-start(bf16[256,2816]{1,0:T(8,128)(2,1)} %slice_bitcast_fusion.4), channel_id=1, source_target_pairs={{0,8},{4,12},{8,0},{12,4},{16,24},{20,28},{24,16},{28,20},{1,9},{5... | collective-permute-start | bytes 4325384 | tf_op jit(solution)/shard_map/ppermute | solution.py:564
  537.7 57.6 %collective-permute-start.81 = (bf16[2,256,1408]{2,1,0:T(8,128)(2,1)}, bf16[2,256,1408]{2,1,0:T(8,128)(2,1)}, u32[]{:S(2)}, u32[]{:S(2)}) collective-permute-start(bf16[2,256,1408]{2,1,0:T(8,128)(2,1)} %get-tuple-element.538), channel_id=1, source_target_pairs={{0,8},{4,12},{8,0},{12,4},{16,24},{20,28},{24,16},{28,20},{1,9},{5... | collective-permute-start | bytes 4325384 | tf_op jit(solution)/shard_map/ppermute | solution.py:564
  538.3 57.0 %collective-permute-start.82 = (bf16[2,256,1408]{2,1,0:T(8,128)(2,1)}, bf16[2,256,1408]{2,1,0:T(8,128)(2,1)}, u32[]{:S(2)}, u32[]{:S(2)}) collective-permute-start(bf16[2,256,1408]{2,1,0:T(8,128)(2,1)} %get-tuple-element.538), channel_id=1, source_target_pairs={{0,16},{4,20},{8,24},{12,28},{16,0},{20,4},{24,8},{28,12},{1,17},{... | collective-permute-start | bytes 4325384 | tf_op jit(solution)/shard_map/ppermute | solution.py:564
  559.1 33.7 %collective-permute-start.20 = (bf16[512,256]{1,0:T(8,128)(2,1)}, bf16[512,256]{1,0:T(8,128)(2,1)}, u32[]{:S(2)}, u32[]{:S(2)}) collective-permute-start(bf16[512,256]{1,0:T(8,128)(2,1)} %get-tuple-element.909), channel_id=1, source_target_pairs={{0,1},{1,0},{2,3},{3,2},{4,5},{5,4},{6,7},{7,6},{8,9},{9,8},{10,11... | collective-permute-start | bytes 786440 | tf_op jit(solution)/shard_map/cond/branch_1_fun/ppermute | solution.py:564
  560.0 32.8 %collective-permute-start.21 = (bf16[512,256]{1,0:T(8,128)(2,1)}, bf16[512,256]{1,0:T(8,128)(2,1)}, u32[]{:S(2)}, u32[]{:S(2)}) collective-permute-start(bf16[512,256]{1,0:T(8,128)(2,1)} %get-tuple-element.908), channel_id=1, source_target_pairs={{0,2},{1,3},{2,0},{3,1},{4,6},{5,7},{6,4},{7,5},{8,10},{9,11},{10,... | collective-permute-start | bytes 786440 | tf_op jit(solution)/shard_map/cond/branch_1_fun/ppermute | solution.py:564
  560.9 31.8 %collective-permute-start.22 = (bf16[512,256]{1,0:T(8,128)(2,1)S(1)}, bf16[512,256]{1,0:T(8,128)(2,1)}, u32[]{:S(2)}, u32[]{:S(2)}) collective-permute-start(bf16[512,256]{1,0:T(8,128)(2,1)S(1)} %get-tuple-element.907), channel_id=1, source_target_pairs={{0,3},{1,2},{2,1},{3,0},{4,7},{5,6},{6,5},{7,4},{8,11},{9,10},{10,... | collective-permute-start | bytes 786440 | tf_op jit(solution)/shard_map/cond/branch_1_fun/ppermute | solution.py:564
  595.9 45.9 %collective-permute-start.86 = (bf16[8,256,256]{2,1,0:T(8,128)(2,1)}, bf16[8,256,256]{2,1,0:T(8,128)(2,1)}, u32[]{:S(2)}, u32[]{:S(2)}) collective-permute-start(bf16[8,256,256]{2,1,0:T(8,128)(2,1)} %get-tuple-element.946.refs_5_), channel_id=1, source_target_pairs={{0,4},{4,0},{8,12},{12,8},{16,20},{20,16},{24,28},{28,24},{1,5},{5... | collective-permute-start | bytes 3145736 | tf_op jit(solution)/shard_map/ppermute | solution.py:564
  638.7 36.2 %collective-permute-start.89 = (bf16[256,1408]{1,0:T(8,128)(2,1)}, bf16[256,1408]{1,0:T(8,128)(2,1)}, u32[]{:S(2)}, u32[]{:S(2)}) collective-permute-start(bf16[256,1408]{1,0:T(8,128)(2,1)} %slice_bitcast_fusion.7), channel_id=1, source_target_pairs={{0,16},{4,20},{8,24},{12,28},{16,0},{20,4},{24,8},{28,12},{1,17},{... | collective-permute-start | bytes 2162696 | tf_op jit(solution)/shard_map/ppermute | solution.py:564
  640.7 34.2 %collective-permute-start.90 = (bf16[256,1408]{1,0:T(8,128)(2,1)}, bf16[256,1408]{1,0:T(8,128)(2,1)}, u32[]{:S(2)}, u32[]{:S(2)}) collective-permute-start(bf16[256,1408]{1,0:T(8,128)(2,1)} %slice_bitcast_fusion.6), channel_id=1, source_target_pairs={{0,8},{4,12},{8,0},{12,4},{16,24},{20,28},{24,16},{28,20},{1,9},{5... | collective-permute-start | bytes 2162696 | tf_op jit(solution)/shard_map/ppermute | solution.py:564
  702.5 33.5 %collective-permute-start.10 = (bf16[512,1024]{1,0:T(8,128)(2,1)}, bf16[512,1024]{1,0:T(8,128)(2,1)}, u32[]{:S(2)}, u32[]{:S(2)}) collective-permute-start(bf16[512,1024]{1,0:T(8,128)(2,1)} %get-tuple-element.312.refs_11_), channel_id=1, source_target_pairs={{0,4},{4,0},{8,12},{12,8},{16,20},{20,16},{24,28},{28,24},{1,5},{5... | collective-permute-start | bytes 3145736 | tf_op jit(solution)/shard_map/cond/branch_1_fun/ppermute | solution.py:564
  702.6 33.4 %collective-permute-start.7 = (bf16[512,1024]{1,0:T(8,128)(2,1)}, bf16[512,1024]{1,0:T(8,128)(2,1)}, u32[]{:S(2)}, u32[]{:S(2)}) collective-permute-start(bf16[512,1024]{1,0:T(8,128)(2,1)} %get-tuple-element.312.refs_11_), channel_id=1, source_target_pairs={{0,8},{4,12},{8,0},{12,4},{16,24},{20,28},{24,16},{28,20},{1,9},{5... | collective-permute-start | bytes 3145736 | tf_op jit(solution)/shard_map/cond/branch_1_fun/ppermute | solution.py:564
  705.4 48.0 %collective-permute-start.8 = (bf16[512,1024]{1,0:T(8,128)(2,1)}, bf16[512,1024]{1,0:T(8,128)(2,1)}, u32[]{:S(2)}, u32[]{:S(2)}) collective-permute-start(bf16[512,1024]{1,0:T(8,128)(2,1)} %get-tuple-element.312.refs_11_), channel_id=1, source_target_pairs={{0,16},{4,20},{8,24},{12,28},{16,0},{20,4},{24,8},{28,12},{1,17},{... | collective-permute-start | bytes 3145736 | tf_op jit(solution)/shard_map/cond/branch_1_fun/ppermute | solution.py:564
  705.4 48.0 %collective-permute-start.9 = (bf16[512,1024]{1,0:T(8,128)(2,1)}, bf16[512,1024]{1,0:T(8,128)(2,1)}, u32[]{:S(2)}, u32[]{:S(2)}) collective-permute-start(bf16[512,1024]{1,0:T(8,128)(2,1)} %get-tuple-element.312.refs_11_), channel_id=1, source_target_pairs={{0,24},{4,28},{8,16},{12,20},{16,8},{20,12},{24,0},{28,4},{1,25},{... | collective-permute-start | bytes 3145736 | tf_op jit(solution)/shard_map/cond/branch_1_fun/ppermute | solution.py:564
  755.9 32.5 %collective-permute-start.93 = (bf16[512,1024]{1,0:T(8,128)(2,1)}, bf16[512,1024]{1,0:T(8,128)(2,1)}, u32[]{:S(2)}, u32[]{:S(2)}) collective-permute-start(bf16[512,1024]{1,0:T(8,128)(2,1)} %get-tuple-element.563.refs_1_), channel_id=1, source_target_pairs={{0,4},{4,0},{8,12},{12,8},{16,20},{20,16},{24,28},{28,24},{1,5},{5... | collective-permute-start | bytes 3145736 | tf_op jit(solution)/shard_map/ppermute | solution.py:564
  831.6 33.5 %all-to-all-start.1 = ((bf16[8,64,768]{2,1,0:T(8,128)(2,1)}), bf16[8,64,768]{2,1,0:T(8,128)(2,1)S(1)}, u32[]{:S(2)}, u32[]{:S(2)}) async-start(bf16[8,64,768]{2,1,0:T(8,128)(2,1)} %bitcast.130), calls=%async_computation.1 | async-start | bytes 1572864 | tf_op jit(solution)/shard_map/all_to_all | solution.py:1269
  (208 other events, 2480.0 us)

commit v4 on v3

--- a/solution.py
+++ b/solution.py
@@ -791,7 +791,7 @@
         n1, h1 = join_scaled(n1, ga)
         return n1, h1, join([dy_own, dy_got], 0), wg
 
-    mark(routes, wqk_x, small_t)
+    mark(routes)
     n1, h1, dy, wg = window(first_window, n1_own, dy_own, gate_up_weight)
     n1_t = core_swap(n1)
     wg_x = core_swap(wg)
@@ -823,9 +823,7 @@
                 us=9.5,
         )(down_weight)
 
-    la.step()
     tiles = project(h1, h1_x, (wqk_m, wqk_x), 2, 0)
-    la.step()
     def start_of(k, other, h):
         return 2 * ts * (2 * (chip ^ k) + (core ^ other)) + h * ts
 
@@ -930,10 +928,12 @@
         wd_x, dy_x = core_swap(wd), core_swap(dy)
         return finish_reduce(keep, sent, 2), dy, dy_x, wd_x, places()
 
+    la.step()
     sent, keep, wd, dy, dy_got = window(query_window, tiles, dy)
     la.step()
     qkv_parts, dy_all, dy_x, wd_x, at_places = window(sum_window, sent, keep, wd, dy, dy_got)
     pos_row, pos_col, proj_scalars, all_scalars, back_scalars, starts_all, weight_scalars = at_places
+    la.step()
 
     s_abs = f ^ chip
     positions = jnp.arange(seq, dtype=jnp.int32)

time: 884 us -> 880 us (level)
  waiting for transfers between devices: 168 us -> 159 us
    ppermute x104, waiting for transfers between devices: 168 us -> 159 us  [swap(): return lax.ppermute(x, axis, [(i, i ^ k) for i in range(n)])]
    unnamed x241 -> x233, local copies, waits for them, and re-layouts: 36 us -> 35.1 us
  transfers between devices with their start and end apart: 106 -> 106, of which waited for: 28 -> 28; matrix products, arithmetic and copies ran while one was open for 10% -> 10% of each run, Pallas kernels for 49% -> 50%
where the time goes in v4:
time: 880 us; the launch traced here: 867 us
  Pallas kernels  458 us (52%)
  waiting for transfers between devices  159 us (18%)
  starting transfers between devices  114 us (13%)
  local copies, waits for them, and re-layouts  88.4 us (10%)
  other arithmetic  37.6 us (4%)
    pallas_call x78, Pallas kernels, go(): pl.pallas_call(kernel_body, out_shape=out_shape + [jax.ShapeDtypeStruct(v...  458 us
    ppermute x104, waiting for transfers between devices, swap(): return lax.ppermute(x, axis, [(i, i ^ k) for i in range(n)])  159 us
    ppermute x104, starting transfers between devices, swap(): return lax.ppermute(x, axis, [(i, i ^ k) for i in range(n)])  106 us
    unnamed x233, local copies, waits for them, and re-layouts  35.1 us
  transfers between devices with their start and end apart: 106, of which 28 were waited for; matrix products, arithmetic and copies ran while one was open for 10% of the time, Pallas kernels for 50%

profile of v4, /device:TPU:0, one launch (start us, length us, event | category | flops | bytes accessed | tf_op | source)
XLA Modules:
  0.0 866.9 jit_solution(10668204078113997108)
XLA Ops:
  32.5 35.9 %conditional.8 = (bf16[2048,256]{1,0:T(8,128)(2,1)}, bf16[2048,256]{1,0:T(8,128)(2,1)S(1)}, bf16[1024,256]{1,0:T(8,128)(2,1)S(1)}, bf16[8,256,2816]{2,1,0:T(8,128)(2,1)}) conditional(s32[]{:T(128)} %bitcast.57, () %tuple.78, (bf16[512,256]{1,0:T(8,128)(2,1)S(1)}, f32[256,8,2,1408]{3,2,1,0:T(2,128)}, s32[2048,4]{1,0:T(8,128)S(1)}, ...), branch_computations={%region_2.3_spmd, %region_3.4_spmd} | conditional | flops 32450000896 | bytes 14155816 | solution.py:611
  38.3 25.8 %branch_1_fun.15.refs_5_ = bf16[8,256,2816]{2,1,0:T(8,128)(2,1)} custom-call(s32[1]{0:T(128)} %constant.101.clone.first, f32[256,8,2,1408]{3,2,1,0:T(2,128)} %get-tuple-element.574.refs_0_, s32[2048,4]{1,0:T(8,128)S(1)} %get-tuple-element.219.refs_1_), custom_call_target="tpu_custom_call" | custom-call | flops 28600000512 | tf_op jit(solution)/shard_map/cond/branch_1_fun/pallas_call | solution.py:64
  93.1 28.7 %conditional.9 = (bf16[2,256,1024]{2,1,0:T(8,128)(2,1)}, bf16[2,256,1024]{2,1,0:T(8,128)(2,1)}, bf16[2,256,1024]{2,1,0:T(8,128)(2,1)}, bf16[2,256,1024]{2,1,0:T(...) conditional(s32[]{:T(128)} %bitcast.57, () %tuple.77, ...), branch_computations={%region_4.5_spmd, %region_5.6_spmd} | conditional | flops 19249999872 | bytes 11534628 | solution.py:611
  106.9 9.4 %branch_1_fun.19 = bf16[8,256,1408]{2,1,0:T(8,128)(2,1)} custom-call(s32[1]{0:T(128)} %constant.105.clone.first, f32[256,8,1408]{2,1,0:T(8,128)} %get-tuple-element.576.refs_0_, bf16[2,256,1024]{2,1,0:T(8,128)(2,1)} %get-tuple-element.992.refs_1_), custom_call_target="tpu_custom_call" | custom-call | flops 10449999872 | tf_op jit(solution)/shard_map/cond/branch_1_fun/pallas_call | solution.py:64
  123.1 25.9 %conditional.10 = (bf16[256,1024]{1,0:T(8,128)(2,1)}, bf16[256,1024]{1,0:T(8,128)(2,1)}, bf16[256,1024]{1,0:T(8,128)(2,1)}, bf16[256,1024]{1,0:T(8,128)(2,1)}, b...) conditional(s32[]{:T(128)} %bitcast.57, () %tuple.76, ...), branch_computations={%region_6.7_spmd, %region_7.48_spmd} | conditional | flops 6272583168 | bytes 34947716 | solution.py:611
  168.3 21.4 %shard_map.406 = (bf16[2,256,1408]{2,1,0:T(8,128)(2,1)}, bf16[2,256,1408]{2,1,0:T(8,128)(2,1)}, bf16[2,256,1408]{2,1,0:T(8,128)(2,1)}, bf16[2,256,1408]{2,1,0:T(8,128)(2,1)}) custom-call(s32[62]{0:T(128)S(1)} %get-tuple-element.479.first, s32[2,2048]{1,0:T(2,128)S(1)} %get-tuple-element.480.refs_0_, bf16[2048,256]{1,0:T(8,128)(2,1)} %get-tuple-element.473.refs_1_.refs_0_, ...), custom_call_target="tpu_custom_call" | custom-call | flops 29699999744 | tf_op jit(solution)/shard_map/pallas_call | solution.py:64
  224.3 8.8 %collective-permute-done.45.refs_1_ = bf16[512,256]{1,0:T(8,128)(2,1)S(1)} collective-permute-done((bf16[512,256]{1,0:T(8,128)(2,1)S(1)}, bf16[512,256]{1,0:T(8,128)(2,1)S(1)}, u32[]{:S(2)}, u32[]{:S(2)}) %collective-permute-start.45) | collective-permute-done | bytes 262176 | tf_op jit(solution)/shard_map/ppermute | solution.py:564
  287.2 16.6 %shard_map.420 = (bf16[2,256,2816]{2,1,0:T(8,128)(2,1)}, bf16[2,256,2816]{2,1,0:T(8,128)(2,1)}) custom-call(s32[92]{0:T(128)S(1)} %get-tuple-element.500.first, s32[2,2048]{1,0:T(2,128)S(1)} %get-tuple-element.480.refs_0_, bf16[2048,256]{1,0:T(8,128)(2,1)} %get-tuple-element.501.refs_1_, bf16[2048,256]{1,0:T(8,128)(2,1)} %multiply_convert_fusion.refs_2_, ...), custom_call_target="tpu_custom_call" | custom-call | flops 18699999232 | tf_op jit(solution)/shard_map/pallas_call | solution.py:64
  308.4 15.1 %shard_map.422 = (bf16[2,256,2816]{2,1,0:T(8,128)(2,1)}, bf16[2,256,2816]{2,1,0:T(8,128)(2,1)}) custom-call(s32[92]{0:T(128)S(1)} %get-tuple-element.500.first, s32[2,2048]{1,0:T(2,128)S(1)} %get-tuple-element.480.refs_0_, bf16[2048,256]{1,0:T(8,128)(2,1)} %get-tuple-element.501.refs_1_, bf16[2048,256]{1,0:T(8,128)(2,1)} %multiply_convert_fusion.refs_2_, ...), custom_call_target="tpu_custom_call" | custom-call | flops 18699999232 | tf_op jit(solution)/shard_map/pallas_call | solution.py:64
  326.4 13.0 %shard_map.424.refs_2_ = bf16[256,4096]{1,0:T(8,128)(2,1)} custom-call(s32[16]{0:T(128)} %get-tuple-element.510.first, s32[2,2048]{1,0:T(2,128)S(1)} %get-tuple-element.480.refs_0_, bf16[2048,256]{1,0:T(8,128)(2,1)} %get-tuple-element.501.refs_1_, f32[16,1024]{1,0:T(8,128)} %shard_map.423.refs_2_.refs_0_), custom_call_target="tpu_custom_call" | custom-call | flops 14300000256 | tf_op jit(solution)/shard_map/pallas_call | solution.py:64
  339.5 12.4 %shard_map.425.refs_4_ = bf16[256,4096]{1,0:T(8,128)(2,1)S(1)} custom-call(s32[16]{0:T(128)} %get-tuple-element.510.first, s32[2,2048]{1,0:T(2,128)S(1)} %get-tuple-element.480.refs_0_, bf16[2048,256]{1,0:T(8,128)(2,1)} %get-tuple-element.473.refs_1_.refs_0_, bf16[256,4096]{1,0:T(8,128)(2,1)} %shard_map.424.refs_2_), custom_call_target="tpu_custom_call" | custom-call | flops 14300000256 | tf_op jit(solution)/shard_map/pallas_call | solution.py:64
  351.8 16.4 %collective-permute-done.62.refs_1_ = bf16[2,256,2816]{2,1,0:T(8,128)(2,1)} collective-permute-done((bf16[2,256,2816]{2,1,0:T(8,128)(2,1)}, bf16[2,256,2816]{2,1,0:T(8,128)(2,1)}, u32[]{:S(2)}, u32[]{:S(2)}) %collective-permute-start.62) | collective-permute-done | bytes 2883616 | tf_op jit(solution)/shard_map/ppermute | solution.py:564
  384.6 21.3 %collective-permute-done.64 = bf16[1,256,2816]{2,1,0:T(8,128)(2,1)S(1)} collective-permute-done((bf16[1,256,2816]{2,1,0:T(8,128)(2,1)}, bf16[1,256,2816]{2,1,0:T(8,128)(2,1)S(1)}, u32[]{:S(2)}, u32[]{:S(2)}) %collective-permute-start.64) | collective-permute-done | bytes 1441824 | tf_op jit(solution)/shard_map/ppermute | solution.py:564
  413.9 12.6 %shard_map.429 = (bf16[2,256,2816]{2,1,0:T(8,128)(2,1)}, bf16[2,256,1408]{2,1,0:T(8,128)(2,1)}, f32[8,2048]{1,0:T(8,128)}) custom-call(s32[2]{0:T(128)} %pad_add_fusion.8.first, s32[2,2048]{1,0:T(2,128)S(1)} %get-tuple-element.480.refs_0_, f32[8,2048]{1,0:T(8,128)} %maximum_maximum_fusion.refs_1_, bf16[256,2816]{1,0:T(8,128)(2,1)} %bitcast.352, ...), custom_call_target="tpu_custom_call" | custom-call | flops 14300000256 | tf_op jit(solution)/shard_map/pallas_call | solution.py:64
  435.5 11.3 %shard_map.431.refs_2_.refs_6_ = f32[2048,256]{1,0:T(8,128)S(1)} custom-call(s32[46]{0:T(128)S(1)} %copy-done.125, s32[2048,2]{1,0:T(8,128)} %copy-done.15, bf16[2,256,2816]{2,1,0:T(8,128)(2,1)} %get-tuple-element.517.refs_2_.refs_1_, bf16[2,256,2816]{2,1,0:T(8,128)(2,1)} %collective-permute-done.68.refs_2_, ...), custom_call_target="tpu_custom_call", output_to_operand_aliasing={{}: (5, {})} | custom-call | flops 14960000000 | tf_op jit(solution)/shard_map/pallas_call | solution.py:64
  450.0 8.7 shard_map.433.refs_2_
  460.1 31.8 %collective-permute-done.72.refs_1_ = bf16[2,256,2816]{2,1,0:T(8,128)(2,1)} collective-permute-done((bf16[2,256,2816]{2,1,0:T(8,128)(2,1)}, bf16[2,256,2816]{2,1,0:T(8,128)(2,1)}, u32[]{:S(2)}, u32[]{:S(2)}) %collective-permute-start.72) | collective-permute-done | bytes 2883616 | tf_op jit(solution)/shard_map/ppermute | solution.py:564
  502.9 22.5 %shard_map.436 = (f32[2048,256]{1,0:T(8,128)}, bf16[2,256,1408]{2,1,0:T(8,128)(2,1)}) custom-call(s32[62]{0:T(128)S(1)} %copy-done.122, s32[2048,2]{1,0:T(8,128)} %copy-done.15, bf16[2,256,2816]{2,1,0:T(8,128)(2,1)} %get-tuple-element.522.refs_1_, ...), custom_call_target="tpu_custom_call", output_to_operand_aliasing={{0}: (7, {}), {1}: (9, {})} | custom-call | flops 29920000000 | tf_op jit(solution)/shard_map/pallas_call | solution.py:64
  542.1 13.0 %shard_map.439 = f32[2048,256]{1,0:T(8,128)} custom-call(s32[46]{0:T(128)S(1)} %copy-done.127, s32[2048,2]{1,0:T(8,128)} %copy-done.15, bf16[256,2816]{1,0:T(8,128)(2,1)S(1)} %get-tuple-element.527.refs_1_, bf16[256,2816]{1,0:T(8,128)(2,1)} %get-tuple-element.528.refs_2_, bf16[256,2816]{1,0:T(8,128)(2,1)} %copy-done.84, ...), custom_call_target="tpu_custom_call", output_to_operand_aliasing={{}: (7, {})} | custom-call | flops 14960000000 | tf_op jit(solution)/shard_map/pallas_call | solution.py:64
  555.1 38.8 %conditional.11 = (bf16[512,256]{1,0:T(8,128)(2,1)S(1)}, f32[256,8,2,1408]{3,2,1,0:T(2,128)}) conditional(s32[]{:T(128)} %bitcast.57, () %tuple.83, (f32[2048,256]{1,0:T(8,128)}, s32[25]{0:T(128)S(1)}, bf16[256,4096]{1,0:T(8,128)(2,1)}, bf16[2,256,2816]{2,1,0:T(8,128)(2,1)}, bf16[2,256,2816]{2,1,0:T(8,128)(2,1)}, ...), branch_computations={%region_57.59_spmd, %region_58.60_spmd} | conditional | flops 34650525696 | bytes 23330838 | solution.py:611
  562.0 29.3 %branch_1_fun.23.refs_4_ = f32[256,8,2,1408]{3,2,1,0:T(2,128)} custom-call(s32[25]{0:T(128)S(1)} %get-tuple-element.273.first, bf16[256,4096]{1,0:T(8,128)(2,1)} %get-tuple-element.274.refs_0_, bf16[2,256,2816]{2,1,0:T(8,128)(2,1)} %get-tuple-element.275.refs_1_, bf16[2,256,2816]{2,1,0:T(8,128)(2,1)} %get-tuple-element.276.refs_2_, ...), custom_call_target="tpu_custom_call" | custom-call | flops 32999999488 | tf_op jit(solution)/shard_map/cond/branch_1_fun/pallas_call | solution.py:64
  599.6 22.8 %conditional.12 = (f32[2048,256]{1,0:T(8,128)S(1)}, bf16[512,256]{1,0:T(8,128)(2,1)S(1)}, bf16[512,256]{1,0:T(8,128)(2,1)}, bf16[512,256]{1,0:T(8,128)(2,1)}, bf16[512,256]{1,0:T(8,128)(2,1)}) conditional(s32[]{:T(128)} %bitcast.57, () %tuple.82, (s32[62]{0:T(128)S(1)}, s32[2048,2]{0,1:T(2,128)}, bf16[2,256,1408]{2,1,0:T(8,128)(2,1)}, ...), branch_computations={%region_59.61_spmd, %region_60.62_spmd} | conditional | flops 24640000000 | bytes 3702944 | solution.py:611
  606.0 16.3 %branch_1_fun.25 = f32[2048,256]{1,0:T(8,128)S(1)} custom-call(s32[62]{0:T(128)S(1)} %get-tuple-element.286.first, s32[2048,2]{1,0:T(8,128)} %copy.261.refs_0_, bf16[2,256,1408]{2,1,0:T(8,128)(2,1)} %get-tuple-element.288.refs_1_, bf16[2,256,1408]{2,1,0:T(8,128)(2,1)} %get-tuple-element.289.refs_2_, ...), custom_call_target="tpu_custom_call", output_to_operand_aliasing={{}: (7, {})} | custom-call | flops 24640000000 | tf_op jit(solution)/shard_map/cond/branch_1_fun/pallas_call | solution.py:64
  646.0 22.4 %conditional.13 = (bf16[2,256,512]{2,1,0:T(8,128)(2,1)}, bf16[2,256,512]{2,1,0:T(8,128)(2,1)}, bf16[2,256,512]{2,1,0:T(8,128)(2,1)}, bf16[2,256,512]{2,1,0:T(8,128)(2,1)}) conditional(s32[]{:T(128)} %bitcast.57, () %tuple.75, (bf16[2,256,512]{2,1,0:T(8,128)(2,1)}, bf16[2,256,512]{2,1,0:T(8,128)(2,1)}, s32[]{:T(128)}, s32[2048,4]{1,0:T(8,128)S(1)}, ...), branch_computations={%region_64.66_spmd, %region_65.67_spmd} | conditional | flops 7699999744 | bytes 4194532 | solution.py:611
  656.8 11.6 %collective-permute-done.15 = bf16[2,256,512]{2,1,0:T(8,128)(2,1)} collective-permute-done((bf16[2,256,512]{2,1,0:T(8,128)(2,1)}, bf16[2,256,512]{2,1,0:T(8,128)(2,1)}, u32[]{:S(2)}, u32[]{:S(2)}) %collective-permute-start.15) | collective-permute-done | bytes 524320 | tf_op jit(solution)/shard_map/cond/branch_1_fun/ppermute | solution.py:564
  680.4 9.4 %shard_map.447.refs_12_ = f32[2048,256]{1,0:T(8,128)S(1)} custom-call(s32[46]{0:T(128)S(1)} %copy-done.128, s32[2048,2]{1,0:T(8,128)} %copy-done.15, bf16[256,1408]{1,0:T(8,128)(2,1)} %get-tuple-element.553.refs_1_, bf16[256,1408]{1,0:T(8,128)(2,1)} %get-tuple-element.554.refs_2_, bf16[256,1408]{1,0:T(8,128)(2,1)} %copy-done.18, ...), custom_call_target="tpu_custom_call", output_to_operand_aliasing={{}: (7, {})} | custom-call | flops 12320000000 | tf_op jit(solution)/shard_map/pallas_call | solution.py:64
  699.9 50.4 %conditional.14 = (bf16[512,1024]{1,0:T(8,128)(2,1)}, bf16[512,1024]{1,0:T(8,128)(2,1)}, bf16[512,1024]{1,0:T(8,128)(2,1)}, bf16[512,1024]{1,0:T(8,128)(2,1)}, b...) conditional(s32[]{:T(128)} %bitcast.57, () %tuple.74, (bf16[512,1024]{1,0:T(8,128)(2,1)}, ...), branch_computations={%region_66.68_spmd, %region_67.69_spmd} | conditional | flops 110000000 | bytes 19923192 | solution.py:611
  709.7 24.0 %branch_1_fun.27 = f32[256,8,1408]{2,1,0:T(8,128)} custom-call(s32[25]{0:T(128)S(1)} %get-tuple-element.308.first, bf16[256,4096]{1,0:T(8,128)(2,1)} %get-tuple-element.309.refs_0_, bf16[2,256,1408]{2,1,0:T(8,128)(2,1)} %get-tuple-element.310.refs_1_, bf16[2,256,1408]{2,1,0:T(8,128)(2,1)} %get-tuple-element.311.refs_2_, ...), custom_call_target="tpu_custom_call" | custom-call | flops 110000000 | tf_op jit(solution)/shard_map/cond/branch_1_fun/pallas_call | solution.py:64
  733.7 16.2 %collective-permute-done.8 = bf16[512,1024]{1,0:T(8,128)(2,1)} collective-permute-done((bf16[512,1024]{1,0:T(8,128)(2,1)}, bf16[512,1024]{1,0:T(8,128)(2,1)}, u32[]{:S(2)}, u32[]{:S(2)}) %collective-permute-start.8) | collective-permute-done | bytes 1048608 | tf_op jit(solution)/shard_map/cond/branch_1_fun/ppermute | solution.py:564
  794.2 29.9 %conditional.15 = (f32[512,256]{1,0:T(8,128)}, f32[256,8,512]{2,1,0:T(8,128)}, f32[256,2,512]{2,1,0:T(2,128)}) conditional(s32[]{:T(128)} %bitcast.57, () %tuple.73, (bf16[4,512,256]{2,1,0:T(8,128)(2,1)S(1)}, s32[]{:T(128)}, s32[]{:T(128)}, bf16[2048,256]{1,0:T(8,128)(2,1)S(1)}, s32[4,512,2]{2,1,0:T(8,128)S(1)}, ...), branch_computations={%region_68.70_spmd, %region_69.71_spmd} | conditional | flops 23650000896 | bytes 7405800 | solution.py:611
  801.6 20.2 %branch_1_fun.28 = (f32[256,8,512]{2,1,0:T(8,128)}, f32[256,2,512]{2,1,0:T(2,128)}) custom-call(s32[5]{0:T(128)} %pad_add_fusion.2.first, bf16[4,256,512]{2,1,0:T(8,128)(2,1)} %bitcast.316, s32[4,512,2]{2,1,0:T(8,128)S(1)} %get-tuple-element.324.refs_1_, f32[4,512,2]{2,1,0:T(8,128)S(1)} %copy-done.10, bf16[512,1024]{1,0:T(8,128)(2,1)} %get-tuple-element.326.refs_3_, ...), custom_call_target="tpu_custom_call" | custom-call | flops 22000001024 | tf_op jit(solution)/shard_map/cond/branch_1_fun/pallas_call | solution.py:64
  831.0 18.3 %shard_map.460.refs_2_ = f32[256,8,512]{2,1,0:T(8,128)} custom-call(s32[5]{0:T(128)} %pad_add_fusion.9.first, bf16[4,256,512]{2,1,0:T(8,128)(2,1)} %bitcast.315, s32[4,512,2]{2,1,0:T(8,128)S(1)} %bitcast.291, f32[4,512,2]{2,1,0:T(8,128)} %bitcast.313, bf16[512,512]{1,0:T(8,128)(2,1)} %get-tuple-element.484.refs_2_.refs_5_.refs_3_, ...), custom_call_target="tpu_custom_call" | custom-call | flops 22000001024 | tf_op jit(solution)/shard_map/pallas_call | solution.py:64
  (769 shorter events, 456.4 us)
Async XLA Ops:
  14.2 63.4 %collective-permute-start.31 = (bf16[2,256]{1,0:T(2,128)(2,1)S(1)}, bf16[2,256]{1,0:T(2,128)(2,1)S(1)}, u32[]{:S(2)}, u32[]{:S(2)}) collective-permute-start(bf16[2,256]{1,0:T(2,128)(2,1)S(1)} %pad_maximum_fusion.5), channel_id=1, source_target_pairs={{0,4},{4,0},{8,12},{12,8},{16,20},{20,16},{24,28},{28,24},{1,5},{5... | collective-permute-start | bytes 3080 | tf_op jit(solution)/shard_map/ppermute | solution.py:564
  32.5 31.6 %collective-permute-start = (bf16[512,256]{1,0:T(8,128)(2,1)S(1)}, bf16[512,256]{1,0:T(8,128)(2,1)S(1)}, u32[]{:S(2)}, u32[]{:S(2)}) collective-permute-start(bf16[512,256]{1,0:T(8,128)(2,1)S(1)} %get-tuple-element.196.refs_1_), channel_id=1, source_target_pairs={{0,1},{1,0},{2,3},{3,2},{4,5},{5,4},{6,7},{7,6},{8,9},{9,8},{10,11... | collective-permute-start | bytes 786440 | tf_op jit(solution)/shard_map/cond/branch_1_fun/ppermute | solution.py:564
  78.0 209.3 %collective-permute-start.58 = (bf16[8,256,2816]{2,1,0:T(8,128)(2,1)}, bf16[8,256,2816]{2,1,0:T(8,128)(2,1)}, u32[]{:S(2)}, u32[]{:S(2)}) collective-permute-start(bf16[8,256,2816]{2,1,0:T(8,128)(2,1)} %get-tuple-element.502.refs_3_.refs_5_), channel_id=1, source_target_pairs={{0,4},{4,0},{8,12},{12,8},{16,20},{20,16},{24,28},{28,24},{1,5},{5... | collective-permute-start | bytes 34603016 | tf_op jit(solution)/shard_map/ppermute | solution.py:564
  89.7 32.2 %collective-permute-start.34 = (f32[8,512]{1,0:T(8,128)S(1)}, f32[8,512]{1,0:T(8,128)S(1)}, u32[]{:S(2)}, u32[]{:S(2)}) collective-permute-start(f32[8,512]{1,0:T(8,128)S(1)} %shard_map.401.refs_0_), channel_id=1, source_target_pairs={{0,8},{4,12},{8,0},{12,4},{16,24},{20,28},{24,16},{28,20},{1,9},{5... | collective-permute-start | bytes 49160 | tf_op jit(solution)/shard_map/ppermute | solution.py:564
  166.4 33.6 %collective-permute-start.44 = (bf16[512,512]{1,0:T(8,128)(2,1)}, bf16[512,512]{1,0:T(8,128)(2,1)}, u32[]{:S(2)}, u32[]{:S(2)}) collective-permute-start(bf16[512,512]{1,0:T(8,128)(2,1)} %get-tuple-element.484.refs_2_.refs_5_.refs_3_), channel_id=1, source_target_pairs={{0,4},{4,0},{8,12},{12,8},{16,20},{20,16},{24,28},{28,24},{1,5},{5... | collective-permute-start | bytes 1572872 | tf_op jit(solution)/shard_map/ppermute | solution.py:564
  218.3 36.4 %collective-permute-start.52 = (bf16[2,256,1408]{2,1,0:T(8,128)(2,1)}, bf16[2,256,1408]{2,1,0:T(8,128)(2,1)S(1)}, u32[]{:S(2)}, u32[]{:S(2)}) collective-permute-start(bf16[2,256,1408]{2,1,0:T(8,128)(2,1)} %get-tuple-element.493), channel_id=1, source_target_pairs={{0,8},{4,12},{8,0},{12,4},{16,24},{20,28},{24,16},{28,20},{1,9},{5... | collective-permute-start | bytes 4325384 | tf_op jit(solution)/shard_map/ppermute | solution.py:564
  218.8 38.3 %collective-permute-start.53 = (bf16[2,256,1408]{2,1,0:T(8,128)(2,1)}, bf16[2,256,1408]{2,1,0:T(8,128)(2,1)}, u32[]{:S(2)}, u32[]{:S(2)}) collective-permute-start(bf16[2,256,1408]{2,1,0:T(8,128)(2,1)} %get-tuple-element.495), channel_id=1, source_target_pairs={{0,16},{4,20},{8,24},{12,28},{16,0},{20,4},{24,8},{28,12},{1,17},{... | collective-permute-start | bytes 4325384 | tf_op jit(solution)/shard_map/ppermute | solution.py:564
  284.9 38.6 %collective-permute-start.56 = (f32[16,512]{1,0:T(8,128)S(1)}, f32[16,512]{1,0:T(8,128)S(1)}, u32[]{:S(2)}, u32[]{:S(2)}) collective-permute-start(f32[16,512]{1,0:T(8,128)S(1)} %copy-done.100), channel_id=1, source_target_pairs={{0,1},{1,0},{2,3},{3,2},{4,5},{5,4},{6,7},{7,6},{8,9},{9,8},{10,11... | collective-permute-start | bytes 98312 | tf_op jit(solution)/shard_map/ppermute | solution.py:564
  303.9 64.4 %collective-permute-start.62 = (bf16[2,256,2816]{2,1,0:T(8,128)(2,1)}, bf16[2,256,2816]{2,1,0:T(8,128)(2,1)}, u32[]{:S(2)}, u32[]{:S(2)}) collective-permute-start(bf16[2,256,2816]{2,1,0:T(8,128)(2,1)} %get-tuple-element.505.refs_4_), channel_id=1, source_target_pairs={{0,8},{4,12},{8,0},{12,4},{16,24},{20,28},{24,16},{28,20},{1,9},{5... | collective-permute-start | bytes 8650760 | tf_op jit(solution)/shard_map/ppermute | solution.py:564
  303.9 64.7 %collective-permute-start.63 = (bf16[2,256,2816]{2,1,0:T(8,128)(2,1)}, bf16[2,256,2816]{2,1,0:T(8,128)(2,1)}, u32[]{:S(2)}, u32[]{:S(2)}) collective-permute-start(bf16[2,256,2816]{2,1,0:T(8,128)(2,1)} %get-tuple-element.509), channel_id=1, source_target_pairs={{0,16},{4,20},{8,24},{12,28},{16,0},{20,4},{24,8},{28,12},{1,17},{... | collective-permute-start | bytes 8650760 | tf_op jit(solution)/shard_map/ppermute | solution.py:564
  325.5 52.8 %collective-permute-start.61 = (f32[16,1024]{1,0:T(8,128)}, f32[16,1024]{1,0:T(8,128)S(1)}, u32[]{:S(2)}, u32[]{:S(2)}) collective-permute-start(f32[16,1024]{1,0:T(8,128)} %shard_map.423.refs_2_.refs_0_), channel_id=1, source_target_pairs={{0,2},{1,3},{2,0},{3,1},{4,6},{5,7},{6,4},{7,5},{8,10},{9,11},{10,... | collective-permute-start | bytes 196616 | tf_op jit(solution)/shard_map/ppermute | solution.py:564
  373.1 32.8 %collective-permute-start.64 = (bf16[1,256,2816]{2,1,0:T(8,128)(2,1)}, bf16[1,256,2816]{2,1,0:T(8,128)(2,1)S(1)}, u32[]{:S(2)}, u32[]{:S(2)}) collective-permute-start(bf16[1,256,2816]{2,1,0:T(8,128)(2,1)} %get-tuple-element.511.refs_4_), channel_id=1, source_target_pairs={{0,16},{4,20},{8,24},{12,28},{16,0},{20,4},{24,8},{28,12},{1,17},{... | collective-permute-start | bytes 4325384 | tf_op jit(solution)/shard_map/ppermute | solution.py:564
  381.3 32.7 %collective-permute-start.65 = (bf16[1,256,2816]{2,1,0:T(8,128)(2,1)}, bf16[1,256,2816]{2,1,0:T(8,128)(2,1)}, u32[]{:S(2)}, u32[]{:S(2)}) collective-permute-start(bf16[1,256,2816]{2,1,0:T(8,128)(2,1)} %get-tuple-element.514), channel_id=1, source_target_pairs={{0,8},{4,12},{8,0},{12,4},{16,24},{20,28},{24,16},{28,20},{1,9},{5... | collective-permute-start | bytes 4325384 | tf_op jit(solution)/shard_map/ppermute | solution.py:564
  426.7 65.3 %collective-permute-start.72 = (bf16[2,256,2816]{2,1,0:T(8,128)(2,1)}, bf16[2,256,2816]{2,1,0:T(8,128)(2,1)}, u32[]{:S(2)}, u32[]{:S(2)}) collective-permute-start(bf16[2,256,2816]{2,1,0:T(8,128)(2,1)} %get-tuple-element.517.refs_2_.refs_1_), channel_id=1, source_target_pairs={{0,8},{4,12},{8,0},{12,4},{16,24},{20,28},{24,16},{28,20},{1,9},{5... | collective-permute-start | bytes 8650760 | tf_op jit(solution)/shard_map/ppermute | solution.py:564
  427.6 64.9 %collective-permute-start.73 = (bf16[2,256,2816]{2,1,0:T(8,128)(2,1)}, bf16[2,256,2816]{2,1,0:T(8,128)(2,1)}, u32[]{:S(2)}, u32[]{:S(2)}) collective-permute-start(bf16[2,256,2816]{2,1,0:T(8,128)(2,1)} %get-tuple-element.517.refs_2_.refs_1_), channel_id=1, source_target_pairs={{0,16},{4,20},{8,24},{12,28},{16,0},{20,4},{24,8},{28,12},{1,17},{... | collective-permute-start | bytes 8650760 | tf_op jit(solution)/shard_map/ppermute | solution.py:564
  493.6 31.7 %collective-permute-start.71 = (f32[12,512]{1,0:T(8,128)S(1)}, f32[12,512]{1,0:T(8,128)S(1)}, u32[]{:S(2)}, u32[]{:S(2)}) collective-permute-start(f32[12,512]{1,0:T(8,128)S(1)} %copy-done.29), channel_id=1, source_target_pairs={{0,8},{4,12},{8,0},{12,4},{16,24},{20,28},{24,16},{28,20},{1,9},{5... | collective-permute-start | bytes 73736 | tf_op jit(solution)/shard_map/ppermute | solution.py:564
  497.3 33.4 %collective-permute-start.77 = (bf16[256,2816]{1,0:T(8,128)(2,1)}, bf16[256,2816]{1,0:T(8,128)(2,1)S(1)}, u32[]{:S(2)}, u32[]{:S(2)}) collective-permute-start(bf16[256,2816]{1,0:T(8,128)(2,1)} %slice_bitcast_fusion.5), channel_id=1, source_target_pairs={{0,16},{4,20},{8,24},{12,28},{16,0},{20,4},{24,8},{28,12},{1,17},{... | collective-permute-start | bytes 4325384 | tf_op jit(solution)/shard_map/ppermute | solution.py:564
  501.3 33.2 %collective-permute-start.78 = (bf16[256,2816]{1,0:T(8,128)(2,1)}, bf16[256,2816]{1,0:T(8,128)(2,1)}, u32[]{:S(2)}, u32[]{:S(2)}) collective-permute-start(bf16[256,2816]{1,0:T(8,128)(2,1)} %slice_bitcast_fusion.4), channel_id=1, source_target_pairs={{0,8},{4,12},{8,0},{12,4},{16,24},{20,28},{24,16},{28,20},{1,9},{5... | collective-permute-start | bytes 4325384 | tf_op jit(solution)/shard_map/ppermute | solution.py:564
  535.7 58.2 %collective-permute-start.81 = (bf16[2,256,1408]{2,1,0:T(8,128)(2,1)}, bf16[2,256,1408]{2,1,0:T(8,128)(2,1)}, u32[]{:S(2)}, u32[]{:S(2)}) collective-permute-start(bf16[2,256,1408]{2,1,0:T(8,128)(2,1)} %get-tuple-element.532), channel_id=1, source_target_pairs={{0,8},{4,12},{8,0},{12,4},{16,24},{20,28},{24,16},{28,20},{1,9},{5... | collective-permute-start | bytes 4325384 | tf_op jit(solution)/shard_map/ppermute | solution.py:564
  536.5 57.3 %collective-permute-start.82 = (bf16[2,256,1408]{2,1,0:T(8,128)(2,1)}, bf16[2,256,1408]{2,1,0:T(8,128)(2,1)}, u32[]{:S(2)}, u32[]{:S(2)}) collective-permute-start(bf16[2,256,1408]{2,1,0:T(8,128)(2,1)} %get-tuple-element.532), channel_id=1, source_target_pairs={{0,16},{4,20},{8,24},{12,28},{16,0},{20,4},{24,8},{28,12},{1,17},{... | collective-permute-start | bytes 4325384 | tf_op jit(solution)/shard_map/ppermute | solution.py:564
  557.6 33.7 %collective-permute-start.20 = (bf16[512,256]{1,0:T(8,128)(2,1)}, bf16[512,256]{1,0:T(8,128)(2,1)}, u32[]{:S(2)}, u32[]{:S(2)}) collective-permute-start(bf16[512,256]{1,0:T(8,128)(2,1)} %get-tuple-element.903), channel_id=1, source_target_pairs={{0,1},{1,0},{2,3},{3,2},{4,5},{5,4},{6,7},{7,6},{8,9},{9,8},{10,11... | collective-permute-start | bytes 786440 | tf_op jit(solution)/shard_map/cond/branch_1_fun/ppermute | solution.py:564
  558.5 32.8 %collective-permute-start.21 = (bf16[512,256]{1,0:T(8,128)(2,1)S(1)}, bf16[512,256]{1,0:T(8,128)(2,1)}, u32[]{:S(2)}, u32[]{:S(2)}) collective-permute-start(bf16[512,256]{1,0:T(8,128)(2,1)S(1)} %get-tuple-element.902), channel_id=1, source_target_pairs={{0,2},{1,3},{2,0},{3,1},{4,6},{5,7},{6,4},{7,5},{8,10},{9,11},{10,... | collective-permute-start | bytes 786440 | tf_op jit(solution)/shard_map/cond/branch_1_fun/ppermute | solution.py:564
  560.1 31.2 %collective-permute-start.22 = (bf16[512,256]{1,0:T(8,128)(2,1)S(1)}, bf16[512,256]{1,0:T(8,128)(2,1)}, u32[]{:S(2)}, u32[]{:S(2)}) collective-permute-start(bf16[512,256]{1,0:T(8,128)(2,1)S(1)} %get-tuple-element.901), channel_id=1, source_target_pairs={{0,3},{1,2},{2,1},{3,0},{4,7},{5,6},{6,5},{7,4},{8,11},{9,10},{10,... | collective-permute-start | bytes 786440 | tf_op jit(solution)/shard_map/cond/branch_1_fun/ppermute | solution.py:564
  594.5 44.7 %collective-permute-start.86 = (bf16[8,256,256]{2,1,0:T(8,128)(2,1)}, bf16[8,256,256]{2,1,0:T(8,128)(2,1)}, u32[]{:S(2)}, u32[]{:S(2)}) collective-permute-start(bf16[8,256,256]{2,1,0:T(8,128)(2,1)} %get-tuple-element.940.refs_5_), channel_id=1, source_target_pairs={{0,4},{4,0},{8,12},{12,8},{16,20},{20,16},{24,28},{28,24},{1,5},{5... | collective-permute-start | bytes 3145736 | tf_op jit(solution)/shard_map/ppermute | solution.py:564
  636.3 36.2 %collective-permute-start.89 = (bf16[256,1408]{1,0:T(8,128)(2,1)}, bf16[256,1408]{1,0:T(8,128)(2,1)}, u32[]{:S(2)}, u32[]{:S(2)}) collective-permute-start(bf16[256,1408]{1,0:T(8,128)(2,1)} %slice_bitcast_fusion.7), channel_id=1, source_target_pairs={{0,16},{4,20},{8,24},{12,28},{16,0},{20,4},{24,8},{28,12},{1,17},{... | collective-permute-start | bytes 2162696 | tf_op jit(solution)/shard_map/ppermute | solution.py:564
  638.4 34.1 %collective-permute-start.90 = (bf16[256,1408]{1,0:T(8,128)(2,1)}, bf16[256,1408]{1,0:T(8,128)(2,1)}, u32[]{:S(2)}, u32[]{:S(2)}) collective-permute-start(bf16[256,1408]{1,0:T(8,128)(2,1)} %slice_bitcast_fusion.6), channel_id=1, source_target_pairs={{0,8},{4,12},{8,0},{12,4},{16,24},{20,28},{24,16},{28,20},{1,9},{5... | collective-permute-start | bytes 2162696 | tf_op jit(solution)/shard_map/ppermute | solution.py:564
  700.2 33.6 %collective-permute-start.10 = (bf16[512,1024]{1,0:T(8,128)(2,1)}, bf16[512,1024]{1,0:T(8,128)(2,1)}, u32[]{:S(2)}, u32[]{:S(2)}) collective-permute-start(bf16[512,1024]{1,0:T(8,128)(2,1)} %get-tuple-element.306.refs_11_), channel_id=1, source_target_pairs={{0,4},{4,0},{8,12},{12,8},{16,20},{20,16},{24,28},{28,24},{1,5},{5... | collective-permute-start | bytes 3145736 | tf_op jit(solution)/shard_map/cond/branch_1_fun/ppermute | solution.py:564
  700.3 33.5 %collective-permute-start.7 = (bf16[512,1024]{1,0:T(8,128)(2,1)}, bf16[512,1024]{1,0:T(8,128)(2,1)}, u32[]{:S(2)}, u32[]{:S(2)}) collective-permute-start(bf16[512,1024]{1,0:T(8,128)(2,1)} %get-tuple-element.306.refs_11_), channel_id=1, source_target_pairs={{0,8},{4,12},{8,0},{12,4},{16,24},{20,28},{24,16},{28,20},{1,9},{5... | collective-permute-start | bytes 3145736 | tf_op jit(solution)/shard_map/cond/branch_1_fun/ppermute | solution.py:564
  701.9 48.0 %collective-permute-start.8 = (bf16[512,1024]{1,0:T(8,128)(2,1)}, bf16[512,1024]{1,0:T(8,128)(2,1)}, u32[]{:S(2)}, u32[]{:S(2)}) collective-permute-start(bf16[512,1024]{1,0:T(8,128)(2,1)} %get-tuple-element.306.refs_11_), channel_id=1, source_target_pairs={{0,16},{4,20},{8,24},{12,28},{16,0},{20,4},{24,8},{28,12},{1,17},{... | collective-permute-start | bytes 3145736 | tf_op jit(solution)/shard_map/cond/branch_1_fun/ppermute | solution.py:564
  701.9 48.0 %collective-permute-start.9 = (bf16[512,1024]{1,0:T(8,128)(2,1)}, bf16[512,1024]{1,0:T(8,128)(2,1)}, u32[]{:S(2)}, u32[]{:S(2)}) collective-permute-start(bf16[512,1024]{1,0:T(8,128)(2,1)} %get-tuple-element.306.refs_11_), channel_id=1, source_target_pairs={{0,24},{4,28},{8,16},{12,20},{16,8},{20,12},{24,0},{28,4},{1,25},{... | collective-permute-start | bytes 3145736 | tf_op jit(solution)/shard_map/cond/branch_1_fun/ppermute | solution.py:564
  752.4 32.9 %collective-permute-start.93 = (bf16[512,1024]{1,0:T(8,128)(2,1)}, bf16[512,1024]{1,0:T(8,128)(2,1)}, u32[]{:S(2)}, u32[]{:S(2)}) collective-permute-start(bf16[512,1024]{1,0:T(8,128)(2,1)} %get-tuple-element.557.refs_1_), channel_id=1, source_target_pairs={{0,4},{4,0},{8,12},{12,8},{16,20},{20,16},{24,28},{28,24},{1,5},{5... | collective-permute-start | bytes 3145736 | tf_op jit(solution)/shard_map/ppermute | solution.py:564
  827.5 33.4 %all-to-all-start.1 = ((bf16[8,64,768]{2,1,0:T(8,128)(2,1)}), bf16[8,64,768]{2,1,0:T(8,128)(2,1)S(1)}, u32[]{:S(2)}, u32[]{:S(2)}) async-start(bf16[8,64,768]{2,1,0:T(8,128)(2,1)} %bitcast.130), calls=%async_computation.1 | async-start | bytes 1572864 | tf_op jit(solution)/shard_map/all_to_all | solution.py:1269
  (203 other events, 2457.0 us)
